TPU v7x, 512 devices: a whole 4x8x8 slice. The times are simulated.
512 devices in a mesh: dp: 4 (over x), tensor: 8 (over y), expert: 16 (over z, core).
Axes of the slice: x: 4, y: 8, z: 8, core: 2. Of those that a mesh axis runs over, the one named last changes fastest.
Arguments:
- tokens_a: bfloat16 [1024, 7168], P(('dp', 'expert')), may hold values from -6 to 6
- norm_gain: float32 [7168], replicated, may hold values from 0.25 to 1.75
- expert_ids: int32 [1024, 8], P(('dp', 'expert')), may hold values from 0 to 15, all different within a row; in each aligned block of 16 rows (0 to 15, 16 to 31, ...) at most 12 rows name the same one
- route_weights: float32 [1024, 8], P(('dp', 'expert')), may hold values from 0.1 to 0.5
- w_gate: bfloat16 [16, 7168, 2048], P('expert', 'dp', 'tensor'), may hold values from -0.0625 to 0.0625
- w_up: bfloat16 [16, 7168, 2048], P('expert', 'dp', 'tensor'), may hold values from -0.0625 to 0.0625
- w_down: bfloat16 [16, 2048, 7168], P('expert', 'tensor', 'dp'), may hold values from -0.125 to 0.125
- queries_b: bfloat16 [64, 16, 128, 576], P(('dp', 'expert'), None, 'tensor'), may hold values from -25 to 25
- cache_b: bfloat16 [64, 16, 256, 576], P(('dp', 'expert'), 'tensor'), may hold values from -1.6875 to 1.6875
- lengths_b: int32 [64, 16], P(('dp', 'expert'), 'tensor'), may hold values from 2 to 256
Outputs:
- mixed: bfloat16 [1024, 7168], P(('dp', 'expert'), 'tensor')
- latent_b: bfloat16 [64, 16, 128, 512], P(('dp', 'expert'), None, 'tensor')
Inputs may be any that keep to these rules, and one draw needn't show every extreme that they name: `expert_ids`: each row names 8 different experts; among the 16 rows of one device no expert is named by more than 12 rows, a bound that some block reaches.
All inputs are finite; a program needn't handle non-finite values.
Results may differ from a plain program's by a relative error of at most 0.007.
Values may be sent and summed in bfloat16 or wider, within the bound.
No kernel may reach another device: no remote copies, remote signals or barrier semaphores. Data moves between devices by JAX's collectives and lax.ppermute only.
A program may use at most 64 MiB of HBM per device.

v0:
```python
import jax
import jax.numpy as jnp
from jax import lax
from jax.sharding import PartitionSpec as P

LAT = 512


score_scale = 192.0 ** (-0.5)


def norm_rows(tokens_a, norm_gain):
    values = tokens_a.astype(jnp.float32)
    row_scale = lax.rsqrt(jnp.mean(values * values, axis=-1, keepdims=True) + 1e-06)
    return (values * row_scale * norm_gain).astype(jnp.bfloat16)


def attend(queries, cache, lengths):
    scores = (
        jnp.einsum("rhc,rlc->rhl", queries, cache, preferred_element_type=jnp.float32) * score_scale
    )
    live_mask = lax.broadcasted_iota(jnp.int32, scores.shape, 2) < lengths[:, None, None]
    scores = jnp.where(live_mask, scores, -1e30)
    row_max = jnp.max(scores, axis=2, keepdims=True)
    exp_terms = jnp.exp(scores - row_max)
    softmax_bf = (exp_terms / jnp.sum(exp_terms, axis=2, keepdims=True)).astype(jnp.bfloat16)
    latent = jnp.einsum(
        "rhl,rlc->rhc", softmax_bf, cache[:, :, :LAT], preferred_element_type=jnp.float32
    )
    return latent.astype(jnp.bfloat16)


def shards(
    tokens_a,
    norm_gain,
    expert_ids,
    route_weights,
    w_gate,
    w_up,
    w_down,
    queries_b,
    cache_b,
    lengths_b,
):
    dp_size = lax.axis_size("dp")
    expert_size = lax.axis_size("expert")
    tensor_size = lax.axis_size("tensor")
    row_count = tokens_a.shape[0]
    local_experts = w_gate.shape[0]
    experts_all = local_experts * expert_size
    capacity = row_count * expert_ids.shape[1] * 3 // (2 * experts_all)
    width_dev = w_gate.shape[1]
    normed = norm_rows(tokens_a, norm_gain)
    chosen = expert_ids[:, :, None] == lax.broadcasted_iota(jnp.int32, (1, 1, experts_all), 2)
    weight = jnp.sum(
        jnp.where(chosen, route_weights[:, :, None], jnp.zeros_like(route_weights)[:, :, None]),
        axis=1,
    )
    routed = jnp.any(chosen, axis=1).astype(jnp.int32)
    slot_place = jnp.cumsum(routed, axis=0) - 1
    slot_hit = (routed[:, :, None] == 1) & (
        slot_place[:, :, None] == lax.broadcasted_iota(jnp.int32, (1, 1, capacity), 2)
    )
    select_rows = slot_hit.astype(jnp.bfloat16)
    outgoing = jnp.einsum(
        "rec,rd->ecd", select_rows, normed, preferred_element_type=jnp.float32
    ).astype(jnp.bfloat16)
    send_block = outgoing.reshape(
        expert_size, local_experts * capacity, dp_size, width_dev
    ).transpose(2, 0, 1, 3)
    send_flat = send_block.reshape(dp_size * expert_size, local_experts * capacity, width_dev)
    arrived = lax.all_to_all(send_flat, ("dp", "expert"), split_axis=0, concat_axis=0, tiled=True)
    arrived = arrived.reshape(dp_size * expert_size, local_experts, capacity, width_dev)
    gate_part = jnp.einsum("gjcd,jdf->gjcf", arrived, w_gate, preferred_element_type=jnp.float32)
    up_part = jnp.einsum("gjcd,jdf->gjcf", arrived, w_up, preferred_element_type=jnp.float32)
    gate_sum, up_sum = lax.psum((gate_part, up_part), "dp")
    active = (jax.nn.silu(gate_sum) * up_sum).astype(jnp.bfloat16)
    down_part = jnp.einsum(
        "gjcf,jfd->gjcd", active, w_down, preferred_element_type=jnp.float32
    ).astype(jnp.bfloat16)
    back_flat = down_part.reshape(dp_size * expert_size, local_experts * capacity, width_dev)
    returned = lax.all_to_all(back_flat, ("dp", "expert"), split_axis=0, concat_axis=0, tiled=True)
    returned = returned.reshape(dp_size, expert_size, local_experts, capacity, width_dev)
    returned = returned.transpose(1, 2, 3, 0, 4).reshape(experts_all, capacity, dp_size * width_dev)
    combine_coef = jnp.where(slot_hit, weight[:, :, None], jnp.zeros_like(weight)[:, :, None])
    mixed_part = jnp.einsum(
        "rec,ecd->rd", combine_coef, returned.astype(jnp.float32), precision=lax.Precision.HIGHEST
    )
    mixed = lax.psum_scatter(mixed_part, "tensor", scatter_dimension=1, tiled=True).astype(
        jnp.bfloat16
    )
    rows_b = queries_b.shape[1]
    heads_dev = queries_b.shape[2]
    channels = queries_b.shape[3]
    rows_owned = cache_b.shape[1]
    asked_blocks = queries_b[0].reshape(tensor_size, rows_owned, heads_dev, channels)
    pieces = lax.all_to_all(asked_blocks, "tensor", split_axis=0, concat_axis=0, tiled=True)
    head_count = pieces.shape[2]
    merged = pieces.transpose(1, 0, 2, 3).reshape(rows_owned, tensor_size * head_count, channels)
    result = attend(merged, cache_b[0], lengths_b[0])
    result = result.reshape(rows_owned, tensor_size, head_count, LAT).transpose(1, 0, 2, 3)
    answers = lax.all_to_all(result, "tensor", split_axis=0, concat_axis=0, tiled=True)
    latent = answers.reshape(rows_b, heads_dev, LAT)
    latent_b = latent.reshape(1, rows_b, heads_dev, LAT)
    return (mixed, latent_b)


def solution(mesh):
    placed = (
        P(("dp", "expert"), None),
        P(),
        P(("dp", "expert"), None),
        P(("dp", "expert"), None),
        P("expert", "dp", "tensor"),
        P("expert", "dp", "tensor"),
        P("expert", "tensor", "dp"),
        P(("dp", "expert"), None, "tensor", None),
        P(("dp", "expert"), "tensor", None, None),
        P(("dp", "expert"), "tensor"),
    )
    return jax.shard_map(
        shards,
        mesh=mesh,
        in_specs=placed,
        out_specs=(P(("dp", "expert"), "tensor"), P(("dp", "expert"), None, "tensor", None)),
        check_vma=False,
    )
```

profile of v0, /device:TPU:1, one launch (start us, length us, event | category | flops | bytes accessed | tf_op | source)
XLA Modules:
  0.0 342.6 jit_solution(13411539265890951869)
XLA Ops:
  7.2 0.0 copy-start
  7.2 0.0 all-reduce.3.cloned.1.call-start
  7.2 0.8 copy.44
  8.1 0.1 fusion.32
  8.2 1.1 fusion.19
  9.3 3.2 convolution_convert_fusion
  12.5 6.2 %reshape.73 = bf16[16,12,4,1792]{3,2,0,1:T(4,128)(2,1)} reshape(bf16[16,12,7168]{2,0,1:T(8,128)(2,1)} %convolution_convert_fusion) | data formatting | bytes 5505024 | tf_op jit(solution)/shard_map/reshape | solution.py:68
  18.7 3.3 copy.47
  22.1 0.0 copy-start.4
  22.1 99.5 %all_to_all.20 = bf16[64,12,1792]{2,1,0:T(8,128)(2,1)S(1)} all-to-all(bf16[64,12,1792]{2,1,0:T(8,128)(2,1)S(1)} %bitcast.59), channel_id=1, replica_groups=mesh['dp'=4,'tensor'=8,'expert'=16] {'dp','expert'}, dimensions={0} | all-to-all | bytes 5505024 | tf_op jit(solution)/shard_map/all_to_all | solution.py:72
  121.6 0.0 copy-done.4
  121.6 0.0 copy-start.5
  121.6 1.9 fusion.5
  123.5 0.0 copy-done.5
  123.5 1.9 fusion.8
  125.4 0.0 all-reduce.3.cloned.1.call-update
  125.5 6.8 %all-to-all-start.2 = ((bf16[8,2,16,576]{3,2,1,0:T(8,128)(2,1)}), bf16[8,2,16,576]{3,2,1,0:T(8,128)(2,1)S(1)}, u32[]{:S(2)}, u32[]{:S(2)}) async-start(bf16[8,2,16,576]{3,2,1,0:T(8,128)(2,1)} %bitcast.20), calls=%async_computation.3 | async-start | bytes 655360 | tf_op jit(solution)/shard_map/all_to_all | solution.py:97
  132.3 51.3 %all-reduce.3.cloned.1.call-done = (f32[64,1,12,256]{3,0,2,1:T(8,128)}, f32[64,1,12,256]{3,0,2,1:T(8,128)}) async-done(((f32[64,1,12,256]{3,0,2,1:T(8,128)}, f32[64,1,12,256]{3,0,2,1:T(8,128)}), (f32[64,1,12,256]{3,0,2,1:T(8,128)}, f32[64,1,12,256]{3,0,2,1:T(8,128)})) %all-reduce.3.cloned.1.call-update) | async-done | bytes 1572880 | tf_op jit(solution)/shard_map/psum | solution.py:76
  183.6 0.0 copy-done
  183.6 2.3 convolution_convert_fusion.1
  186.0 3.4 copy.50
  189.3 0.0 copy-start.2
  189.3 0.0 copy-start.1
  189.3 0.0 all-to-all-done.2
  189.3 10.2 %all-to-all-start.1 = ((bf16[64,12,1792]{2,1,0:T(8,128)(2,1)}), bf16[64,12,1792]{2,1,0:T(8,128)(2,1)}, u32[]{:S(2)}, u32[]{:S(2)}) async-start(bf16[64,12,1792]{2,1,0:T(8,128)(2,1)} %copy.50), calls=%async_computation.1 | async-start | bytes 7340032 | tf_op jit(solution)/shard_map/all_to_all | solution.py:82
  199.6 0.2 reduce-scatter.2.cloned.1.call-start
  199.8 0.0 copy-done.2
  199.8 0.1 copy.45
  199.9 0.0 copy-done.1
  199.9 0.3 copy.53
  200.2 0.1 select_reduce_fusion
  200.3 83.9 %all-to-all-done.1 = bf16[64,12,1792]{2,1,0:T(8,128)(2,1)} async-done(((bf16[64,12,1792]{2,1,0:T(8,128)(2,1)}), bf16[64,12,1792]{2,1,0:T(8,128)(2,1)}, u32[]{:S(2)}, u32[]{:S(2)}) %all-to-all-start.1) | async-done | bytes 2752544 | tf_op jit(solution)/shard_map/all_to_all | solution.py:82
  284.2 5.7 %copy.72 = bf16[4,16,1,12,1792]{4,0,1,3,2:T(4,128)(2,1)} copy(bf16[4,16,1,12,1792]{4,3,1,0,2:T(8,128)(2,1)} %bitcast.16) | data formatting | bytes 5505024 | tf_op jit(solution)/shard_map/reshape | solution.py:83
  289.9 5.9 %reshape.80 = bf16[16,12,7168]{2,0,1:T(8,128)(2,1)} reshape(bf16[16,1,12,4,1792]{4,3,0,2,1:T(4,128)(2,1)} %bitcast.61) | data formatting | bytes 5505024 | tf_op jit(solution)/shard_map/reshape | solution.py:84
  295.8 0.0 copy-start.3
  295.8 5.5 %convolution_bitcast_fusion = f32[16,7168]{1,0:T(8,128)} fusion(bf16[16,12,7168]{2,0,1:T(8,128)(2,1)} %reshape.80, f32[16,16]{1,0:T(8,128)S(1)} %select_reduce_fusion, s32[16,16]{1,0:T(8,128)S(1)} %broadcast_add_fusion, pred[16,16]{1,0:T(8,128)(4,1)S(1)} %get-tuple-element.4), kind=kOutput, calls=%fused_computation.2 | convolution fusion | flops 264250368 | bytes 3213568 | tf_op jit(solution)/shard_map/rec,ecd->rd/dot_general | solution.py:86
  301.3 0.0 reduce-scatter.2.cloned.1.call-update
  301.3 0.0 copy-done.3
  301.4 0.3 fusion.13
  301.6 0.2 fusion.42
  301.8 0.6 convolution_convert_fusion.2
  302.4 18.1 %all_to_all.21 = bf16[8,2,16,512]{3,2,1,0:T(8,128)(2,1)S(1)} all-to-all(bf16[8,2,16,512]{3,2,1,0:T(8,128)(2,1)S(1)} %bitcast.65), channel_id=1, replica_groups=mesh['dp'=4,'tensor'=8,'expert'=16] {'tensor'}, dimensions={0} | all-to-all | bytes 524288 | tf_op jit(solution)/shard_map/all_to_all | solution.py:102
  320.6 13.0 %reduce-scatter.2.cloned.1.call-done = f32[16,896]{1,0:T(8,128)} async-done(((f32[16,7168]{1,0:T(8,128)}), f32[16,896]{1,0:T(8,128)}) %reduce-scatter.2.cloned.1.call-update) | async-done | bytes 57360 | tf_op jit(solution)/shard_map/reduce_scatter | solution.py:89
  333.6 1.4 convert_element_type.46
  335.0 0.7 copy.77
  (6 shorter events, 0.1 us)
Async XLA Ops:
  7.2 176.4 %copy-start = (bf16[1,256,1792]{2,1,0:T(8,128)(2,1)S(1)}, bf16[1,256,1792]{2,1,0:T(8,128)(2,1)}, u32[]{:S(2)}) copy-start(bf16[1,256,1792]{2,1,0:T(8,128)(2,1)} %param.16) | copy-start | bytes 2752516
  7.2 176.4 %all-reduce.3.cloned.1.call-start = ((), (), s32[]{:S(2)}) async-start(), calls=%async_computation.6 | async-start | bytes 3145728 | tf_op jit(solution)/shard_map/psum | solution.py:76
  22.1 99.5 %copy-start.4 = (bf16[1,1792,256]{2,1,0:T(8,128)(2,1)S(1)}, bf16[1,1792,256]{2,1,0:T(8,128)(2,1)}, u32[]{:S(2)}) copy-start(bf16[1,1792,256]{2,1,0:T(8,128)(2,1)} %param.14) | copy-start | bytes 2752516
  121.6 1.9 copy-start.5
  125.5 63.9 %all-to-all-start.2 = ((bf16[8,2,16,576]{3,2,1,0:T(8,128)(2,1)}), bf16[8,2,16,576]{3,2,1,0:T(8,128)(2,1)S(1)}, u32[]{:S(2)}, u32[]{:S(2)}) async-start(bf16[8,2,16,576]{3,2,1,0:T(8,128)(2,1)} %bitcast.20), calls=%async_computation.3 | async-start | bytes 655360 | tf_op jit(solution)/shard_map/all_to_all | solution.py:97
  189.3 10.5 %copy-start.2 = (f32[16,8]{0,1:T(8,128)S(1)}, f32[16,8]{0,1:T(8,128)}, u32[]{:S(2)}) copy-start(f32[16,8]{0,1:T(8,128)} %param.13) | copy-start | bytes 1540
  189.3 10.6 %copy-start.1 = (bf16[1,2,256,576]{2,3,1,0:T(8,128)(2,1)S(1)}, bf16[1,2,256,576]{2,3,1,0:T(8,128)(2,1)}, u32[]{:S(2)}) copy-start(bf16[1,2,256,576]{2,3,1,0:T(8,128)(2,1)} %param.18) | copy-start | bytes 1769476
  189.3 94.9 %all-to-all-start.1 = ((bf16[64,12,1792]{2,1,0:T(8,128)(2,1)}), bf16[64,12,1792]{2,1,0:T(8,128)(2,1)}, u32[]{:S(2)}, u32[]{:S(2)}) async-start(bf16[64,12,1792]{2,1,0:T(8,128)(2,1)} %copy.50), calls=%async_computation.1 | async-start | bytes 7340032 | tf_op jit(solution)/shard_map/all_to_all | solution.py:82
  199.6 134.0 %reduce-scatter.2.cloned.1.call-start = ((), (), s32[]{:S(2)}) async-start(), calls=%async_computation.5 | async-start | bytes 516096 | tf_op jit(solution)/shard_map/reduce_scatter | solution.py:89
  295.8 5.5 %copy-start.3 = (s32[1,2]{1,0:T(1,128)S(1)}, s32[1,2]{1,0:T(1,128)}, u32[]{:S(2)}) copy-start(s32[1,2]{1,0:T(1,128)} %param.19) | copy-start | bytes 28
Sparse Core Ops, SparseCore 0:
  125.6 57.9 all-reduce.2
  301.5 32.0 reduce-scatter.1
where the time goes:
time: 347 us; the launch traced here: 343 us
  waiting for transfers between devices  148 us (43%)
  blocking collectives  118 us (34%)
  local copies, waits for them, and re-layouts  26.5 us (8%)
  starting transfers between devices  17.3 us (5%)
  matrix products  15.7 us (5%)
  between operations  14.1 us (4%)
    all_to_all x1, blocking collectives, shards(): lax.all_to_all(send_flat, ('dp', 'expert'), split_axis=0, concat_axis=0,...  99.5 us
    all_to_all x1, waiting for transfers between devices, shards(): lax.all_to_all(back_flat, ('dp', 'expert'), split_axis=0, concat_axis=0,...  83.9 us
    psum x1, waiting for transfers between devices, shards(): gate_sum, up_sum = lax.psum((gate_part, up_part), 'dp')  51.3 us
    all_to_all x1, blocking collectives, shards(): lax.all_to_all(result, 'tensor', split_axis=0, concat_axis=0, tiled=True)  18.1 us
    reduce_scatter x1, waiting for transfers between devices, shards(): lax.psum_scatter(mixed_part, 'tensor', scatter_dimension=1, tiled=True)  13 us
    all_to_all x1, starting transfers between devices, shards(): lax.all_to_all(back_flat, ('dp', 'expert'), split_axis=0, concat_axis=0,...  10.2 us
  transfers between devices with their start and end apart: 4, of which 3 were waited for; matrix products, arithmetic and copies ran while one was open for 2% of the time, Pallas kernels for 0%

commit v1 on v0

v1 whole, which is shorter than its diff:
```python
import functools

import jax
import jax.numpy as jnp
from jax import lax
from jax.experimental import pallas as pl
from jax.experimental.pallas import tpu as pltpu
from jax.sharding import Mesh, PartitionSpec as P

LAT = 512
BF = jnp.bfloat16
F32 = jnp.float32
score_scale = 192.0 ** (-0.5)
VMEM = pl.BlockSpec(memory_space=pltpu.VMEM)
PARAMS = pltpu.CompilerParams(vmem_limit_bytes=48 * 1024 * 1024)


def norm_kernel(tokens_ref, gain_ref, out_ref):
    values = tokens_ref[...].astype(F32)
    row_scale = lax.rsqrt(jnp.mean(values * values, axis=-1, keepdims=True) + 1e-06)
    normed = (values * row_scale * gain_ref[...]).astype(BF)
    parts, _, width = out_ref.shape
    for part in range(parts):
        out_ref[part] = normed[:, part * width : (part + 1) * width]


def gate_up_kernel(rows_ref, gate_ref, up_ref, out_ref):
    z_count, cores, x_count, rows, width = rows_ref.shape
    me = lax.axis_index("c")
    flat = rows_ref[...].reshape(z_count * cores * x_count * rows, width)
    hidden = gate_ref.shape[1]
    for number, weight in enumerate((gate_ref, up_ref)):
        part = jnp.dot(flat, weight[...], preferred_element_type=F32).astype(BF)
        part = part.reshape(z_count, cores, x_count, rows, hidden)
        for core in range(cores):
            place = lax.rem(core + me, cores)
            for x in range(x_count):
                out_ref[x, place, :, :, number * hidden : (number + 1) * hidden] = part[:, core, x]


def active_kernel(parts_ref, out_ref):
    hidden = out_ref.shape[1]
    total = parts_ref[0].astype(F32)
    for x in range(1, parts_ref.shape[0]):
        total = total + parts_ref[x].astype(F32)
    gate, up = total[:, :hidden], total[:, hidden:]
    out_ref[...] = (gate / (1.0 + jnp.exp(-gate)) * up).astype(BF)


def down_kernel(mine_ref, other_ref, coef_ref, *refs):
    weights, (keep_ref, send_ref) = refs[:-2], refs[-2:]
    x_count = len(weights)
    me = lax.axis_index("x")
    half = keep_ref.shape[1]
    coef = coef_ref[...]
    for shift, weight in enumerate(weights):
        place = lax.rem(me + x_count - shift, x_count)
        first = jnp.dot(mine_ref[...], weight[0], preferred_element_type=F32).astype(BF).astype(F32)
        second = jnp.dot(other_ref[...], weight[1], preferred_element_type=F32).astype(BF).astype(F32)
        total = (first + second) * coef
        keep_ref[place] = total[:half]
        send_ref[place] = total[half:].astype(BF)


def attend(queries, cache, lengths):
    scores = (
        jnp.einsum("rhc,rlc->rhl", queries, cache, preferred_element_type=F32) * score_scale
    )
    live_mask = lax.broadcasted_iota(jnp.int32, scores.shape, 2) < lengths[:, None, None]
    scores = jnp.where(live_mask, scores, -1e30)
    row_max = jnp.max(scores, axis=2, keepdims=True)
    exp_terms = jnp.exp(scores - row_max)
    softmax_bf = (exp_terms / jnp.sum(exp_terms, axis=2, keepdims=True)).astype(BF)
    latent = jnp.einsum("rhl,rlc->rhc", softmax_bf, cache[:, :, :LAT], preferred_element_type=F32)
    return latent.astype(BF)


def attention(queries_b, cache_b, lengths_b):
    rows_b, heads_dev, channels = queries_b.shape[1:]
    tensor_size = lax.axis_size("k") * lax.axis_size("h")
    rows_owned = cache_b.shape[1]
    asked = queries_b[0].reshape(tensor_size, rows_owned, heads_dev, channels)
    pieces = lax.all_to_all(asked, ("k", "h"), split_axis=0, concat_axis=0, tiled=True)
    merged = pieces.transpose(1, 0, 2, 3).reshape(rows_owned, tensor_size * heads_dev, channels)
    result = attend(merged, cache_b[0], lengths_b[0])
    result = result.reshape(rows_owned, tensor_size, heads_dev, LAT).transpose(1, 0, 2, 3)
    answers = lax.all_to_all(result, ("k", "h"), split_axis=0, concat_axis=0, tiled=True)
    return answers.reshape(1, rows_b, heads_dev, LAT)


def swap(array, axis):
    return lax.ppermute(array, axis, [(0, 1), (1, 0)])


def shards(
    tokens_a,
    norm_gain,
    expert_ids,
    route_weights,
    w_gate,
    w_up,
    w_down,
    queries_b,
    cache_b,
    lengths_b,
):
    x_size, z_size, cores = lax.axis_size("x"), lax.axis_size("z"), lax.axis_size("c")
    rows = tokens_a.shape[0]
    width = w_gate.shape[1]
    hidden = w_gate.shape[2]
    experts = z_size * cores
    group_rows = experts * rows

    normed = pl.pallas_call(
        norm_kernel,
        out_shape=jax.ShapeDtypeStruct((x_size, rows, width), BF),
        in_specs=[VMEM, VMEM],
        out_specs=VMEM,
        compiler_params=PARAMS,
        name="norm_rows",
    )(tokens_a, norm_gain.reshape(1, -1))
    sliced = lax.all_to_all(normed, "x", split_axis=0, concat_axis=0, tiled=True)
    gathered = lax.all_gather(
        sliced.reshape(x_size * rows, width), ("z", "c"), axis=0, tiled=True
    ).reshape(z_size, cores, x_size, rows, width)

    side = lax.axis_index("h")
    columns = w_down.shape[2] // 2
    left, right = w_down[0][:, :columns], w_down[0][:, columns:]
    w_mine = jnp.where(side == 0, left, right)
    w_theirs = swap(jnp.where(side == 0, right, left), "h")
    w_pair = jnp.stack([w_mine, w_theirs])
    w_all = [w_pair] + [
        lax.ppermute(w_pair, "x", [(i, (i + s) % x_size) for i in range(x_size)])
        for s in range(1, x_size)
    ]

    chosen = expert_ids.T[None] == lax.broadcasted_iota(jnp.int32, (experts, 1, 1), 0)
    weight = jnp.sum(jnp.where(chosen, route_weights.T[None], 0.0), axis=1)
    coef = lax.all_to_all(weight, ("z", "c"), split_axis=0, concat_axis=0, tiled=True)
    coef = coef.reshape(z_size, cores, rows)
    core = lax.axis_index("c")
    coef = jnp.where(
        core == 0,
        jnp.stack([coef[:, 0], coef[:, 1]]),
        jnp.stack([coef[:, 1], coef[:, 0]]),
    ).reshape(group_rows, 1)

    latent_b = attention(queries_b, cache_b, lengths_b)

    steps = 2
    partial = pl.pallas_call(
        gate_up_kernel,
        grid=(steps,),
        out_shape=jax.ShapeDtypeStruct((x_size, cores, z_size, rows, 2 * hidden), BF),
        in_specs=[
            pl.BlockSpec((z_size // steps, cores, x_size, rows, width), lambda i: (i, 0, 0, 0, 0)),
            pl.BlockSpec((width, hidden), lambda i: (0, 0)),
            pl.BlockSpec((width, hidden), lambda i: (0, 0)),
        ],
        out_specs=pl.BlockSpec(
            (x_size, cores, z_size // steps, rows, 2 * hidden), lambda i: (0, 0, i, 0, 0)
        ),
        compiler_params=PARAMS,
        cost_estimate=pl.CostEstimate(
            flops=4 * x_size * group_rows * width * hidden,
            bytes_accessed=2 * x_size * group_rows * (width + 2 * hidden) + 4 * width * hidden,
            transcendentals=0,
        ),
        name="gate_up",
    )(gathered, w_gate[0], w_up[0])
    partial = partial.reshape(x_size, group_rows, 2 * hidden)
    parts = lax.all_to_all(partial, "x", split_axis=0, concat_axis=0, tiled=True)
    active = pl.pallas_call(
        active_kernel,
        out_shape=jax.ShapeDtypeStruct((group_rows, hidden), BF),
        in_specs=[VMEM],
        out_specs=VMEM,
        compiler_params=PARAMS,
        name="active_rows",
    )(parts)
    active_other = swap(active, "h")

    half = group_rows // cores
    keep, send = pl.pallas_call(
        down_kernel,
        out_shape=(
            jax.ShapeDtypeStruct((x_size, half, columns), F32),
            jax.ShapeDtypeStruct((x_size, half, columns), BF),
        ),
        in_specs=[VMEM] * (3 + x_size),
        out_specs=(VMEM, VMEM),
        compiler_params=PARAMS,
        name="down_rows",
    )(active, active_other, coef, *w_all)
    both = (keep + swap(send, "c").astype(F32)).astype(BF)
    by_y = lax.all_to_all(both, "k", split_axis=0, concat_axis=0, tiled=True)
    sum_y = jnp.sum(by_y.astype(F32), axis=0).astype(BF).reshape(z_size, rows, columns)
    by_z = lax.all_to_all(sum_y, "z", split_axis=0, concat_axis=0, tiled=True)
    mixed = jnp.sum(by_z.astype(F32), axis=0).astype(BF)
    return (mixed, latent_b)


def solution(mesh):
    x_size, y_size, e_size = (mesh.shape[name] for name in ("dp", "tensor", "expert"))
    cores = 2
    fine = Mesh(
        mesh.devices.reshape(x_size, y_size // 2, 2, e_size // cores, cores),
        ("x", "k", "h", "z", "c"),
    )
    rows, tensor, expert = ("x", "z", "c"), ("k", "h"), ("z", "c")
    placed = (
        P(rows, None),
        P(),
        P(rows, None),
        P(rows, None),
        P(expert, "x", tensor),
        P(expert, "x", tensor),
        P(expert, tensor, "x"),
        P(rows, None, tensor, None),
        P(rows, tensor, None, None),
        P(rows, tensor),
    )
    return jax.shard_map(
        shards,
        mesh=fine,
        in_specs=placed,
        out_specs=(P(rows, tensor), P(rows, None, tensor, None)),
        check_vma=False,
    )
```

time: 347 us -> 225 us (0.65)
  blocking collectives: 118 us -> 10.2 us
  starting transfers between devices: 17.3 us -> 48.9 us
  local copies, waits for them, and re-layouts: 26.5 us -> 3.57 us
  waiting for transfers between devices: 148 us -> 129 us
  matrix products: 15.7 us -> 0.85 us
  Pallas kernels: 0 us -> 9.34 us
    all_to_all x2 -> x1, blocking collectives: 118 us -> 10.2 us  [shards(): lax.all_to_all(normed, 'x', split_axis=0, concat_axis=0, tiled=True)]
    psum x1 -> x0, waiting for transfers between devices: 51.3 us -> none  [shards(): gate_sum, up_sum = lax.psum((gate_part, up_part), 'dp')]
    all_gather x0 -> x1, waiting for transfers between devices: none -> 45.3 us  [shards(): lax.all_gather(sliced.reshape(x_size * rows, width), ('z', 'c'), axis=0,...]
    all_to_all x2 -> x6, waiting for transfers between devices: 83.9 us -> 57.6 us  [the longest x1 21.4 us: shards(): by_y = lax.all_to_all(both, 'k', split_axis=0, concat_axis=0, tiled=True)]
    ppermute x0 -> x6, waiting for transfers between devices: none -> 25.7 us  [the longest x3 25.7 us: shards(): lax.ppermute(w_pair, 'x', [(i, (i + s) % x_size) for i in range(x_size)])]
    ppermute x0 -> x6, starting transfers between devices: none -> 20.4 us  [the longest x3 10.8 us: shards(): lax.ppermute(w_pair, 'x', [(i, (i + s) % x_size) for i in range(x_size)])]
    reshape x4 -> x1, local copies, waits for them, and re-layouts: 17.8 us -> 0.73 us  [attention(): result.reshape(rows_owned, tensor_size, heads_dev, LAT)]
    dot_general x6 -> x1, matrix products: 15.1 us -> 0.27 us  [attend(): jnp.einsum('rhc,rlc->rhl', queries, cache, preferred_element_type=F32)]
  transfers between devices with their start and end apart: 4 -> 13, of which waited for: 3 -> 9; matrix products, arithmetic and copies ran while one was open for 2% -> 3% of each run, Pallas kernels for 0% -> 2%
where the time goes in v1:
time: 225 us; the launch traced here: 222 us
  waiting for transfers between devices  129 us (57%)
  starting transfers between devices  48.9 us (22%)
  between operations  14.2 us (6%)
  blocking collectives  10.2 us (5%)
  Pallas kernels  9.34 us (4%)
  other arithmetic  6.35 us (3%)
  local copies, waits for them, and re-layouts  3.57 us (2%)
    all_gather x1, waiting for transfers between devices, shards(): lax.all_gather(sliced.reshape(x_size * rows, width), ('z', 'c'), axis=0,...  45.3 us
    ppermute x3, waiting for transfers between devices, shards(): lax.ppermute(w_pair, 'x', [(i, (i + s) % x_size) for i in range(x_size)])  25.7 us
    all_to_all x1, waiting for transfers between devices, shards(): by_y = lax.all_to_all(both, 'k', split_axis=0, concat_axis=0, tiled=True)  21.4 us
    all_to_all x1, waiting for transfers between devices, attention(): lax.all_to_all(asked, ('k', 'h'), split_axis=0, concat_axis=0, tiled=True)  11.1 us
    ppermute x3, starting transfers between devices, shards(): lax.ppermute(w_pair, 'x', [(i, (i + s) % x_size) for i in range(x_size)])  10.8 us
    all_to_all x1, blocking collectives, shards(): lax.all_to_all(normed, 'x', split_axis=0, concat_axis=0, tiled=True)  10.2 us
    ppermute x3, starting transfers between devices, swap(): return lax.ppermute(array, axis, [(0, 1), (1, 0)])  9.65 us
    all_to_all x1, waiting for transfers between devices, attention(): lax.all_to_all(result, ('k', 'h'), split_axis=0, concat_axis=0, tiled=True)  9.34 us
  transfers between devices with their start and end apart: 13, of which 9 were waited for; matrix products, arithmetic and copies ran while one was open for 3% of the time, Pallas kernels for 2%

profile of v1, /device:TPU:1, one launch (start us, length us, event | category | flops | bytes accessed | tf_op | source)
XLA Modules:
  0.0 222.0 jit_solution(16394492084964804599)
XLA Ops:
  7.2 0.0 all-gather.2.cloned.1.call-start
  7.2 0.9 copy-done
  8.2 0.7 copy-done.1
  8.9 0.2 norm_rows.1
  9.1 10.2 %all_to_all.39 = bf16[4,16,1792]{2,1,0:T(8,128)(2,1)} all-to-all(bf16[4,16,1792]{2,1,0:T(8,128)(2,1)S(1)} %norm_rows.1), channel_id=1, replica_groups=mesh['x'=4,'k'=4,'h'=2,'z'=8,'c'=2] {'x'}, dimensions={0} | all-to-all | bytes 458752 | tf_op jit(solution)/shard_map/all_to_all | solution.py:122
  19.3 0.0 all-gather.2.cloned.1.call-update
  19.4 1.2 select_bitcast_fusion
  20.6 3.2 %collective-permute-start.1 = (bf16[256,896]{1,0:T(8,128)(2,1)S(1)}, bf16[256,896]{1,0:T(8,128)(2,1)S(1)}, u32[]{:S(2)}, u32[]{:S(2)}) collective-permute-start(bf16[256,896]{1,0:T(8,128)(2,1)S(1)} %get-tuple-element.7), channel_id=1, source_target_pairs={{0,16},{16,0},{1,17},{17,1},{2,18},{18,2},{3,19},{19,3},{4,20},{20... | collective-permute-start | bytes 1376264 | tf_op jit(solution)/shard_map/ppermute | solution.py:92
  23.9 45.3 %all-gather.2.cloned.1.call-done = bf16[1024,1792]{1,0:T(8,128)(2,1)} async-done(((bf16[64,1792]{1,0:T(8,128)(2,1)}), bf16[1024,1792]{1,0:T(8,128)(2,1)}) %all-gather.2.cloned.1.call-update) | async-done | bytes 3670032 | tf_op jit(solution)/shard_map/all_gather | solution.py:123
  69.1 4.6 %gate_up.1 = bf16[4,2,8,16,512]{4,3,2,1,0:T(8,128)(2,1)} custom-call(bf16[8,2,4,16,1792]{4,3,2,1,0:T(8,128)(2,1)} %bitcast.52, bf16[1792,256]{1,0:T(8,128)(2,1)S(1)} %bitcast.36, bf16[1792,256]{1,0:T(8,128)(2,1)S(1)} %bitcast.37), custom_call_target="tpu_custom_call" | custom-call | flops 1879048192 | bytes 6553600 | tf_op jit(solution)/shard_map/gate_up/pallas_call | solution.py:152
  73.7 4.1 %all-to-all-start.1 = ((bf16[4,256,512]{2,1,0:T(8,128)(2,1)}), bf16[4,256,512]{2,1,0:T(8,128)(2,1)S(1)}, u32[]{:S(2)}, u32[]{:S(2)}) async-start(bf16[4,256,512]{2,1,0:T(8,128)(2,1)} %bitcast.5), calls=%async_computation.1 | async-start | bytes 2097152 | tf_op jit(solution)/shard_map/all_to_all | solution.py:173
  77.8 0.0 collective-permute-done.1
  77.8 0.1 pad_maximum_fusion.refs_0_
  77.9 3.4 %collective-permute-start.2 = (bf16[2,256,896]{2,1,0:T(8,128)(2,1)S(1)}, bf16[2,256,896]{2,1,0:T(8,128)(2,1)S(1)}, u32[]{:S(2)}, u32[]{:S(2)}) collective-permute-start(bf16[2,256,896]{2,1,0:T(8,128)(2,1)S(1)} %pad_maximum_fusion.refs_0_), channel_id=1, source_target_pairs={{0,128},{128,256},{256,384},{384,0},{1,129},{129,257},{257,385},{3... | collective-permute-start | bytes 2752520 | tf_op jit(solution)/shard_map/ppermute | solution.py:134
  81.3 4.3 %collective-permute-start.3 = (bf16[2,256,896]{2,1,0:T(8,128)(2,1)S(1)}, bf16[2,256,896]{2,1,0:T(8,128)(2,1)}, u32[]{:S(2)}, u32[]{:S(2)}) collective-permute-start(bf16[2,256,896]{2,1,0:T(8,128)(2,1)S(1)} %pad_maximum_fusion.refs_0_), channel_id=1, source_target_pairs={{0,256},{128,384},{256,0},{384,128},{1,257},{129,385},{257,1},{385... | collective-permute-start | bytes 2752520 | tf_op jit(solution)/shard_map/ppermute | solution.py:134
  85.6 3.1 %collective-permute-start.4 = (bf16[2,256,896]{2,1,0:T(8,128)(2,1)S(1)}, bf16[2,256,896]{2,1,0:T(8,128)(2,1)}, u32[]{:S(2)}, u32[]{:S(2)}) collective-permute-start(bf16[2,256,896]{2,1,0:T(8,128)(2,1)S(1)} %pad_maximum_fusion.refs_0_), channel_id=1, source_target_pairs={{0,384},{128,0},{256,128},{384,256},{1,385},{129,1},{257,129},{385... | collective-permute-start | bytes 2752520 | tf_op jit(solution)/shard_map/ppermute | solution.py:134
  88.7 0.6 select_reduce_fusion
  89.4 3.2 %all-to-all-done.1.parts_ref = bf16[4,256,512]{2,1,0:T(8,128)(2,1)S(1)} async-done(((bf16[4,256,512]{2,1,0:T(8,128)(2,1)}), bf16[4,256,512]{2,1,0:T(8,128)(2,1)S(1)}, u32[]{:S(2)}, u32[]{:S(2)}) %all-to-all-start.1) | async-done | bytes 1048608 | tf_op jit(solution)/shard_map/all_to_all | solution.py:173
  92.5 6.6 %all-to-all-start.2 = ((f32[16,1,16]{2,1,0:T(1,128)}), f32[16,1,16]{2,1,0:T(1,128)S(1)}, u32[]{:S(2)}, u32[]{:S(2)}) async-start(f32[16,1,16]{2,1,0:T(1,128)} %bitcast.9), calls=%async_computation.2 | async-start | bytes 16384 | tf_op jit(solution)/shard_map/all_to_all | solution.py:140
  99.2 0.2 active_rows.1.mine_ref
  99.3 3.1 %collective-permute-start = (bf16[256,256]{1,0:T(8,128)(2,1)S(1)}, bf16[256,256]{1,0:T(8,128)(2,1)S(1)}, u32[]{:S(2)}, u32[]{:S(2)}) collective-permute-start(bf16[256,256]{1,0:T(8,128)(2,1)S(1)} %active_rows.1.mine_ref), channel_id=1, source_target_pairs={{0,16},{16,0},{1,17},{17,1},{2,18},{18,2},{3,19},{19,3},{4,20},{20... | collective-permute-start | bytes 393224 | tf_op jit(solution)/shard_map/ppermute | solution.py:92
  102.5 3.6 %all-to-all-done.2 = f32[16,1,16]{2,1,0:T(1,128)S(1)} async-done(((f32[16,1,16]{2,1,0:T(1,128)}), f32[16,1,16]{2,1,0:T(1,128)S(1)}, u32[]{:S(2)}, u32[]{:S(2)}) %all-to-all-start.2) | async-done | bytes 1056 | tf_op jit(solution)/shard_map/all_to_all | solution.py:140
  106.1 0.1 select_n.46.coef_ref
  106.2 5.6 %collective-permute-done.2.refs_1_ = bf16[2,256,896]{2,1,0:T(8,128)(2,1)S(1)} collective-permute-done((bf16[2,256,896]{2,1,0:T(8,128)(2,1)S(1)}, bf16[2,256,896]{2,1,0:T(8,128)(2,1)S(1)}, u32[]{:S(2)}, u32[]{:S(2)}) %collective-permute-start.2) | collective-permute-done | bytes 917536 | tf_op jit(solution)/shard_map/ppermute | solution.py:134
  111.8 20.1 %collective-permute-done.3.refs_2_ = bf16[2,256,896]{2,1,0:T(8,128)(2,1)} collective-permute-done((bf16[2,256,896]{2,1,0:T(8,128)(2,1)S(1)}, bf16[2,256,896]{2,1,0:T(8,128)(2,1)}, u32[]{:S(2)}, u32[]{:S(2)}) %collective-permute-start.3) | collective-permute-done | bytes 917536 | tf_op jit(solution)/shard_map/ppermute | solution.py:134
  132.0 0.0 collective-permute-done.4.refs_3_
  132.0 0.0 collective-permute-done.other_ref
  132.0 4.3 %down_rows.1 = (f32[4,128,896]{2,1,0:T(8,128)}, bf16[4,128,896]{2,1,0:T(8,128)(2,1)}) custom-call(bf16[256,256]{1,0:T(8,128)(2,1)S(1)} %active_rows.1.mine_ref, bf16[256,256]{1,0:T(8,128)(2,1)S(1)} %collective-permute-done.other_ref, f32[256,1]{1,0:T(8,128)S(1)} %select_n.46.coef_ref, bf16[2,256,896]{2,1,0:T(8,128)(2,1)S(1)} %pad_maximum_fusion.refs_0_, ...), custom_call_target="tpu_custom_call" | custom-call | tf_op jit(solution)/shard_map/down_rows/pallas_call | solution.py:185
  136.3 3.3 %collective-permute-start.5 = (bf16[4,128,896]{2,1,0:T(8,128)(2,1)}, bf16[4,128,896]{2,1,0:T(8,128)(2,1)S(1)}, u32[]{:S(2)}, u32[]{:S(2)}) collective-permute-start(bf16[4,128,896]{2,1,0:T(8,128)(2,1)} %get-tuple-element.5), channel_id=1, source_target_pairs={{0,1},{1,0},{2,3},{3,2},{4,5},{5,4},{6,7},{7,6},{8,9},{9,8},{10,11... | collective-permute-start | bytes 2752520 | tf_op jit(solution)/shard_map/ppermute | solution.py:92
  139.6 6.5 %all-to-all-start.5 = ((bf16[8,2,16,576]{3,2,1,0:T(8,128)(2,1)}), bf16[8,2,16,576]{3,2,1,0:T(8,128)(2,1)S(1)}, u32[]{:S(2)}, u32[]{:S(2)}) async-start(bf16[8,2,16,576]{3,2,1,0:T(8,128)(2,1)} %bitcast.18), calls=%async_computation.5 | async-start | bytes 655360 | tf_op jit(solution)/shard_map/all_to_all | solution.py:83
  146.1 0.0 collective-permute-done.5
  146.1 0.0 copy-start.4
  146.1 2.7 %add_convert_fusion = bf16[4,128,896]{2,1,0:T(8,128)(2,1)} fusion(f32[4,128,896]{2,1,0:T(8,128)} %get-tuple-element.4, bf16[4,128,896]{2,1,0:T(8,128)(2,1)S(1)} %collective-permute-done.5), kind=kLoop, calls=%fused_computation.1 | loop fusion | flops 1376256 | bytes 3670016 | tf_op jit(solution)/shard_map/convert_element_type | solution.py:196
  148.8 11.1 %all-to-all-done.5 = bf16[8,2,16,576]{3,2,1,0:T(8,128)(2,1)S(1)} async-done(((bf16[8,2,16,576]{3,2,1,0:T(8,128)(2,1)}), bf16[8,2,16,576]{3,2,1,0:T(8,128)(2,1)S(1)}, u32[]{:S(2)}, u32[]{:S(2)}) %all-to-all-start.5) | async-done | bytes 294944 | tf_op jit(solution)/shard_map/all_to_all | solution.py:83
  159.9 3.5 %all-to-all-start.3 = ((bf16[4,128,896]{2,1,0:T(8,128)(2,1)}), bf16[4,128,896]{2,1,0:T(8,128)(2,1)S(1)}, u32[]{:S(2)}, u32[]{:S(2)}) async-start(bf16[4,128,896]{2,1,0:T(8,128)(2,1)} %add_convert_fusion), calls=%async_computation.3 | async-start | bytes 1835008 | tf_op jit(solution)/shard_map/all_to_all | solution.py:197
  163.4 0.3 copy.31
  163.7 0.3 fusion.3
  164.0 0.2 fusion.9
  164.2 0.6 convolution_convert_fusion
  164.8 0.7 copy.40
  165.5 21.4 %all-to-all-done.3 = bf16[4,128,896]{2,1,0:T(8,128)(2,1)S(1)} async-done(((bf16[4,128,896]{2,1,0:T(8,128)(2,1)}), bf16[4,128,896]{2,1,0:T(8,128)(2,1)S(1)}, u32[]{:S(2)}, u32[]{:S(2)}) %all-to-all-start.3) | async-done | bytes 917536 | tf_op jit(solution)/shard_map/all_to_all | solution.py:197
  186.9 3.8 %all-to-all-start.6 = ((bf16[8,2,16,512]{3,2,1,0:T(8,128)(2,1)}), bf16[8,2,16,512]{3,2,1,0:T(8,128)(2,1)S(1)}, u32[]{:S(2)}, u32[]{:S(2)}) async-start(bf16[8,2,16,512]{3,2,1,0:T(8,128)(2,1)} %bitcast.34), calls=%async_computation.6 | async-start | bytes 524288 | tf_op jit(solution)/shard_map/all_to_all | solution.py:87
  190.7 0.9 reduce_sum.43
  191.5 9.3 %all-to-all-done.6 = bf16[8,2,16,512]{3,2,1,0:T(8,128)(2,1)S(1)} async-done(((bf16[8,2,16,512]{3,2,1,0:T(8,128)(2,1)}), bf16[8,2,16,512]{3,2,1,0:T(8,128)(2,1)S(1)}, u32[]{:S(2)}, u32[]{:S(2)}) %all-to-all-start.6) | async-done | bytes 262176 | tf_op jit(solution)/shard_map/all_to_all | solution.py:87
  200.9 3.9 %all-to-all-start.4 = ((bf16[8,16,896]{2,1,0:T(8,128)(2,1)}), bf16[8,16,896]{2,1,0:T(8,128)(2,1)S(1)}, u32[]{:S(2)}, u32[]{:S(2)}) async-start(bf16[8,16,896]{2,1,0:T(8,128)(2,1)} %bitcast.16), calls=%async_computation.4 | async-start | bytes 458752 | tf_op jit(solution)/shard_map/all_to_all | solution.py:199
  204.8 9.0 %all-to-all-done.4 = bf16[8,16,896]{2,1,0:T(8,128)(2,1)S(1)} async-done(((bf16[8,16,896]{2,1,0:T(8,128)(2,1)}), bf16[8,16,896]{2,1,0:T(8,128)(2,1)S(1)}, u32[]{:S(2)}, u32[]{:S(2)}) %all-to-all-start.4) | async-done | bytes 229408 | tf_op jit(solution)/shard_map/all_to_all | solution.py:199
  213.8 0.6 reduce_sum.44
  214.5 0.7 copy.42
  (16 shorter events, 0.1 us)
Async XLA Ops:
  7.2 62.0 %all-gather.2.cloned.1.call-start = ((), (), s32[]{:S(2)}) async-start(), calls=%async_computation.7 | async-start | bytes 3899392 | tf_op jit(solution)/shard_map/all_gather | solution.py:123
  7.2 0.9 copy-start
  8.1 0.7 copy-start.1
  8.9 60.2 %copy-start.2 = (bf16[1,1792,256]{2,1,0:T(8,128)(2,1)S(1)}, bf16[1,1792,256]{2,1,0:T(8,128)(2,1)}, u32[]{:S(2)}) copy-start(bf16[1,1792,256]{2,1,0:T(8,128)(2,1)} %param.14) | copy-start | bytes 2752516
  8.9 60.2 %copy-start.3 = (bf16[1,1792,256]{2,1,0:T(8,128)(2,1)S(1)}, bf16[1,1792,256]{2,1,0:T(8,128)(2,1)}, u32[]{:S(2)}) copy-start(bf16[1,1792,256]{2,1,0:T(8,128)(2,1)} %param.15) | copy-start | bytes 2752516
  20.6 57.2 %collective-permute-start.1 = (bf16[256,896]{1,0:T(8,128)(2,1)S(1)}, bf16[256,896]{1,0:T(8,128)(2,1)S(1)}, u32[]{:S(2)}, u32[]{:S(2)}) collective-permute-start(bf16[256,896]{1,0:T(8,128)(2,1)S(1)} %get-tuple-element.7), channel_id=1, source_target_pairs={{0,16},{16,0},{1,17},{17,1},{2,18},{18,2},{3,19},{19,3},{4,20},{20... | collective-permute-start | bytes 1376264 | tf_op jit(solution)/shard_map/ppermute | solution.py:92
  73.7 15.0 %copy-start.5 = (f32[16,8]{0,1:T(8,128)S(1)}, f32[16,8]{0,1:T(8,128)}, u32[]{:S(2)}) copy-start(f32[16,8]{0,1:T(8,128)} %param.13) | copy-start | bytes 1540
  73.7 15.0 %copy-start.6 = (s32[16,8]{0,1:T(8,128)S(1)}, s32[16,8]{0,1:T(8,128)}, u32[]{:S(2)}) copy-start(s32[16,8]{0,1:T(8,128)} %param.12) | copy-start | bytes 1540
  73.7 18.8 %all-to-all-start.1 = ((bf16[4,256,512]{2,1,0:T(8,128)(2,1)}), bf16[4,256,512]{2,1,0:T(8,128)(2,1)S(1)}, u32[]{:S(2)}, u32[]{:S(2)}) async-start(bf16[4,256,512]{2,1,0:T(8,128)(2,1)} %bitcast.5), calls=%async_computation.1 | async-start | bytes 2097152 | tf_op jit(solution)/shard_map/all_to_all | solution.py:173
  77.9 33.9 %collective-permute-start.2 = (bf16[2,256,896]{2,1,0:T(8,128)(2,1)S(1)}, bf16[2,256,896]{2,1,0:T(8,128)(2,1)S(1)}, u32[]{:S(2)}, u32[]{:S(2)}) collective-permute-start(bf16[2,256,896]{2,1,0:T(8,128)(2,1)S(1)} %pad_maximum_fusion.refs_0_), channel_id=1, source_target_pairs={{0,128},{128,256},{256,384},{384,0},{1,129},{129,257},{257,385},{3... | collective-permute-start | bytes 2752520 | tf_op jit(solution)/shard_map/ppermute | solution.py:134
  81.3 50.6 %collective-permute-start.3 = (bf16[2,256,896]{2,1,0:T(8,128)(2,1)S(1)}, bf16[2,256,896]{2,1,0:T(8,128)(2,1)}, u32[]{:S(2)}, u32[]{:S(2)}) collective-permute-start(bf16[2,256,896]{2,1,0:T(8,128)(2,1)S(1)} %pad_maximum_fusion.refs_0_), channel_id=1, source_target_pairs={{0,256},{128,384},{256,0},{384,128},{1,257},{129,385},{257,1},{385... | collective-permute-start | bytes 2752520 | tf_op jit(solution)/shard_map/ppermute | solution.py:134
  85.6 46.3 %collective-permute-start.4 = (bf16[2,256,896]{2,1,0:T(8,128)(2,1)S(1)}, bf16[2,256,896]{2,1,0:T(8,128)(2,1)}, u32[]{:S(2)}, u32[]{:S(2)}) collective-permute-start(bf16[2,256,896]{2,1,0:T(8,128)(2,1)S(1)} %pad_maximum_fusion.refs_0_), channel_id=1, source_target_pairs={{0,384},{128,0},{256,128},{384,256},{1,385},{129,1},{257,129},{385... | collective-permute-start | bytes 2752520 | tf_op jit(solution)/shard_map/ppermute | solution.py:134
  92.5 13.6 %all-to-all-start.2 = ((f32[16,1,16]{2,1,0:T(1,128)}), f32[16,1,16]{2,1,0:T(1,128)S(1)}, u32[]{:S(2)}, u32[]{:S(2)}) async-start(f32[16,1,16]{2,1,0:T(1,128)} %bitcast.9), calls=%async_computation.2 | async-start | bytes 16384 | tf_op jit(solution)/shard_map/all_to_all | solution.py:140
  99.3 32.6 %collective-permute-start = (bf16[256,256]{1,0:T(8,128)(2,1)S(1)}, bf16[256,256]{1,0:T(8,128)(2,1)S(1)}, u32[]{:S(2)}, u32[]{:S(2)}) collective-permute-start(bf16[256,256]{1,0:T(8,128)(2,1)S(1)} %active_rows.1.mine_ref), channel_id=1, source_target_pairs={{0,16},{16,0},{1,17},{17,1},{2,18},{18,2},{3,19},{19,3},{4,20},{20... | collective-permute-start | bytes 393224 | tf_op jit(solution)/shard_map/ppermute | solution.py:92
  136.3 9.8 %collective-permute-start.5 = (bf16[4,128,896]{2,1,0:T(8,128)(2,1)}, bf16[4,128,896]{2,1,0:T(8,128)(2,1)S(1)}, u32[]{:S(2)}, u32[]{:S(2)}) collective-permute-start(bf16[4,128,896]{2,1,0:T(8,128)(2,1)} %get-tuple-element.5), channel_id=1, source_target_pairs={{0,1},{1,0},{2,3},{3,2},{4,5},{5,4},{6,7},{7,6},{8,9},{9,8},{10,11... | collective-permute-start | bytes 2752520 | tf_op jit(solution)/shard_map/ppermute | solution.py:92
  139.6 20.2 %all-to-all-start.5 = ((bf16[8,2,16,576]{3,2,1,0:T(8,128)(2,1)}), bf16[8,2,16,576]{3,2,1,0:T(8,128)(2,1)S(1)}, u32[]{:S(2)}, u32[]{:S(2)}) async-start(bf16[8,2,16,576]{3,2,1,0:T(8,128)(2,1)} %bitcast.18), calls=%async_computation.5 | async-start | bytes 655360 | tf_op jit(solution)/shard_map/all_to_all | solution.py:83
  146.1 17.3 %copy-start.4 = (bf16[1,2,256,576]{2,3,1,0:T(8,128)(2,1)S(1)}, bf16[1,2,256,576]{2,3,1,0:T(8,128)(2,1)}, u32[]{:S(2)}) copy-start(bf16[1,2,256,576]{2,3,1,0:T(8,128)(2,1)} %param.18) | copy-start | bytes 1769476
  148.8 14.9 %copy-start.7 = (s32[1,2]{1,0:T(1,128)S(1)}, s32[1,2]{1,0:T(1,128)}, u32[]{:S(2)}) copy-start(s32[1,2]{1,0:T(1,128)} %param.19) | copy-start | bytes 28
  159.9 27.0 %all-to-all-start.3 = ((bf16[4,128,896]{2,1,0:T(8,128)(2,1)}), bf16[4,128,896]{2,1,0:T(8,128)(2,1)S(1)}, u32[]{:S(2)}, u32[]{:S(2)}) async-start(bf16[4,128,896]{2,1,0:T(8,128)(2,1)} %add_convert_fusion), calls=%async_computation.3 | async-start | bytes 1835008 | tf_op jit(solution)/shard_map/all_to_all | solution.py:197
  186.9 14.0 %all-to-all-start.6 = ((bf16[8,2,16,512]{3,2,1,0:T(8,128)(2,1)}), bf16[8,2,16,512]{3,2,1,0:T(8,128)(2,1)S(1)}, u32[]{:S(2)}, u32[]{:S(2)}) async-start(bf16[8,2,16,512]{3,2,1,0:T(8,128)(2,1)} %bitcast.34), calls=%async_computation.6 | async-start | bytes 524288 | tf_op jit(solution)/shard_map/all_to_all | solution.py:87
  200.9 12.9 %all-to-all-start.4 = ((bf16[8,16,896]{2,1,0:T(8,128)(2,1)}), bf16[8,16,896]{2,1,0:T(8,128)(2,1)S(1)}, u32[]{:S(2)}, u32[]{:S(2)}) async-start(bf16[8,16,896]{2,1,0:T(8,128)(2,1)} %bitcast.16), calls=%async_computation.4 | async-start | bytes 458752 | tf_op jit(solution)/shard_map/all_to_all | solution.py:199
Sparse Core Ops, SparseCore 0:
  19.5 49.5 all-gather.1

commit v2 on v1

v2 whole, which is shorter than its diff:
```python
import functools

import jax
import jax.numpy as jnp
from jax import lax
from jax.experimental import pallas as pl
from jax.experimental.pallas import tpu as pltpu
from jax.sharding import Mesh, PartitionSpec as P

LAT = 512
BF = jnp.bfloat16
F32 = jnp.float32
score_scale = 192.0 ** (-0.5)
VMEM = pl.BlockSpec(memory_space=pltpu.VMEM)
PARAMS = pltpu.CompilerParams(vmem_limit_bytes=48 * 1024 * 1024)
WIDE = pltpu.CompilerParams(vmem_limit_bytes=60 * 1024 * 1024)


def norm_kernel(tokens_ref, gain_ref, ids_ref, route_ref, out_ref):
    values = tokens_ref[...].astype(F32)
    row_scale = lax.rsqrt(jnp.mean(values * values, axis=-1, keepdims=True) + 1e-06)
    normed = (values * row_scale * gain_ref[...]).astype(BF)
    parts, _, columns = out_ref.shape
    width = normed.shape[1] // parts
    experts = lax.axis_size("z") * lax.axis_size("c")
    ids, route = ids_ref[...], route_ref[...]
    table = jnp.concatenate(
        [
            jnp.sum(jnp.where(ids == expert, route, 0.0), axis=0, keepdims=True)
            for expert in range(experts)
        ],
        axis=0,
    )
    high = table.astype(BF)
    low = (table - high.astype(F32)).astype(BF)
    both = jnp.concatenate([high.astype(F32), low.astype(F32)], axis=0).astype(BF)
    shape = (2 * experts, columns - width)
    spread = lax.broadcasted_iota(jnp.int32, shape, 0) == lax.broadcasted_iota(jnp.int32, shape, 1)
    extra = lax.dot_general(
        both, spread.astype(F32).astype(BF), (((0,), (0,)), ((), ())), preferred_element_type=F32
    ).astype(BF)
    for part in range(parts):
        out_ref[part, :, :width] = normed[:, part * width : (part + 1) * width]
        out_ref[part, :, width:columns] = extra


def gate_up_kernel(rows_ref, gate_ref, up_ref, out_ref):
    z_count, cores, x_count, rows, width = rows_ref.shape
    me = lax.axis_index("c")
    flat = rows_ref[...].reshape(z_count * cores * x_count * rows, width)
    hidden = gate_ref.shape[1]
    for number, weight in enumerate((gate_ref, up_ref)):
        part = jnp.dot(flat, weight[...], preferred_element_type=F32).astype(BF)
        part = part.reshape(z_count, cores, x_count, rows, hidden)
        for core in range(cores):
            place = 1 - lax.rem(core + me, cores)
            for x in range(x_count):
                out_ref[x, place, :, :, number * hidden : (number + 1) * hidden] = part[:, core, x]


def active_kernel(parts_ref, out_ref):
    hidden = out_ref.shape[1]
    total = parts_ref[0].astype(F32)
    for x in range(1, parts_ref.shape[0]):
        total = total + parts_ref[x].astype(F32)
    gate, up = total[:, :hidden], total[:, hidden:]
    out_ref[...] = (gate / (1.0 + jnp.exp(-gate)) * up).astype(BF)


def down_kernel(place_ref, mine_ref, other_ref, route_ref, *refs):
    (pair_ref, lower_ref, upper_ref), across = refs[:3], refs[3:5]
    added, out_ref = refs[5:-1], refs[-1]
    weights = [ref.at[half] for ref in (pair_ref, lower_ref, upper_ref) for half in (0, 1)]
    weights += across
    x_count = out_ref.shape[0]
    me = lax.axis_index("x")
    rows = mine_ref.shape[0]
    route = route_ref[...].reshape(rows, route_ref.shape[-1]).astype(F32)
    lane = lax.broadcasted_iota(jnp.int32, route.shape, 1)
    experts = lax.axis_size("z") * lax.axis_size("c")
    own = lax.axis_index("z") * lax.axis_size("c") + lax.axis_index("c")
    hit = (lane == own) | (lane == own + experts)
    coef = jnp.sum(jnp.where(hit, route, 0.0), axis=1, keepdims=True)
    for step, number in ((0, 0), (3, 2), (1, 4), (2, 6)):
        place = lax.rem(me + step, x_count)
        first = jnp.dot(mine_ref[...], weights[number][...], preferred_element_type=F32)
        second = jnp.dot(other_ref[...], weights[number + 1][...], preferred_element_type=F32)
        total = (first.astype(BF).astype(F32) + second.astype(BF).astype(F32)) * coef
        for ref in added:
            total = total + ref[place].astype(F32)
        out_ref[place] = total.astype(BF)


def attend(queries, cache, lengths):
    scores = (
        jnp.einsum("rhc,rlc->rhl", queries, cache, preferred_element_type=F32) * score_scale
    )
    live_mask = lax.broadcasted_iota(jnp.int32, scores.shape, 2) < lengths[:, None, None]
    scores = jnp.where(live_mask, scores, -1e30)
    row_max = jnp.max(scores, axis=2, keepdims=True)
    exp_terms = jnp.exp(scores - row_max)
    softmax_bf = (exp_terms / jnp.sum(exp_terms, axis=2, keepdims=True)).astype(BF)
    latent = jnp.einsum("rhl,rlc->rhc", softmax_bf, cache[:, :, :LAT], preferred_element_type=F32)
    return latent.astype(BF)


def attention(queries_b, cache_b, lengths_b):
    heads_dev, channels = queries_b.shape[2:]
    tensor_size = lax.axis_size("k") * lax.axis_size("h")
    rows_owned = cache_b.shape[1]
    asked = queries_b[0].reshape(tensor_size, rows_owned, heads_dev, channels)
    pieces = lax.all_to_all(asked, ("k", "h"), split_axis=0, concat_axis=0, tiled=True)
    merged = pieces.transpose(1, 0, 2, 3).reshape(rows_owned, tensor_size * heads_dev, channels)
    result = attend(merged, cache_b[0], lengths_b[0])
    return result.reshape(rows_owned, tensor_size, heads_dev, LAT).transpose(1, 0, 2, 3)


def answer(result):
    answers = lax.all_to_all(result, ("k", "h"), split_axis=0, concat_axis=0, tiled=True)
    tensor_size, rows_owned, heads_dev, channels = answers.shape
    return answers.reshape(1, tensor_size * rows_owned, heads_dev, channels)


def swap(array, axis):
    return lax.ppermute(array, axis, [(0, 1), (1, 0)])


def shift(array, step):
    size = lax.axis_size("x")
    return lax.ppermute(array, "x", [(i, (i + step) % size) for i in range(size)])


def gate_up(gathered, w_gate, w_up):
    z_size, cores, x_size, rows, _ = gathered.shape
    width, hidden = w_gate.shape
    steps = 2
    partial = pl.pallas_call(
        gate_up_kernel,
        grid=(steps,),
        out_shape=jax.ShapeDtypeStruct((x_size, cores, z_size, rows, 2 * hidden), BF),
        in_specs=[
            pl.BlockSpec((z_size // steps, cores, x_size, rows, width), lambda i: (i, 0, 0, 0, 0)),
            pl.BlockSpec((width, hidden), lambda i: (0, 0)),
            pl.BlockSpec((width, hidden), lambda i: (0, 0)),
        ],
        out_specs=pl.BlockSpec(
            (x_size, cores, z_size // steps, rows, 2 * hidden), lambda i: (0, 0, i, 0, 0)
        ),
        compiler_params=WIDE,
        name="gate_up",
    )(gathered, w_gate, w_up)
    return partial.reshape(x_size, cores * z_size * rows, 2 * hidden)


def swiglu(parts):
    return pl.pallas_call(
        active_kernel,
        out_shape=jax.ShapeDtypeStruct((parts.shape[1], parts.shape[2] // 2), BF),
        in_specs=[VMEM],
        out_specs=VMEM,
        compiler_params=PARAMS,
        name="active_rows",
    )(parts)


def down(half, mine, other, gathered, place, weights, added):
    z_size, cores, x_size, rows, columns = gathered.shape
    count, hidden = mine.shape[0] // cores, mine.shape[1]
    lanes = 128
    last = columns // lanes - 1
    whole = pl.BlockSpec(memory_space=pltpu.VMEM)
    out_columns = weights[0].shape[2]
    return pl.pallas_call(
        down_kernel,
        out_shape=jax.ShapeDtypeStruct((x_size, count, out_columns), BF),
        grid_spec=pltpu.PrefetchScalarGridSpec(
            num_scalar_prefetch=1,
            grid=(1,),
            in_specs=[
                pl.BlockSpec((count, hidden), lambda i, p: (half, 0)),
                pl.BlockSpec((count, hidden), lambda i, p: (half, 0)),
                pl.BlockSpec((z_size, 1, 1, rows, lanes), lambda i, p: (0, p[0], p[1], 0, last)),
            ]
            + [whole] * (len(weights) + len(added)),
            out_specs=whole,
        ),
        compiler_params=PARAMS,
        name="down_rows",
    )(place, mine, other, gathered, *weights, *added)


def shards(
    tokens_a,
    norm_gain,
    expert_ids,
    route_weights,
    w_gate,
    w_up,
    w_down,
    queries_b,
    cache_b,
    lengths_b,
):
    x_size, z_size, cores = lax.axis_size("x"), lax.axis_size("z"), lax.axis_size("c")
    rows = tokens_a.shape[0]
    width = w_gate.shape[1]
    lanes = 128

    normed = pl.pallas_call(
        norm_kernel,
        grid=(1,),
        out_shape=jax.ShapeDtypeStruct((x_size, rows, width + lanes), BF),
        in_specs=[
            pl.BlockSpec(shape, lambda i: (0, 0))
            for shape in (tokens_a.shape, (1, norm_gain.shape[0])) + 2 * (expert_ids.shape[::-1],)
        ],
        out_specs=VMEM,
        compiler_params=WIDE,
        name="norm_rows",
    )(tokens_a, norm_gain.reshape(1, -1), expert_ids.T, route_weights.T)
    sliced = lax.all_to_all(normed, "x", split_axis=0, concat_axis=0, tiled=True)
    gathered = lax.all_gather(
        sliced.reshape(x_size * rows, width + lanes), ("z", "c"), axis=0, tiled=True
    ).reshape(z_size, cores, x_size, rows, width + lanes)

    normed, w_down = lax.optimization_barrier((normed, w_down))
    side = lax.axis_index("h")
    columns = w_down.shape[2] // 2
    left, right = w_down[0][:, :columns], w_down[0][:, columns:]
    mine = jnp.where(side == 0, left, right)
    theirs = swap(jnp.where(side == 0, right, left), "h")
    pair = jnp.stack([mine, theirs])
    lower, upper = shift(pair, 1), shift(pair, -1)
    across = (shift(lower[0], 1), shift(upper[1], -1))

    result = attention(queries_b, cache_b, lengths_b)
    latent_b = answer(result)
    gathered, latent_b, pair, lower, upper, across = lax.optimization_barrier(
        (gathered, latent_b, pair, lower, upper, across)
    )
    core, x_place = lax.axis_index("c"), lax.axis_index("x")
    partial = gate_up(gathered, w_gate[0], w_up[0])
    parts = lax.all_to_all(partial, "x", split_axis=0, concat_axis=0, tiled=True)
    weights = (pair, lower, upper, *across)
    active = swiglu(parts)
    active_other = swap(active, "h")
    added = ()
    for half in range(cores):
        place = jnp.stack([lax.rem(core + 1 + half, cores), x_place])
        out = down(half, active, active_other, gathered, place, weights, added)
        if not added:
            added = (swap(out, "c"),)
    both = out.reshape(-1, rows, columns)
    landed = lax.all_to_all(both, ("k", "z"), split_axis=0, concat_axis=0, tiled=True)
    mixed = jnp.sum(landed.astype(F32), axis=0).astype(BF)
    return (mixed, latent_b)


def solution(mesh):
    x_size, y_size, e_size = (mesh.shape[name] for name in ("dp", "tensor", "expert"))
    cores = 2
    fine = Mesh(
        mesh.devices.reshape(x_size, y_size // 2, 2, e_size // cores, cores),
        ("x", "k", "h", "z", "c"),
    )
    rows, tensor, expert = ("x", "z", "c"), ("k", "h"), ("z", "c")
    placed = (
        P(rows, None),
        P(),
        P(rows, None),
        P(rows, None),
        P(expert, "x", tensor),
        P(expert, "x", tensor),
        P(expert, tensor, "x"),
        P(rows, None, tensor, None),
        P(rows, tensor, None, None),
        P(rows, tensor),
    )
    return jax.shard_map(
        shards,
        mesh=fine,
        in_specs=placed,
        out_specs=(P(rows, tensor), P(rows, None, tensor, None)),
        check_vma=False,
    )
```

time: 225 us -> 168 us (0.75); the launches traced: 222 us -> 168 us
  waiting for transfers between devices: 129 us -> 49.5 us
  blocking collectives: 10.2 us -> 24.6 us
  starting transfers between devices: 48.9 us -> 53.8 us
  local copies, waits for them, and re-layouts: 3.57 us -> 7.74 us
  other arithmetic: 6.35 us -> 2.43 us
  Pallas kernels: 9.34 us -> 13.2 us
    all_gather x1, waiting for transfers between devices: 45.3 us -> 1.16 us  [shards(): lax.all_gather(sliced.reshape(x_size * rows, width + lanes), ('z', 'c'),...]
    ppermute x3 -> x4, waiting for transfers between devices: 25.7 us -> 7.21 us  [shift(): lax.ppermute(array, 'x', [(i, (i + step) % size) for i in range(size)])]
    all_to_all x5 -> x2, waiting for transfers between devices: 46.5 us -> 29.8 us  [the longest x1 28 us: shards(): lax.all_to_all(both, ('k', 'z'), split_axis=0, concat_axis=0, tiled=True)]
    all_to_all x0 -> x1, blocking collectives: none -> 14.2 us  [shards(): lax.all_to_all(partial, 'x', split_axis=0, concat_axis=0, tiled=True)]
    ppermute x3, starting transfers between devices: 9.65 us -> 16.7 us  [swap(): return lax.ppermute(array, axis, [(0, 1), (1, 0)])]
    ppermute x3, waiting for transfers between devices: 0.01 us -> 5.21 us  [swap(): return lax.ppermute(array, axis, [(0, 1), (1, 0)])]
    all_to_all x1, waiting for transfers between devices: 11.1 us -> 6.12 us  [attention(): lax.all_to_all(asked, ('k', 'h'), split_axis=0, concat_axis=0, tiled=True)]
    pallas_call x4 -> x5, Pallas kernels: 9.34 us -> 13.2 us  [the longest x2 6.02 us: down(): pl.pallas_call(down_kernel, out_shape=jax.ShapeDtypeStruct((x_size, count...]
  transfers between devices with their start and end apart: 13 -> 11, of which waited for: 9 -> 9; matrix products, arithmetic and copies ran while one was open for 3% -> 5% of each run, Pallas kernels for 2% -> 0%
where the time goes in v2:
time: 168 us
  starting transfers between devices  53.8 us (32%)
  waiting for transfers between devices  49.5 us (29%)
  blocking collectives  24.6 us (15%)
  between operations  14.2 us (8%)
  Pallas kernels  13.2 us (8%)
  local copies, waits for them, and re-layouts  7.74 us (5%)
  other arithmetic  2.43 us (1%)
  matrix products  2.06 us (1%)
    all_to_all x1, waiting for transfers between devices, shards(): lax.all_to_all(both, ('k', 'z'), split_axis=0, concat_axis=0, tiled=True)  28 us
    ppermute x3, starting transfers between devices, swap(): return lax.ppermute(array, axis, [(0, 1), (1, 0)])  16.7 us
    all_to_all x1, starting transfers between devices, shards(): lax.all_to_all(both, ('k', 'z'), split_axis=0, concat_axis=0, tiled=True)  15.8 us
    all_to_all x1, blocking collectives, shards(): lax.all_to_all(partial, 'x', split_axis=0, concat_axis=0, tiled=True)  14.2 us
    ppermute x4, starting transfers between devices, shift(): lax.ppermute(array, 'x', [(i, (i + step) % size) for i in range(size)])  11.2 us
    all_to_all x1, blocking collectives, shards(): lax.all_to_all(normed, 'x', split_axis=0, concat_axis=0, tiled=True)  10.4 us
    ppermute x4, waiting for transfers between devices, shift(): lax.ppermute(array, 'x', [(i, (i + step) % size) for i in range(size)])  7.21 us
    all_to_all x1, waiting for transfers between devices, attention(): lax.all_to_all(asked, ('k', 'h'), split_axis=0, concat_axis=0, tiled=True)  6.12 us
  transfers between devices with their start and end apart: 11, of which 9 were waited for; matrix products, arithmetic and copies ran while one was open for 5% of the time, Pallas kernels for 0%

profile of v2, /device:TPU:1, one launch (start us, length us, event | category | flops | bytes accessed | tf_op | source)
XLA Modules:
  0.0 167.5 jit_solution(15144720882737538427)
XLA Ops:
  7.2 0.0 copy-start.1
  7.2 0.0 all-gather.2.cloned.1.call-start
  7.2 1.9 %norm_rows.1 = bf16[4,16,1920]{2,1,0:T(8,128)(2,1)} custom-call(bf16[16,7168]{1,0:T(8,128)(2,1)} %tokens_ref.1, f32[1,7168]{1,0:T(1,128)} %bitcast.51, s32[8,16]{1,0:T(8,128)} %bitcast.52, f32[8,16]{1,0:T(8,128)} %bitcast.53), custom_call_target="tpu_custom_call" | custom-call | tf_op jit(solution)/shard_map/norm_rows/pallas_call | solution.py:209
  9.2 10.4 %all_to_all.25 = bf16[4,16,1920]{2,1,0:T(8,128)(2,1)} all-to-all(bf16[4,16,1920]{2,1,0:T(8,128)(2,1)} %norm_rows.1), channel_id=1, replica_groups=mesh['x'=4,'k'=4,'h'=2,'z'=8,'c'=2] {'x'}, dimensions={0} | all-to-all | bytes 491520 | tf_op jit(solution)/shard_map/all_to_all | solution.py:221
  19.6 0.0 all-gather.2.cloned.1.call-update
  19.6 1.2 select_bitcast_fusion
  20.9 3.2 %collective-permute-start = (bf16[256,896]{1,0:T(8,128)(2,1)S(1)}, bf16[256,896]{1,0:T(8,128)(2,1)S(1)}, u32[]{:S(2)}, u32[]{:S(2)}) collective-permute-start(bf16[256,896]{1,0:T(8,128)(2,1)S(1)} %get-tuple-element.19), channel_id=1, source_target_pairs={{0,16},{16,0},{1,17},{17,1},{2,18},{18,2},{3,19},{19,3},{4,20},{20... | collective-permute-start | bytes 1376264 | tf_op jit(solution)/shard_map/ppermute | solution.py:125
  24.1 5.9 %all-to-all-start.1 = ((bf16[8,2,16,576]{3,2,1,0:T(8,128)(2,1)}), bf16[8,2,16,576]{3,2,1,0:T(8,128)(2,1)}, u32[]{:S(2)}, u32[]{:S(2)}) async-start(bf16[8,2,16,576]{3,2,1,0:T(8,128)(2,1)} %bitcast.49), calls=%async_computation.1 | async-start | bytes 655360 | tf_op jit(solution)/shard_map/all_to_all | solution.py:112
  30.0 0.1 collective-permute-done
  30.1 0.1 pad_maximum_fusion.refs_0_
  30.2 2.8 %collective-permute-start.2 = (bf16[2,256,896]{2,1,0:T(8,128)(2,1)S(1)}, bf16[2,256,896]{2,1,0:T(8,128)(2,1)S(1)}, u32[]{:S(2)}, u32[]{:S(2)}) collective-permute-start(bf16[2,256,896]{2,1,0:T(8,128)(2,1)S(1)} %pad_maximum_fusion.refs_0_), channel_id=1, source_target_pairs={{0,384},{128,0},{256,128},{384,256},{1,385},{129,1},{257,129},{385... | collective-permute-start | bytes 2752520 | tf_op jit(solution)/shard_map/ppermute | solution.py:130
  33.0 2.5 %collective-permute-start.1 = (bf16[2,256,896]{2,1,0:T(8,128)(2,1)S(1)}, bf16[2,256,896]{2,1,0:T(8,128)(2,1)S(1)}, u32[]{:S(2)}, u32[]{:S(2)}) collective-permute-start(bf16[2,256,896]{2,1,0:T(8,128)(2,1)S(1)} %pad_maximum_fusion.refs_0_), channel_id=1, source_target_pairs={{0,128},{128,256},{256,384},{384,0},{1,129},{129,257},{257,385},{3... | collective-permute-start | bytes 2752520 | tf_op jit(solution)/shard_map/ppermute | solution.py:130
  35.5 1.1 copy.22
  36.6 6.1 %all-to-all-done.1 = bf16[8,2,16,576]{3,2,1,0:T(8,128)(2,1)} async-done(((bf16[8,2,16,576]{3,2,1,0:T(8,128)(2,1)}), bf16[8,2,16,576]{3,2,1,0:T(8,128)(2,1)}, u32[]{:S(2)}, u32[]{:S(2)}) %all-to-all-start.1) | async-done | bytes 294944 | tf_op jit(solution)/shard_map/all_to_all | solution.py:112
  42.7 1.0 copy.21
  43.7 0.3 fusion.3
  44.0 0.0 copy-start.3
  44.0 0.7 copy-done.3
  44.7 0.2 fusion.8
  44.9 1.8 %convolution_convert_fusion = bf16[2,128,512]{2,1,0:T(8,128)(2,1)S(1)} fusion(bf16[2,256,576]{2,1,0:T(8,128)(2,1)} %bitcast.47, f32[2,128]{1,0:T(2,128)S(1)} %fusion.8, f32[2,128,256]{2,1,0:T(8,128)} %copy-done.3), kind=kOutput, calls=%fused_computation.2 | convolution fusion | flops 67437056 | bytes 1311744 | tf_op jit(solution)/shard_map/rhl,rlc->rhc/dot_general | solution.py:103
  46.7 0.7 copy.31
  47.4 4.2 %all-to-all-start.2 = ((bf16[8,2,16,512]{3,2,1,0:T(8,128)(2,1)}), bf16[8,2,16,512]{3,2,1,0:T(8,128)(2,1)S(1)}, u32[]{:S(2)}, u32[]{:S(2)}) async-start(bf16[8,2,16,512]{3,2,1,0:T(8,128)(2,1)} %bitcast.35), calls=%async_computation.2 | async-start | bytes 524288 | tf_op jit(solution)/shard_map/all_to_all | solution.py:119
  51.6 0.0 collective-permute-done.2.refs_2_
  51.6 0.8 slice_bitcast_fusion
  52.4 4.0 %collective-permute-start.4 = (bf16[256,896]{1,0:T(8,128)(2,1)}, bf16[256,896]{1,0:T(8,128)(2,1)S(1)}, u32[]{:S(2)}, u32[]{:S(2)}) collective-permute-start(bf16[256,896]{1,0:T(8,128)(2,1)} %slice_bitcast_fusion), channel_id=1, source_target_pairs={{0,384},{128,0},{256,128},{384,256},{1,385},{129,1},{257,129},{385... | collective-permute-start | bytes 1376264 | tf_op jit(solution)/shard_map/ppermute | solution.py:130
  56.4 0.0 collective-permute-done.1.refs_1_
  56.4 0.8 slice_bitcast_fusion.1
  57.2 1.9 %collective-permute-start.3 = (bf16[256,896]{1,0:T(8,128)(2,1)}, bf16[256,896]{1,0:T(8,128)(2,1)}, u32[]{:S(2)}, u32[]{:S(2)}) collective-permute-start(bf16[256,896]{1,0:T(8,128)(2,1)} %slice_bitcast_fusion.1), channel_id=1, source_target_pairs={{0,128},{128,256},{256,384},{384,0},{1,129},{129,257},{257,385},{3... | collective-permute-start | bytes 1376264 | tf_op jit(solution)/shard_map/ppermute | solution.py:130
  59.1 1.8 %all-to-all-done.2 = bf16[8,2,16,512]{3,2,1,0:T(8,128)(2,1)S(1)} async-done(((bf16[8,2,16,512]{3,2,1,0:T(8,128)(2,1)}), bf16[8,2,16,512]{3,2,1,0:T(8,128)(2,1)S(1)}, u32[]{:S(2)}, u32[]{:S(2)}) %all-to-all-start.2) | async-done | bytes 262176 | tf_op jit(solution)/shard_map/all_to_all | solution.py:119
  60.9 2.3 %collective-permute-done.4.refs_4_ = bf16[256,896]{1,0:T(8,128)(2,1)S(1)} collective-permute-done((bf16[256,896]{1,0:T(8,128)(2,1)}, bf16[256,896]{1,0:T(8,128)(2,1)S(1)}, u32[]{:S(2)}, u32[]{:S(2)}) %collective-permute-start.4) | collective-permute-done | bytes 458784 | tf_op jit(solution)/shard_map/ppermute | solution.py:130
  63.2 4.9 %collective-permute-done.3.refs_3_ = bf16[256,896]{1,0:T(8,128)(2,1)} collective-permute-done((bf16[256,896]{1,0:T(8,128)(2,1)}, bf16[256,896]{1,0:T(8,128)(2,1)}, u32[]{:S(2)}, u32[]{:S(2)}) %collective-permute-start.3) | collective-permute-done | bytes 458784 | tf_op jit(solution)/shard_map/ppermute | solution.py:130
  68.1 1.2 all-gather.2.cloned.1.call-done
  69.3 5.1 %gate_up.1 = bf16[4,2,8,16,512]{4,3,2,1,0:T(8,128)(2,1)} custom-call(bf16[8,2,4,16,1920]{4,3,2,1,0:T(8,128)(2,1)} %bitcast.37, bf16[1792,256]{1,0:T(8,128)(2,1)} %bitcast.45, bf16[1792,256]{1,0:T(8,128)(2,1)} %bitcast.46), custom_call_target="tpu_custom_call" | custom-call | tf_op jit(solution)/shard_map/gate_up/pallas_call | solution.py:137
  74.4 14.2 %all_to_all.26.parts_ref = bf16[4,256,512]{2,1,0:T(8,128)(2,1)S(1)} all-to-all(bf16[4,256,512]{2,1,0:T(8,128)(2,1)} %bitcast.40), channel_id=1, replica_groups=mesh['x'=4,'k'=4,'h'=2,'z'=8,'c'=2] {'x'}, dimensions={0} | all-to-all | bytes 2097152 | tf_op jit(solution)/shard_map/all_to_all | solution.py:243
  88.6 0.2 active_rows.1.mine_ref
  88.8 3.1 %collective-permute-start.5 = (bf16[256,256]{1,0:T(8,128)(2,1)S(1)}, bf16[256,256]{1,0:T(8,128)(2,1)S(1)}, u32[]{:S(2)}, u32[]{:S(2)}) collective-permute-start(bf16[256,256]{1,0:T(8,128)(2,1)S(1)} %active_rows.1.mine_ref), channel_id=1, source_target_pairs={{0,16},{16,0},{1,17},{17,1},{2,18},{18,2},{3,19},{19,3},{4,20},{20... | collective-permute-start | bytes 393224 | tf_op jit(solution)/shard_map/ppermute | solution.py:125
  91.9 0.1 pad_add_fusion.1.place_ref
  91.9 2.8 %collective-permute-done.5.other_ref = bf16[256,256]{1,0:T(8,128)(2,1)S(1)} collective-permute-done((bf16[256,256]{1,0:T(8,128)(2,1)S(1)}, bf16[256,256]{1,0:T(8,128)(2,1)S(1)}, u32[]{:S(2)}, u32[]{:S(2)}) %collective-permute-start.5) | collective-permute-done | bytes 131104 | tf_op jit(solution)/shard_map/ppermute | solution.py:125
  94.8 3.3 %down_rows.2 = bf16[4,128,896]{2,1,0:T(8,128)(2,1)} custom-call(s32[2]{0:T(128)S(1)} %pad_add_fusion.1.place_ref, bf16[256,256]{1,0:T(8,128)(2,1)S(1)} %active_rows.1.mine_ref, bf16[256,256]{1,0:T(8,128)(2,1)S(1)} %collective-permute-done.5.other_ref, bf16[8,2,4,16,1920]{4,3,2,1,0:T(8,128)(2,1)} %bitcast.38, ...), custom_call_target="tpu_custom_call" | custom-call | tf_op jit(solution)/shard_map/down_rows/pallas_call | solution.py:173
  98.1 10.4 %collective-permute-start.6 = (bf16[4,128,896]{2,1,0:T(8,128)(2,1)}, bf16[4,128,896]{2,1,0:T(8,128)(2,1)}, u32[]{:S(2)}, u32[]{:S(2)}) collective-permute-start(bf16[4,128,896]{2,1,0:T(8,128)(2,1)} %down_rows.2), channel_id=1, source_target_pairs={{0,1},{1,0},{2,3},{3,2},{4,5},{5,4},{6,7},{7,6},{8,9},{9,8},{10,11... | collective-permute-start | bytes 2752520 | tf_op jit(solution)/shard_map/ppermute | solution.py:125
  108.5 0.1 pad_add_fusion.place_ref
  108.5 2.3 %collective-permute-done.6.refs_5_ = bf16[4,128,896]{2,1,0:T(8,128)(2,1)} collective-permute-done((bf16[4,128,896]{2,1,0:T(8,128)(2,1)}, bf16[4,128,896]{2,1,0:T(8,128)(2,1)}, u32[]{:S(2)}, u32[]{:S(2)}) %collective-permute-start.6) | collective-permute-done | bytes 917536 | tf_op jit(solution)/shard_map/ppermute | solution.py:125
  110.9 2.7 %down_rows.3 = bf16[4,128,896]{2,1,0:T(8,128)(2,1)S(1)} custom-call(s32[2]{0:T(128)S(1)} %pad_add_fusion.place_ref, bf16[256,256]{1,0:T(8,128)(2,1)S(1)} %active_rows.1.mine_ref, bf16[256,256]{1,0:T(8,128)(2,1)S(1)} %collective-permute-done.5.other_ref, bf16[8,2,4,16,1920]{4,3,2,1,0:T(8,128)(2,1)} %bitcast.39, ...), custom_call_target="tpu_custom_call" | custom-call | tf_op jit(solution)/shard_map/down_rows/pallas_call | solution.py:173
  113.6 0.9 copy-done
  114.5 15.8 %all-to-all-start.4 = ((bf16[32,16,896]{2,1,0:T(8,128)(2,1)}), bf16[32,16,896]{2,1,0:T(8,128)(2,1)S(1)}, u32[]{:S(2)}, u32[]{:S(2)}) async-start(bf16[32,16,896]{2,1,0:T(8,128)(2,1)} %bitcast.36), calls=%async_computation.4 | async-start | bytes 1835008 | tf_op jit(solution)/shard_map/all_to_all | solution.py:254
  130.3 28.0 %all-to-all-done.4 = bf16[32,16,896]{2,1,0:T(8,128)(2,1)S(1)} async-done(((bf16[32,16,896]{2,1,0:T(8,128)(2,1)}), bf16[32,16,896]{2,1,0:T(8,128)(2,1)S(1)}, u32[]{:S(2)}, u32[]{:S(2)}) %all-to-all-start.4) | async-done | bytes 917536 | tf_op jit(solution)/shard_map/all_to_all | solution.py:254
  158.3 0.7 reduce_sum.22
  159.0 1.7 copy.33
  (6 shorter events, 0.0 us)
Async XLA Ops:
  7.2 28.3 %copy-start.1 = (bf16[1,2,256,576]{2,3,1,0:T(8,128)(2,1)S(1)}, bf16[1,2,256,576]{2,3,1,0:T(8,128)(2,1)}, u32[]{:S(2)}) copy-start(bf16[1,2,256,576]{2,3,1,0:T(8,128)(2,1)} %param.18) | copy-start | bytes 1769476
  7.2 36.5 %copy-start.4 = (s32[1,2]{1,0:T(1,128)S(1)}, s32[1,2]{1,0:T(1,128)}, u32[]{:S(2)}) copy-start(s32[1,2]{1,0:T(1,128)} %param.19) | copy-start | bytes 28
  7.2 62.1 %all-gather.2.cloned.1.call-start = ((), (), s32[]{:S(2)}) async-start(), calls=%async_computation.5 | async-start | bytes 4177920 | tf_op jit(solution)/shard_map/all_gather | solution.py:222
  20.9 9.2 %collective-permute-start = (bf16[256,896]{1,0:T(8,128)(2,1)S(1)}, bf16[256,896]{1,0:T(8,128)(2,1)S(1)}, u32[]{:S(2)}, u32[]{:S(2)}) collective-permute-start(bf16[256,896]{1,0:T(8,128)(2,1)S(1)} %get-tuple-element.19), channel_id=1, source_target_pairs={{0,16},{16,0},{1,17},{17,1},{2,18},{18,2},{3,19},{19,3},{4,20},{20... | collective-permute-start | bytes 1376264 | tf_op jit(solution)/shard_map/ppermute | solution.py:125
  24.1 18.6 %all-to-all-start.1 = ((bf16[8,2,16,576]{3,2,1,0:T(8,128)(2,1)}), bf16[8,2,16,576]{3,2,1,0:T(8,128)(2,1)}, u32[]{:S(2)}, u32[]{:S(2)}) async-start(bf16[8,2,16,576]{3,2,1,0:T(8,128)(2,1)} %bitcast.49), calls=%async_computation.1 | async-start | bytes 655360 | tf_op jit(solution)/shard_map/all_to_all | solution.py:112
  30.2 21.4 %collective-permute-start.2 = (bf16[2,256,896]{2,1,0:T(8,128)(2,1)S(1)}, bf16[2,256,896]{2,1,0:T(8,128)(2,1)S(1)}, u32[]{:S(2)}, u32[]{:S(2)}) collective-permute-start(bf16[2,256,896]{2,1,0:T(8,128)(2,1)S(1)} %pad_maximum_fusion.refs_0_), channel_id=1, source_target_pairs={{0,384},{128,0},{256,128},{384,256},{1,385},{129,1},{257,129},{385... | collective-permute-start | bytes 2752520 | tf_op jit(solution)/shard_map/ppermute | solution.py:130
  33.0 23.4 %collective-permute-start.1 = (bf16[2,256,896]{2,1,0:T(8,128)(2,1)S(1)}, bf16[2,256,896]{2,1,0:T(8,128)(2,1)S(1)}, u32[]{:S(2)}, u32[]{:S(2)}) collective-permute-start(bf16[2,256,896]{2,1,0:T(8,128)(2,1)S(1)} %pad_maximum_fusion.refs_0_), channel_id=1, source_target_pairs={{0,128},{128,256},{256,384},{384,0},{1,129},{129,257},{257,385},{3... | collective-permute-start | bytes 2752520 | tf_op jit(solution)/shard_map/ppermute | solution.py:130
  44.0 0.7 copy-start.3
  47.4 13.5 %all-to-all-start.2 = ((bf16[8,2,16,512]{3,2,1,0:T(8,128)(2,1)}), bf16[8,2,16,512]{3,2,1,0:T(8,128)(2,1)S(1)}, u32[]{:S(2)}, u32[]{:S(2)}) async-start(bf16[8,2,16,512]{3,2,1,0:T(8,128)(2,1)} %bitcast.35), calls=%async_computation.2 | async-start | bytes 524288 | tf_op jit(solution)/shard_map/all_to_all | solution.py:119
  52.4 10.9 %collective-permute-start.4 = (bf16[256,896]{1,0:T(8,128)(2,1)}, bf16[256,896]{1,0:T(8,128)(2,1)S(1)}, u32[]{:S(2)}, u32[]{:S(2)}) collective-permute-start(bf16[256,896]{1,0:T(8,128)(2,1)} %slice_bitcast_fusion), channel_id=1, source_target_pairs={{0,384},{128,0},{256,128},{384,256},{1,385},{129,1},{257,129},{385... | collective-permute-start | bytes 1376264 | tf_op jit(solution)/shard_map/ppermute | solution.py:130
  57.2 10.9 %collective-permute-start.3 = (bf16[256,896]{1,0:T(8,128)(2,1)}, bf16[256,896]{1,0:T(8,128)(2,1)}, u32[]{:S(2)}, u32[]{:S(2)}) collective-permute-start(bf16[256,896]{1,0:T(8,128)(2,1)} %slice_bitcast_fusion.1), channel_id=1, source_target_pairs={{0,128},{128,256},{256,384},{384,0},{1,129},{129,257},{257,385},{3... | collective-permute-start | bytes 1376264 | tf_op jit(solution)/shard_map/ppermute | solution.py:130
  60.9 13.5 %copy-start.2 = (bf16[8,2,16,512]{3,2,1,0:T(8,128)(2,1)}, bf16[8,2,16,512]{3,2,1,0:T(8,128)(2,1)S(1)}, u32[]{:S(2)}) copy-start(bf16[8,2,16,512]{3,2,1,0:T(8,128)(2,1)S(1)} %all-to-all-done.2) | copy-start | bytes 786436
  88.8 6.0 %collective-permute-start.5 = (bf16[256,256]{1,0:T(8,128)(2,1)S(1)}, bf16[256,256]{1,0:T(8,128)(2,1)S(1)}, u32[]{:S(2)}, u32[]{:S(2)}) collective-permute-start(bf16[256,256]{1,0:T(8,128)(2,1)S(1)} %active_rows.1.mine_ref), channel_id=1, source_target_pairs={{0,16},{16,0},{1,17},{17,1},{2,18},{18,2},{3,19},{19,3},{4,20},{20... | collective-permute-start | bytes 393224 | tf_op jit(solution)/shard_map/ppermute | solution.py:125
  98.1 12.8 %collective-permute-start.6 = (bf16[4,128,896]{2,1,0:T(8,128)(2,1)}, bf16[4,128,896]{2,1,0:T(8,128)(2,1)}, u32[]{:S(2)}, u32[]{:S(2)}) collective-permute-start(bf16[4,128,896]{2,1,0:T(8,128)(2,1)} %down_rows.2), channel_id=1, source_target_pairs={{0,1},{1,0},{2,3},{3,2},{4,5},{5,4},{6,7},{7,6},{8,9},{9,8},{10,11... | collective-permute-start | bytes 2752520 | tf_op jit(solution)/shard_map/ppermute | solution.py:125
  113.6 0.9 copy-start
  114.5 43.7 %all-to-all-start.4 = ((bf16[32,16,896]{2,1,0:T(8,128)(2,1)}), bf16[32,16,896]{2,1,0:T(8,128)(2,1)S(1)}, u32[]{:S(2)}, u32[]{:S(2)}) async-start(bf16[32,16,896]{2,1,0:T(8,128)(2,1)} %bitcast.36), calls=%async_computation.4 | async-start | bytes 1835008 | tf_op jit(solution)/shard_map/all_to_all | solution.py:254
Sparse Core Ops, SparseCore 0:
  19.7 49.5 all-gather.1

commit v3 on v2

--- a/solution.py
+++ b/solution.py
@@ -16,7 +16,20 @@
 WIDE = pltpu.CompilerParams(vmem_limit_bytes=60 * 1024 * 1024)
 
 
-def norm_kernel(tokens_ref, gain_ref, ids_ref, route_ref, out_ref):
+def norm_kernel(tokens_ref, gain_ref, ids_ref, route_ref, down_ref, out_ref, mine_ref, send_ref):
+    count = mine_ref.shape[1]
+    side = lax.axis_index("h")
+    for half in (0, 1):
+        part = down_ref[:, half * count : (half + 1) * count]
+
+        @pl.when(side == half)
+        def _():
+            mine_ref[...] = part
+
+        @pl.when(side != half)
+        def _():
+            send_ref[...] = part
+
     values = tokens_ref[...].astype(F32)
     row_scale = lax.rsqrt(jnp.mean(values * values, axis=-1, keepdims=True) + 1e-06)
     normed = (values * row_scale * gain_ref[...]).astype(BF)
@@ -43,7 +56,6 @@
         out_ref[part, :, :width] = normed[:, part * width : (part + 1) * width]
         out_ref[part, :, width:columns] = extra
 
-
 def gate_up_kernel(rows_ref, gate_ref, up_ref, out_ref):
     z_count, cores, x_count, rows, width = rows_ref.shape
     me = lax.axis_index("c")
@@ -68,10 +80,7 @@
 
 
 def down_kernel(place_ref, mine_ref, other_ref, route_ref, *refs):
-    (pair_ref, lower_ref, upper_ref), across = refs[:3], refs[3:5]
-    added, out_ref = refs[5:-1], refs[-1]
-    weights = [ref.at[half] for ref in (pair_ref, lower_ref, upper_ref) for half in (0, 1)]
-    weights += across
+    weights, added, out_ref = refs[:8], refs[8:-1], refs[-1]
     x_count = out_ref.shape[0]
     me = lax.axis_index("x")
     rows = mine_ref.shape[0]
@@ -91,17 +100,21 @@
         out_ref[place] = total.astype(BF)
 
 
-def attend(queries, cache, lengths):
-    scores = (
-        jnp.einsum("rhc,rlc->rhl", queries, cache, preferred_element_type=F32) * score_scale
-    )
-    live_mask = lax.broadcasted_iota(jnp.int32, scores.shape, 2) < lengths[:, None, None]
-    scores = jnp.where(live_mask, scores, -1e30)
-    row_max = jnp.max(scores, axis=2, keepdims=True)
-    exp_terms = jnp.exp(scores - row_max)
-    softmax_bf = (exp_terms / jnp.sum(exp_terms, axis=2, keepdims=True)).astype(BF)
-    latent = jnp.einsum("rhl,rlc->rhc", softmax_bf, cache[:, :, :LAT], preferred_element_type=F32)
-    return latent.astype(BF)
+def attend_kernel(lengths_ref, queries_ref, cache_ref, out_ref):
+    pieces, rows, heads, channels = queries_ref.shape
+    latents = out_ref.shape[3]
+    for row in range(rows):
+        queries = queries_ref[:, row].reshape(pieces * heads, channels)
+        cache = cache_ref[row]
+        scores = jnp.dot(queries, cache, preferred_element_type=F32) * score_scale
+        live = lax.broadcasted_iota(jnp.int32, scores.shape, 1) < lengths_ref[0, row]
+        scores = jnp.where(live, scores, -1e30)
+        exp_terms = jnp.exp(scores - jnp.max(scores, axis=1, keepdims=True))
+        probs = (exp_terms / jnp.sum(exp_terms, axis=1, keepdims=True)).astype(BF)
+        latent = lax.dot_general(
+            probs, cache[:latents], (((1,), (1,)), ((), ())), preferred_element_type=F32
+        )
+        out_ref[:, row] = latent.astype(BF).reshape(pieces, heads, latents)
 
 
 def attention(queries_b, cache_b, lengths_b):
@@ -110,9 +123,14 @@
     rows_owned = cache_b.shape[1]
     asked = queries_b[0].reshape(tensor_size, rows_owned, heads_dev, channels)
     pieces = lax.all_to_all(asked, ("k", "h"), split_axis=0, concat_axis=0, tiled=True)
-    merged = pieces.transpose(1, 0, 2, 3).reshape(rows_owned, tensor_size * heads_dev, channels)
-    result = attend(merged, cache_b[0], lengths_b[0])
-    return result.reshape(rows_owned, tensor_size, heads_dev, LAT).transpose(1, 0, 2, 3)
+    return pl.pallas_call(
+        attend_kernel,
+        out_shape=jax.ShapeDtypeStruct((*pieces.shape[:3], LAT), BF),
+        in_specs=[pl.BlockSpec(memory_space=pltpu.SMEM), VMEM, VMEM],
+        out_specs=VMEM,
+        compiler_params=WIDE,
+        name="attend",
+    )(lengths_b, pieces, cache_b[0].transpose(0, 2, 1))
 
 
 def answer(result):
@@ -169,7 +187,7 @@
     lanes = 128
     last = columns // lanes - 1
     whole = pl.BlockSpec(memory_space=pltpu.VMEM)
-    out_columns = weights[0].shape[2]
+    out_columns = weights[0].shape[1]
     return pl.pallas_call(
         down_kernel,
         out_shape=jax.ShapeDtypeStruct((x_size, count, out_columns), BF),
@@ -189,6 +207,32 @@
     )(place, mine, other, gathered, *weights, *added)
 
 
+def last_kernel(landed_ref, latent_ref, mixed_ref, latent_out_ref, sem):
+    copy = pltpu.make_async_copy(latent_ref, latent_out_ref, sem)
+    copy.start()
+    total = landed_ref[0].astype(F32)
+    for number in range(1, landed_ref.shape[0]):
+        total = total + landed_ref[number].astype(F32)
+    mixed_ref[...] = total.astype(BF)
+    copy.wait()
+
+
+def last(landed, latent):
+    anywhere = pl.BlockSpec(memory_space=pl.ANY)
+    return pl.pallas_call(
+        last_kernel,
+        out_shape=(
+            jax.ShapeDtypeStruct(landed.shape[1:], BF),
+            jax.ShapeDtypeStruct(latent.shape, BF),
+        ),
+        in_specs=[VMEM, anywhere],
+        out_specs=(VMEM, anywhere),
+        scratch_shapes=[pltpu.SemaphoreType.DMA],
+        compiler_params=PARAMS,
+        name="last_sum",
+    )(landed, latent)
+
+
 def shards(
     tokens_a,
     norm_gain,
@@ -206,42 +250,42 @@
     width = w_gate.shape[1]
     lanes = 128
 
-    normed = pl.pallas_call(
+    columns = w_down.shape[2] // 2
+    half_shape = jax.ShapeDtypeStruct((w_down.shape[1], columns), BF)
+    normed, mine, send = pl.pallas_call(
         norm_kernel,
         grid=(1,),
-        out_shape=jax.ShapeDtypeStruct((x_size, rows, width + lanes), BF),
+        out_shape=(
+            jax.ShapeDtypeStruct((x_size, rows, width + lanes), BF), half_shape, half_shape
+        ),
         in_specs=[
             pl.BlockSpec(shape, lambda i: (0, 0))
             for shape in (tokens_a.shape, (1, norm_gain.shape[0])) + 2 * (expert_ids.shape[::-1],)
+            + (w_down.shape[1:],)
         ],
-        out_specs=VMEM,
+        out_specs=(VMEM, VMEM, VMEM),
         compiler_params=WIDE,
         name="norm_rows",
-    )(tokens_a, norm_gain.reshape(1, -1), expert_ids.T, route_weights.T)
+    )(tokens_a, norm_gain.reshape(1, -1), expert_ids.T, route_weights.T, w_down[0])
     sliced = lax.all_to_all(normed, "x", split_axis=0, concat_axis=0, tiled=True)
     gathered = lax.all_gather(
         sliced.reshape(x_size * rows, width + lanes), ("z", "c"), axis=0, tiled=True
     ).reshape(z_size, cores, x_size, rows, width + lanes)
 
-    normed, w_down = lax.optimization_barrier((normed, w_down))
-    side = lax.axis_index("h")
-    columns = w_down.shape[2] // 2
-    left, right = w_down[0][:, :columns], w_down[0][:, columns:]
-    mine = jnp.where(side == 0, left, right)
-    theirs = swap(jnp.where(side == 0, right, left), "h")
-    pair = jnp.stack([mine, theirs])
-    lower, upper = shift(pair, 1), shift(pair, -1)
-    across = (shift(lower[0], 1), shift(upper[1], -1))
+    theirs = swap(send, "h")
+    mine_lower, mine_upper = shift(mine, 1), shift(mine, -1)
+    theirs_lower, theirs_upper = shift(theirs, 1), shift(theirs, -1)
+    across = (shift(mine_lower, 1), shift(theirs_upper, -1))
+    weights = (mine, theirs, mine_lower, theirs_lower, mine_upper, theirs_upper, *across)
 
     result = attention(queries_b, cache_b, lengths_b)
     latent_b = answer(result)
-    gathered, latent_b, pair, lower, upper, across = lax.optimization_barrier(
-        (gathered, latent_b, pair, lower, upper, across)
-    )
+    gathered, latent_b, near = lax.optimization_barrier((gathered, latent_b, weights[:6]))
     core, x_place = lax.axis_index("c"), lax.axis_index("x")
     partial = gate_up(gathered, w_gate[0], w_up[0])
+    partial, across = lax.optimization_barrier((partial, across))
+    weights = (*near, *across)
     parts = lax.all_to_all(partial, "x", split_axis=0, concat_axis=0, tiled=True)
-    weights = (pair, lower, upper, *across)
     active = swiglu(parts)
     active_other = swap(active, "h")
     added = ()
@@ -252,8 +296,7 @@
             added = (swap(out, "c"),)
     both = out.reshape(-1, rows, columns)
     landed = lax.all_to_all(both, ("k", "z"), split_axis=0, concat_axis=0, tiled=True)
-    mixed = jnp.sum(landed.astype(F32), axis=0).astype(BF)
-    return (mixed, latent_b)
+    return last(landed, latent_b)
 
 
 def solution(mesh):

time: 168 us -> 159 us (0.946)
  blocking collectives: 24.6 us -> 65.9 us
  waiting for transfers between devices: 49.5 us -> 17.6 us
  starting transfers between devices: 53.8 us -> 40.9 us
  local copies, waits for them, and re-layouts: 7.74 us -> 1.44 us
  Pallas kernels: 13.2 us -> 17.8 us
  other arithmetic: 2.43 us -> 0.15 us
  matrix products: 2.06 us -> 0 us
    all_to_all x0 -> x1, blocking collectives: none -> 36.9 us  [shards(): lax.all_to_all(both, ('k', 'z'), split_axis=0, concat_axis=0, tiled=True)]
    all_to_all x1 -> x0, waiting for transfers between devices: 28 us -> none  [shards(): lax.all_to_all(both, ('k', 'z'), split_axis=0, concat_axis=0, tiled=True)]
    all_to_all x1 -> x0, starting transfers between devices: 15.8 us -> none  [shards(): lax.all_to_all(both, ('k', 'z'), split_axis=0, concat_axis=0, tiled=True)]
    all_gather x1, waiting for transfers between devices: 1.16 us -> 9 us  [shards(): lax.all_gather(sliced.reshape(x_size * rows, width + lanes), ('z', 'c'),...]
    ppermute x4 -> x6, waiting for transfers between devices: 7.21 us -> 0.02 us  [shift(): lax.ppermute(array, 'x', [(i, (i + step) % size) for i in range(size)])]
    ppermute x4 -> x6, starting transfers between devices: 11.2 us -> 18.3 us  [shift(): lax.ppermute(array, 'x', [(i, (i + step) % size) for i in range(size)])]
    ppermute x3, starting transfers between devices: 16.7 us -> 10.8 us  [swap(): return lax.ppermute(array, axis, [(0, 1), (1, 0)])]
    all_to_all x1, waiting for transfers between devices: 6.12 us -> 0.97 us  [attention(): lax.all_to_all(asked, ('k', 'h'), split_axis=0, concat_axis=0, tiled=True)]
  transfers between devices with their start and end apart: 11 -> 12, of which waited for: 9 -> 5; matrix products, arithmetic and copies ran while one was open for 5% -> 0% of each run, Pallas kernels for 0% -> 5%
where the time goes in v3:
time: 159 us; the launch traced here: 158 us
  blocking collectives  65.9 us (41%)
  starting transfers between devices  40.9 us (26%)
  Pallas kernels  17.8 us (11%)
  waiting for transfers between devices  17.6 us (11%)
  between operations  14.2 us (9%)
    all_to_all x1, blocking collectives, shards(): lax.all_to_all(both, ('k', 'z'), split_axis=0, concat_axis=0, tiled=True)  36.9 us
    all_to_all x1, blocking collectives, shards(): lax.all_to_all(partial, 'x', split_axis=0, concat_axis=0, tiled=True)  18.6 us
    ppermute x6, starting transfers between devices, shift(): lax.ppermute(array, 'x', [(i, (i + step) % size) for i in range(size)])  18.3 us
    ppermute x3, starting transfers between devices, swap(): return lax.ppermute(array, axis, [(0, 1), (1, 0)])  10.8 us
    all_to_all x1, blocking collectives, shards(): lax.all_to_all(normed, 'x', split_axis=0, concat_axis=0, tiled=True)  10.4 us
    all_gather x1, waiting for transfers between devices, shards(): lax.all_gather(sliced.reshape(x_size * rows, width + lanes), ('z', 'c'),...  9 us
    pallas_call x2, Pallas kernels, down(): pl.pallas_call(down_kernel, out_shape=jax.ShapeDtypeStruct((x_size, count...  6.03 us
    all_to_all x1, starting transfers between devices, attention(): lax.all_to_all(asked, ('k', 'h'), split_axis=0, concat_axis=0, tiled=True)  5.93 us
  transfers between devices with their start and end apart: 12, of which 5 were waited for; matrix products, arithmetic and copies ran while one was open for 0% of the time, Pallas kernels for 5%

profile of v3, /device:TPU:1, one launch (start us, length us, event | category | flops | bytes accessed | tf_op | source)
XLA Modules:
  0.0 157.9 jit_solution(9394876514726968445)
XLA Ops:
  7.2 0.0 all-gather.2.cloned.1.call-start
  7.2 2.5 %norm_rows.1 = (bf16[4,16,1920]{2,1,0:T(8,128)(2,1)}, bf16[256,896]{1,0:T(8,128)(2,1)}, bf16[256,896]{1,0:T(8,128)(2,1)}) custom-call(bf16[16,7168]{1,0:T(8,128)(2,1)} %tokens_ref.1, f32[1,7168]{1,0:T(1,128)} %bitcast.30, s32[8,16]{1,0:T(8,128)} %bitcast.31, f32[8,16]{1,0:T(8,128)} %bitcast.32, bf16[256,1792]{1,0:T(8,128)(2,1)} %bitcast.25), custom_call_target="tpu_custom_call" | custom-call | tf_op jit(solution)/shard_map/norm_rows/pallas_call | solution.py:255
  9.7 10.4 %all_to_all.25 = bf16[4,16,1920]{2,1,0:T(8,128)(2,1)} all-to-all(bf16[4,16,1920]{2,1,0:T(8,128)(2,1)} %get-tuple-element.16), channel_id=1, replica_groups=mesh['x'=4,'k'=4,'h'=2,'z'=8,'c'=2] {'x'}, dimensions={0} | all-to-all | bytes 491520 | tf_op jit(solution)/shard_map/all_to_all | solution.py:270
  20.1 0.0 all-gather.2.cloned.1.call-update
  20.1 3.2 %collective-permute-start = (bf16[256,896]{1,0:T(8,128)(2,1)}, bf16[256,896]{1,0:T(8,128)(2,1)S(1)}, u32[]{:S(2)}, u32[]{:S(2)}) collective-permute-start(bf16[256,896]{1,0:T(8,128)(2,1)} %get-tuple-element.18), channel_id=1, source_target_pairs={{0,16},{16,0},{1,17},{17,1},{2,18},{18,2},{3,19},{19,3},{4,20},{20... | collective-permute-start | bytes 1376264 | tf_op jit(solution)/shard_map/ppermute | solution.py:143
  23.3 5.9 %all-to-all-start.1 = ((bf16[8,2,16,576]{3,2,1,0:T(8,128)(2,1)}), bf16[8,2,16,576]{3,2,1,0:T(8,128)(2,1)S(1)}, u32[]{:S(2)}, u32[]{:S(2)}) async-start(bf16[8,2,16,576]{3,2,1,0:T(8,128)(2,1)} %bitcast.29), calls=%async_computation.1 | async-start | bytes 655360 | tf_op jit(solution)/shard_map/all_to_all | solution.py:125
  29.3 2.3 %collective-permute-start.1 = (bf16[256,896]{1,0:T(8,128)(2,1)}, bf16[256,896]{1,0:T(8,128)(2,1)S(1)}, u32[]{:S(2)}, u32[]{:S(2)}) collective-permute-start(bf16[256,896]{1,0:T(8,128)(2,1)} %get-tuple-element.21.refs_0_), channel_id=1, source_target_pairs={{0,128},{128,256},{256,384},{384,0},{1,129},{129,257},{257,385},{3... | collective-permute-start | bytes 1376264 | tf_op jit(solution)/shard_map/ppermute | solution.py:148
  31.5 0.0 collective-permute-done.refs_1_
  31.6 4.2 %collective-permute-start.4 = (bf16[256,896]{1,0:T(8,128)(2,1)S(1)}, bf16[256,896]{1,0:T(8,128)(2,1)S(1)}, u32[]{:S(2)}, u32[]{:S(2)}) collective-permute-start(bf16[256,896]{1,0:T(8,128)(2,1)S(1)} %collective-permute-done.refs_1_), channel_id=1, source_target_pairs={{0,384},{128,0},{256,128},{384,256},{1,385},{129,1},{257,129},{385... | collective-permute-start | bytes 1376264 | tf_op jit(solution)/shard_map/ppermute | solution.py:148
  35.8 1.9 %collective-permute-start.3 = (bf16[256,896]{1,0:T(8,128)(2,1)}, bf16[256,896]{1,0:T(8,128)(2,1)S(1)}, u32[]{:S(2)}, u32[]{:S(2)}) collective-permute-start(bf16[256,896]{1,0:T(8,128)(2,1)} %get-tuple-element.21.refs_0_), channel_id=1, source_target_pairs={{0,384},{128,0},{256,128},{384,256},{1,385},{129,1},{257,129},{385... | collective-permute-start | bytes 1376264 | tf_op jit(solution)/shard_map/ppermute | solution.py:148
  37.7 3.4 %collective-permute-start.2 = (bf16[256,896]{1,0:T(8,128)(2,1)S(1)}, bf16[256,896]{1,0:T(8,128)(2,1)S(1)}, u32[]{:S(2)}, u32[]{:S(2)}) collective-permute-start(bf16[256,896]{1,0:T(8,128)(2,1)S(1)} %collective-permute-done.refs_1_), channel_id=1, source_target_pairs={{0,128},{128,256},{256,384},{384,0},{1,129},{129,257},{257,385},{3... | collective-permute-start | bytes 1376264 | tf_op jit(solution)/shard_map/ppermute | solution.py:148
  41.1 1.0 all-to-all-done.1.queries_ref
  42.0 0.0 copy-start.3
  42.0 0.7 copy-done.3
  42.8 2.6 %attend.1 = bf16[8,2,16,512]{3,2,1,0:T(8,128)(2,1)} custom-call(s32[1,2]{1,0:T(1,128)} %lengths_ref.1, bf16[8,2,16,576]{3,2,1,0:T(8,128)(2,1)} %copy-done.3, bf16[2,576,256]{2,1,0:T(8,128)(2,1)} %bitcast.28), custom_call_target="tpu_custom_call" | custom-call | tf_op jit(solution)/shard_map/attend/pallas_call | solution.py:126
  45.4 5.9 %all-to-all-start.2 = ((bf16[8,2,16,512]{3,2,1,0:T(8,128)(2,1)}), bf16[8,2,16,512]{3,2,1,0:T(8,128)(2,1)S(1)}, u32[]{:S(2)}, u32[]{:S(2)}) async-start(bf16[8,2,16,512]{3,2,1,0:T(8,128)(2,1)} %attend.1), calls=%async_computation.2 | async-start | bytes 524288 | tf_op jit(solution)/shard_map/all_to_all | solution.py:137
  51.2 0.0 collective-permute-done.1.refs_2_
  51.2 2.5 %collective-permute-start.5 = (bf16[256,896]{1,0:T(8,128)(2,1)S(1)}, bf16[256,896]{1,0:T(8,128)(2,1)S(1)}, u32[]{:S(2)}, u32[]{:S(2)}) collective-permute-start(bf16[256,896]{1,0:T(8,128)(2,1)S(1)} %collective-permute-done.1.refs_2_), channel_id=1, source_target_pairs={{0,128},{128,256},{256,384},{384,0},{1,129},{129,257},{257,385},{3... | collective-permute-start | bytes 1376264 | tf_op jit(solution)/shard_map/ppermute | solution.py:148
  53.8 0.0 collective-permute-done.4.refs_5_
  53.8 4.0 %collective-permute-start.6 = (bf16[256,896]{1,0:T(8,128)(2,1)S(1)}, bf16[256,896]{1,0:T(8,128)(2,1)}, u32[]{:S(2)}, u32[]{:S(2)}) collective-permute-start(bf16[256,896]{1,0:T(8,128)(2,1)S(1)} %collective-permute-done.4.refs_5_), channel_id=1, source_target_pairs={{0,384},{128,0},{256,128},{384,256},{1,385},{129,1},{257,129},{385... | collective-permute-start | bytes 1376264 | tf_op jit(solution)/shard_map/ppermute | solution.py:148
  57.8 0.0 collective-permute-done.3.refs_4_
  57.8 0.0 collective-permute-done.2.refs_3_
  57.8 2.8 %all-to-all-done.2 = bf16[8,2,16,512]{3,2,1,0:T(8,128)(2,1)S(1)} async-done(((bf16[8,2,16,512]{3,2,1,0:T(8,128)(2,1)}), bf16[8,2,16,512]{3,2,1,0:T(8,128)(2,1)S(1)}, u32[]{:S(2)}, u32[]{:S(2)}) %all-to-all-start.2) | async-done | bytes 262176 | tf_op jit(solution)/shard_map/all_to_all | solution.py:137
  60.6 0.0 copy-start.1
  60.6 0.7 copy-done.1
  61.3 9.0 %all-gather.2.cloned.1.call-done = bf16[1024,1920]{1,0:T(8,128)(2,1)} async-done(((bf16[64,1920]{1,0:T(8,128)(2,1)}), bf16[1024,1920]{1,0:T(8,128)(2,1)}) %all-gather.2.cloned.1.call-update) | async-done | bytes 3932176 | tf_op jit(solution)/shard_map/all_gather | solution.py:271
  70.3 0.0 copy-start
  70.3 5.2 %gate_up.1 = bf16[4,2,8,16,512]{4,3,2,1,0:T(8,128)(2,1)} custom-call(bf16[8,2,4,16,1920]{4,3,2,1,0:T(8,128)(2,1)} %bitcast.20, bf16[1792,256]{1,0:T(8,128)(2,1)} %bitcast.26, bf16[1792,256]{1,0:T(8,128)(2,1)} %bitcast.27), custom_call_target="tpu_custom_call" | custom-call | tf_op jit(solution)/shard_map/gate_up/pallas_call | solution.py:155
  75.4 0.0 collective-permute-done.5.refs_6_
  75.4 0.0 collective-permute-done.6.refs_7_
  75.4 18.6 %all_to_all.26.parts_ref = bf16[4,256,512]{2,1,0:T(8,128)(2,1)S(1)} all-to-all(bf16[4,256,512]{2,1,0:T(8,128)(2,1)} %bitcast.23), channel_id=1, replica_groups=mesh['x'=4,'k'=4,'h'=2,'z'=8,'c'=2] {'x'}, dimensions={0} | all-to-all | bytes 2097152 | tf_op jit(solution)/shard_map/all_to_all | solution.py:288
  94.1 0.2 active_rows.1.mine_ref
  94.3 3.1 %collective-permute-start.7 = (bf16[256,256]{1,0:T(8,128)(2,1)S(1)}, bf16[256,256]{1,0:T(8,128)(2,1)S(1)}, u32[]{:S(2)}, u32[]{:S(2)}) collective-permute-start(bf16[256,256]{1,0:T(8,128)(2,1)S(1)} %active_rows.1.mine_ref), channel_id=1, source_target_pairs={{0,16},{16,0},{1,17},{17,1},{2,18},{18,2},{3,19},{19,3},{4,20},{20... | collective-permute-start | bytes 393224 | tf_op jit(solution)/shard_map/ppermute | solution.py:143
  97.4 0.1 pad_add_fusion.1.place_ref
  97.4 2.5 %collective-permute-done.7.other_ref = bf16[256,256]{1,0:T(8,128)(2,1)S(1)} collective-permute-done((bf16[256,256]{1,0:T(8,128)(2,1)S(1)}, bf16[256,256]{1,0:T(8,128)(2,1)S(1)}, u32[]{:S(2)}, u32[]{:S(2)}) %collective-permute-start.7) | collective-permute-done | bytes 131104 | tf_op jit(solution)/shard_map/ppermute | solution.py:143
  100.0 0.0 copy-done
  100.0 3.3 %down_rows.2 = bf16[4,128,896]{2,1,0:T(8,128)(2,1)} custom-call(s32[2]{0:T(128)S(1)} %pad_add_fusion.1.place_ref, bf16[256,256]{1,0:T(8,128)(2,1)S(1)} %active_rows.1.mine_ref, bf16[256,256]{1,0:T(8,128)(2,1)S(1)} %collective-permute-done.7.other_ref, bf16[8,2,4,16,1920]{4,3,2,1,0:T(8,128)(2,1)} %bitcast.21, bf16[256,896]{1,0:T(8,128)(2,1)S(1)} %copy-done, ...), custom_call_target="tpu_custom_call" | custom-call | tf_op jit(solution)/shard_map/down_rows/pallas_call | solution.py:191
  103.3 4.4 %collective-permute-start.8 = (bf16[4,128,896]{2,1,0:T(8,128)(2,1)}, bf16[4,128,896]{2,1,0:T(8,128)(2,1)}, u32[]{:S(2)}, u32[]{:S(2)}) collective-permute-start(bf16[4,128,896]{2,1,0:T(8,128)(2,1)} %down_rows.2), channel_id=1, source_target_pairs={{0,1},{1,0},{2,3},{3,2},{4,5},{5,4},{6,7},{7,6},{8,9},{9,8},{10,11... | collective-permute-start | bytes 2752520 | tf_op jit(solution)/shard_map/ppermute | solution.py:143
  107.7 0.1 pad_add_fusion.place_ref
  107.8 0.0 copy-start.2
  107.8 2.3 %collective-permute-done.8.refs_8_ = bf16[4,128,896]{2,1,0:T(8,128)(2,1)} collective-permute-done((bf16[4,128,896]{2,1,0:T(8,128)(2,1)}, bf16[4,128,896]{2,1,0:T(8,128)(2,1)}, u32[]{:S(2)}, u32[]{:S(2)}) %collective-permute-start.8) | collective-permute-done | bytes 917536 | tf_op jit(solution)/shard_map/ppermute | solution.py:143
  110.1 2.7 %down_rows.3 = bf16[4,128,896]{2,1,0:T(8,128)(2,1)S(1)} custom-call(s32[2]{0:T(128)S(1)} %pad_add_fusion.place_ref, bf16[256,256]{1,0:T(8,128)(2,1)S(1)} %active_rows.1.mine_ref, bf16[256,256]{1,0:T(8,128)(2,1)S(1)} %collective-permute-done.7.other_ref, bf16[8,2,4,16,1920]{4,3,2,1,0:T(8,128)(2,1)} %bitcast.22, bf16[256,896]{1,0:T(8,128)(2,1)S(1)} %copy-done, ...), custom_call_target="tpu_custom_call" | custom-call | tf_op jit(solution)/shard_map/down_rows/pallas_call | solution.py:191
  112.9 36.9 %all_to_all.27.landed_ref = bf16[32,16,896]{2,1,0:T(8,128)(2,1)S(1)} all-to-all(bf16[32,16,896]{2,1,0:T(8,128)(2,1)S(1)} %bitcast.18), channel_id=1, replica_groups=mesh['x'=4,'k'=4,'h'=2,'z'=8,'c'=2] {'k','z'}, dimensions={0} | all-to-all | bytes 1835008 | tf_op jit(solution)/shard_map/all_to_all | solution.py:298
  149.8 0.0 copy-done.2
  149.8 1.3 last_sum.1
Async XLA Ops:
  7.2 63.1 %all-gather.2.cloned.1.call-start = ((), (), s32[]{:S(2)}) async-start(), calls=%async_computation.5 | async-start | bytes 4177920 | tf_op jit(solution)/shard_map/all_gather | solution.py:271
  20.1 11.4 %collective-permute-start = (bf16[256,896]{1,0:T(8,128)(2,1)}, bf16[256,896]{1,0:T(8,128)(2,1)S(1)}, u32[]{:S(2)}, u32[]{:S(2)}) collective-permute-start(bf16[256,896]{1,0:T(8,128)(2,1)} %get-tuple-element.18), channel_id=1, source_target_pairs={{0,16},{16,0},{1,17},{17,1},{2,18},{18,2},{3,19},{19,3},{4,20},{20... | collective-permute-start | bytes 1376264 | tf_op jit(solution)/shard_map/ppermute | solution.py:143
  23.3 18.7 %all-to-all-start.1 = ((bf16[8,2,16,576]{3,2,1,0:T(8,128)(2,1)}), bf16[8,2,16,576]{3,2,1,0:T(8,128)(2,1)S(1)}, u32[]{:S(2)}, u32[]{:S(2)}) async-start(bf16[8,2,16,576]{3,2,1,0:T(8,128)(2,1)} %bitcast.29), calls=%async_computation.1 | async-start | bytes 655360 | tf_op jit(solution)/shard_map/all_to_all | solution.py:125
  29.3 22.0 %collective-permute-start.1 = (bf16[256,896]{1,0:T(8,128)(2,1)}, bf16[256,896]{1,0:T(8,128)(2,1)S(1)}, u32[]{:S(2)}, u32[]{:S(2)}) collective-permute-start(bf16[256,896]{1,0:T(8,128)(2,1)} %get-tuple-element.21.refs_0_), channel_id=1, source_target_pairs={{0,128},{128,256},{256,384},{384,0},{1,129},{129,257},{257,385},{3... | collective-permute-start | bytes 1376264 | tf_op jit(solution)/shard_map/ppermute | solution.py:148
  31.6 22.2 %collective-permute-start.4 = (bf16[256,896]{1,0:T(8,128)(2,1)S(1)}, bf16[256,896]{1,0:T(8,128)(2,1)S(1)}, u32[]{:S(2)}, u32[]{:S(2)}) collective-permute-start(bf16[256,896]{1,0:T(8,128)(2,1)S(1)} %collective-permute-done.refs_1_), channel_id=1, source_target_pairs={{0,384},{128,0},{256,128},{384,256},{1,385},{129,1},{257,129},{385... | collective-permute-start | bytes 1376264 | tf_op jit(solution)/shard_map/ppermute | solution.py:148
  35.8 22.0 %collective-permute-start.3 = (bf16[256,896]{1,0:T(8,128)(2,1)}, bf16[256,896]{1,0:T(8,128)(2,1)S(1)}, u32[]{:S(2)}, u32[]{:S(2)}) collective-permute-start(bf16[256,896]{1,0:T(8,128)(2,1)} %get-tuple-element.21.refs_0_), channel_id=1, source_target_pairs={{0,384},{128,0},{256,128},{384,256},{1,385},{129,1},{257,129},{385... | collective-permute-start | bytes 1376264 | tf_op jit(solution)/shard_map/ppermute | solution.py:148
  37.7 20.1 %collective-permute-start.2 = (bf16[256,896]{1,0:T(8,128)(2,1)S(1)}, bf16[256,896]{1,0:T(8,128)(2,1)S(1)}, u32[]{:S(2)}, u32[]{:S(2)}) collective-permute-start(bf16[256,896]{1,0:T(8,128)(2,1)S(1)} %collective-permute-done.refs_1_), channel_id=1, source_target_pairs={{0,128},{128,256},{256,384},{384,0},{1,129},{129,257},{257,385},{3... | collective-permute-start | bytes 1376264 | tf_op jit(solution)/shard_map/ppermute | solution.py:148
  42.0 0.7 copy-start.3
  45.4 15.2 %all-to-all-start.2 = ((bf16[8,2,16,512]{3,2,1,0:T(8,128)(2,1)}), bf16[8,2,16,512]{3,2,1,0:T(8,128)(2,1)S(1)}, u32[]{:S(2)}, u32[]{:S(2)}) async-start(bf16[8,2,16,512]{3,2,1,0:T(8,128)(2,1)} %attend.1), calls=%async_computation.2 | async-start | bytes 524288 | tf_op jit(solution)/shard_map/all_to_all | solution.py:137
  51.2 24.2 %collective-permute-start.5 = (bf16[256,896]{1,0:T(8,128)(2,1)S(1)}, bf16[256,896]{1,0:T(8,128)(2,1)S(1)}, u32[]{:S(2)}, u32[]{:S(2)}) collective-permute-start(bf16[256,896]{1,0:T(8,128)(2,1)S(1)} %collective-permute-done.1.refs_2_), channel_id=1, source_target_pairs={{0,128},{128,256},{256,384},{384,0},{1,129},{129,257},{257,385},{3... | collective-permute-start | bytes 1376264 | tf_op jit(solution)/shard_map/ppermute | solution.py:148
  53.8 21.7 %collective-permute-start.6 = (bf16[256,896]{1,0:T(8,128)(2,1)S(1)}, bf16[256,896]{1,0:T(8,128)(2,1)}, u32[]{:S(2)}, u32[]{:S(2)}) collective-permute-start(bf16[256,896]{1,0:T(8,128)(2,1)S(1)} %collective-permute-done.4.refs_5_), channel_id=1, source_target_pairs={{0,384},{128,0},{256,128},{384,256},{1,385},{129,1},{257,129},{385... | collective-permute-start | bytes 1376264 | tf_op jit(solution)/shard_map/ppermute | solution.py:148
  60.6 0.7 copy-start.1
  70.3 29.7 %copy-start = (bf16[256,896]{1,0:T(8,128)(2,1)S(1)}, bf16[256,896]{1,0:T(8,128)(2,1)}, u32[]{:S(2)}) copy-start(bf16[256,896]{1,0:T(8,128)(2,1)} %get-tuple-element.21.refs_0_) | copy-start | bytes 1376260
  94.3 5.7 %collective-permute-start.7 = (bf16[256,256]{1,0:T(8,128)(2,1)S(1)}, bf16[256,256]{1,0:T(8,128)(2,1)S(1)}, u32[]{:S(2)}, u32[]{:S(2)}) collective-permute-start(bf16[256,256]{1,0:T(8,128)(2,1)S(1)} %active_rows.1.mine_ref), channel_id=1, source_target_pairs={{0,16},{16,0},{1,17},{17,1},{2,18},{18,2},{3,19},{19,3},{4,20},{20... | collective-permute-start | bytes 393224 | tf_op jit(solution)/shard_map/ppermute | solution.py:143
  103.3 6.9 %collective-permute-start.8 = (bf16[4,128,896]{2,1,0:T(8,128)(2,1)}, bf16[4,128,896]{2,1,0:T(8,128)(2,1)}, u32[]{:S(2)}, u32[]{:S(2)}) collective-permute-start(bf16[4,128,896]{2,1,0:T(8,128)(2,1)} %down_rows.2), channel_id=1, source_target_pairs={{0,1},{1,0},{2,3},{3,2},{4,5},{5,4},{6,7},{7,6},{8,9},{9,8},{10,11... | collective-permute-start | bytes 2752520 | tf_op jit(solution)/shard_map/ppermute | solution.py:143
  107.8 42.0 %copy-start.2 = (bf16[8,2,16,512]{3,2,1,0:T(8,128)(2,1)S(1)}, bf16[8,2,16,512]{3,2,1,0:T(8,128)(2,1)}, u32[]{:S(2)}) copy-start(bf16[8,2,16,512]{3,2,1,0:T(8,128)(2,1)} %copy-done.1) | copy-start | bytes 786436
Sparse Core Ops, SparseCore 0:
  20.2 50.0 all-gather.1

commit v4 on v3

--- a/solution.py
+++ b/solution.py
@@ -79,12 +79,15 @@
     out_ref[...] = (gate / (1.0 + jnp.exp(-gate)) * up).astype(BF)
 
 
-def down_kernel(place_ref, mine_ref, other_ref, route_ref, *refs):
-    weights, added, out_ref = refs[:8], refs[8:-1], refs[-1]
-    x_count = out_ref.shape[0]
+def down_kernel(place_ref, mine_ref, other_ref, route_ref, own_route_ref, *refs):
+    weights, (send_ref, keep_ref) = refs[:8], refs[8:]
+    x_count, half = send_ref.shape[:2]
     me = lax.axis_index("x")
     rows = mine_ref.shape[0]
-    route = route_ref[...].reshape(rows, route_ref.shape[-1]).astype(F32)
+    route = jnp.concatenate(
+        [ref[...].reshape(half, ref.shape[-1]).astype(F32) for ref in (route_ref, own_route_ref)],
+        axis=0,
+    )
     lane = lax.broadcasted_iota(jnp.int32, route.shape, 1)
     experts = lax.axis_size("z") * lax.axis_size("c")
     own = lax.axis_index("z") * lax.axis_size("c") + lax.axis_index("c")
@@ -95,9 +98,8 @@
         first = jnp.dot(mine_ref[...], weights[number][...], preferred_element_type=F32)
         second = jnp.dot(other_ref[...], weights[number + 1][...], preferred_element_type=F32)
         total = (first.astype(BF).astype(F32) + second.astype(BF).astype(F32)) * coef
-        for ref in added:
-            total = total + ref[place].astype(F32)
-        out_ref[place] = total.astype(BF)
+        send_ref[place] = total[:half].astype(BF)
+        keep_ref[place] = total[half:]
 
 
 def attend_kernel(lengths_ref, queries_ref, cache_ref, out_ref):
@@ -117,13 +119,14 @@
         out_ref[:, row] = latent.astype(BF).reshape(pieces, heads, latents)
 
 
-def attention(queries_b, cache_b, lengths_b):
+def attention(queries_b, cache_b, lengths_b, beside):
     heads_dev, channels = queries_b.shape[2:]
     tensor_size = lax.axis_size("k") * lax.axis_size("h")
     rows_owned = cache_b.shape[1]
     asked = queries_b[0].reshape(tensor_size, rows_owned, heads_dev, channels)
     pieces = lax.all_to_all(asked, ("k", "h"), split_axis=0, concat_axis=0, tiled=True)
-    return pl.pallas_call(
+    pieces, beside = lax.optimization_barrier((pieces, beside))
+    result = pl.pallas_call(
         attend_kernel,
         out_shape=jax.ShapeDtypeStruct((*pieces.shape[:3], LAT), BF),
         in_specs=[pl.BlockSpec(memory_space=pltpu.SMEM), VMEM, VMEM],
@@ -131,6 +134,7 @@
         compiler_params=WIDE,
         name="attend",
     )(lengths_b, pieces, cache_b[0].transpose(0, 2, 1))
+    return result, beside
 
 
 def answer(result):
@@ -181,30 +185,31 @@
     )(parts)
 
 
-def down(half, mine, other, gathered, place, weights, added):
+def down(mine, other, gathered, place, weights):
     z_size, cores, x_size, rows, columns = gathered.shape
-    count, hidden = mine.shape[0] // cores, mine.shape[1]
+    count, hidden = mine.shape
     lanes = 128
-    last = columns // lanes - 1
+    last_lanes = columns // lanes - 1
     whole = pl.BlockSpec(memory_space=pltpu.VMEM)
-    out_columns = weights[0].shape[1]
+    shape = (x_size, count // cores, weights[0].shape[1])
     return pl.pallas_call(
         down_kernel,
-        out_shape=jax.ShapeDtypeStruct((x_size, count, out_columns), BF),
+        out_shape=(jax.ShapeDtypeStruct(shape, BF), jax.ShapeDtypeStruct(shape, F32)),
         grid_spec=pltpu.PrefetchScalarGridSpec(
             num_scalar_prefetch=1,
             grid=(1,),
             in_specs=[
-                pl.BlockSpec((count, hidden), lambda i, p: (half, 0)),
-                pl.BlockSpec((count, hidden), lambda i, p: (half, 0)),
-                pl.BlockSpec((z_size, 1, 1, rows, lanes), lambda i, p: (0, p[0], p[1], 0, last)),
+                whole,
+                whole,
+                pl.BlockSpec((z_size, 1, 1, rows, lanes), lambda i, p: (0, p[0], p[1], 0, last_lanes)),
+                pl.BlockSpec((z_size, 1, 1, rows, lanes), lambda i, p: (0, 1 - p[0], p[1], 0, last_lanes)),
             ]
-            + [whole] * (len(weights) + len(added)),
-            out_specs=whole,
+            + [whole] * len(weights),
+            out_specs=(whole, whole),
         ),
         compiler_params=PARAMS,
         name="down_rows",
-    )(place, mine, other, gathered, *weights, *added)
+    )(place, mine, other, gathered, gathered, *weights)
 
 
 def last_kernel(landed_ref, latent_ref, mixed_ref, latent_out_ref, sem):
@@ -276,9 +281,9 @@
     mine_lower, mine_upper = shift(mine, 1), shift(mine, -1)
     theirs_lower, theirs_upper = shift(theirs, 1), shift(theirs, -1)
     across = (shift(mine_lower, 1), shift(theirs_upper, -1))
+    result, mine_upper = attention(queries_b, cache_b, lengths_b, mine_upper)
     weights = (mine, theirs, mine_lower, theirs_lower, mine_upper, theirs_upper, *across)
 
-    result = attention(queries_b, cache_b, lengths_b)
     latent_b = answer(result)
     gathered, latent_b, near = lax.optimization_barrier((gathered, latent_b, weights[:6]))
     core, x_place = lax.axis_index("c"), lax.axis_index("x")
@@ -288,12 +293,9 @@
     parts = lax.all_to_all(partial, "x", split_axis=0, concat_axis=0, tiled=True)
     active = swiglu(parts)
     active_other = swap(active, "h")
-    added = ()
-    for half in range(cores):
-        place = jnp.stack([lax.rem(core + 1 + half, cores), x_place])
-        out = down(half, active, active_other, gathered, place, weights, added)
-        if not added:
-            added = (swap(out, "c"),)
+    place = jnp.stack([lax.rem(core + 1, cores), x_place])
+    sent, kept = down(active, active_other, gathered, place, weights)
+    out = (kept + swap(sent, "c").astype(F32)).astype(BF)
     both = out.reshape(-1, rows, columns)
     landed = lax.all_to_all(both, ("k", "z"), split_axis=0, concat_axis=0, tiled=True)
     return last(landed, latent_b)

time: 159 us -> 158 us (level)
  Pallas kernels: 17.8 us -> 16 us
  waiting for transfers between devices: 17.6 us -> 19.4 us
  other arithmetic: 0.15 us -> 1.75 us
    pallas_call x2 -> x1, Pallas kernels: 6.03 us -> 4.34 us  [down(): pl.pallas_call(down_kernel, out_shape=(jax.ShapeDtypeStruct(shape, BF), j...]
    convert_element_type x0 -> x1, other arithmetic: none -> 1.67 us  [shards(): out = (kept + swap(sent, 'c').astype(F32)).astype(BF)]
where the time goes in v4:
time: 158 us; the launch traced here: 157 us
  blocking collectives  65.9 us (42%)
  starting transfers between devices  39.5 us (25%)
  waiting for transfers between devices  19.4 us (12%)
  Pallas kernels  16 us (10%)
  between operations  14.2 us (9%)
  other arithmetic  1.75 us (1%)
    all_to_all x1, blocking collectives, shards(): lax.all_to_all(both, ('k', 'z'), split_axis=0, concat_axis=0, tiled=True)  36.7 us
    all_to_all x1, blocking collectives, shards(): lax.all_to_all(partial, 'x', split_axis=0, concat_axis=0, tiled=True)  18.8 us
    ppermute x6, starting transfers between devices, shift(): lax.ppermute(array, 'x', [(i, (i + step) % size) for i in range(size)])  17.7 us
    ppermute x3, starting transfers between devices, swap(): return lax.ppermute(array, axis, [(0, 1), (1, 0)])  10.8 us
    all_gather x1, waiting for transfers between devices, shards(): lax.all_gather(sliced.reshape(x_size * rows, width + lanes), ('z', 'c'),...  10.5 us
    all_to_all x1, blocking collectives, shards(): lax.all_to_all(normed, 'x', split_axis=0, concat_axis=0, tiled=True)  10.4 us
    all_to_all x1, starting transfers between devices, attention(): lax.all_to_all(asked, ('k', 'h'), split_axis=0, concat_axis=0, tiled=True)  5.93 us
    all_to_all x1, starting transfers between devices, answer(): lax.all_to_all(result, ('k', 'h'), split_axis=0, concat_axis=0, tiled=True)  5.12 us
  transfers between devices with their start and end apart: 12, of which 5 were waited for; matrix products, arithmetic and copies ran while one was open for 0% of the time, Pallas kernels for 5%

profile of v4, /device:TPU:1, one launch (start us, length us, event | category | flops | bytes accessed | tf_op | source)
XLA Modules:
  0.0 157.5 jit_solution(14072343155541825990)
XLA Ops:
  7.2 0.0 all-gather.2.cloned.1.call-start
  7.2 2.5 %norm_rows.1 = (bf16[4,16,1920]{2,1,0:T(8,128)(2,1)}, bf16[256,896]{1,0:T(8,128)(2,1)}, bf16[256,896]{1,0:T(8,128)(2,1)}) custom-call(bf16[16,7168]{1,0:T(8,128)(2,1)} %tokens_ref.1, f32[1,7168]{1,0:T(1,128)} %bitcast.28, s32[8,16]{1,0:T(8,128)} %bitcast.29, f32[8,16]{1,0:T(8,128)} %bitcast.30, bf16[256,1792]{1,0:T(8,128)(2,1)} %bitcast.24), custom_call_target="tpu_custom_call" | custom-call | tf_op jit(solution)/shard_map/norm_rows/pallas_call | solution.py:260
  9.7 10.4 %all_to_all.25 = bf16[4,16,1920]{2,1,0:T(8,128)(2,1)} all-to-all(bf16[4,16,1920]{2,1,0:T(8,128)(2,1)} %get-tuple-element.20), channel_id=1, replica_groups=mesh['x'=4,'k'=4,'h'=2,'z'=8,'c'=2] {'x'}, dimensions={0} | all-to-all | bytes 491520 | tf_op jit(solution)/shard_map/all_to_all | solution.py:275
  20.1 0.0 all-gather.2.cloned.1.call-update
  20.1 3.2 %collective-permute-start.1 = (bf16[256,896]{1,0:T(8,128)(2,1)}, bf16[256,896]{1,0:T(8,128)(2,1)S(1)}, u32[]{:S(2)}, u32[]{:S(2)}) collective-permute-start(bf16[256,896]{1,0:T(8,128)(2,1)} %get-tuple-element.23), channel_id=1, source_target_pairs={{0,16},{16,0},{1,17},{17,1},{2,18},{18,2},{3,19},{19,3},{4,20},{20... | collective-permute-start | bytes 1376264 | tf_op jit(solution)/shard_map/ppermute | solution.py:147
  23.3 5.9 %all-to-all-start.1 = ((bf16[8,2,16,576]{3,2,1,0:T(8,128)(2,1)}), bf16[8,2,16,576]{3,2,1,0:T(8,128)(2,1)S(1)}, u32[]{:S(2)}, u32[]{:S(2)}) async-start(bf16[8,2,16,576]{3,2,1,0:T(8,128)(2,1)} %bitcast.8), calls=%async_computation.1 | async-start | bytes 655360 | tf_op jit(solution)/shard_map/all_to_all | solution.py:127
  29.3 2.8 %collective-permute-start = (bf16[256,896]{1,0:T(8,128)(2,1)}, bf16[256,896]{1,0:T(8,128)(2,1)S(1)}, u32[]{:S(2)}, u32[]{:S(2)}) collective-permute-start(bf16[256,896]{1,0:T(8,128)(2,1)} %get-tuple-element.27.refs_0_), channel_id=1, source_target_pairs={{0,384},{128,0},{256,128},{384,256},{1,385},{129,1},{257,129},{385... | collective-permute-start | bytes 1376264 | tf_op jit(solution)/shard_map/ppermute | solution.py:152
  32.0 2.5 %collective-permute-start.2 = (bf16[256,896]{1,0:T(8,128)(2,1)}, bf16[256,896]{1,0:T(8,128)(2,1)S(1)}, u32[]{:S(2)}, u32[]{:S(2)}) collective-permute-start(bf16[256,896]{1,0:T(8,128)(2,1)} %get-tuple-element.27.refs_0_), channel_id=1, source_target_pairs={{0,128},{128,256},{256,384},{384,0},{1,129},{129,257},{257,385},{3... | collective-permute-start | bytes 1376264 | tf_op jit(solution)/shard_map/ppermute | solution.py:152
  34.5 0.0 collective-permute-done.1.refs_1_
  34.6 4.0 %collective-permute-start.4 = (bf16[256,896]{1,0:T(8,128)(2,1)S(1)}, bf16[256,896]{1,0:T(8,128)(2,1)S(1)}, u32[]{:S(2)}, u32[]{:S(2)}) collective-permute-start(bf16[256,896]{1,0:T(8,128)(2,1)S(1)} %collective-permute-done.1.refs_1_), channel_id=1, source_target_pairs={{0,384},{128,0},{256,128},{384,256},{1,385},{129,1},{257,129},{385... | collective-permute-start | bytes 1376264 | tf_op jit(solution)/shard_map/ppermute | solution.py:152
  38.6 1.9 %collective-permute-start.3 = (bf16[256,896]{1,0:T(8,128)(2,1)S(1)}, bf16[256,896]{1,0:T(8,128)(2,1)S(1)}, u32[]{:S(2)}, u32[]{:S(2)}) collective-permute-start(bf16[256,896]{1,0:T(8,128)(2,1)S(1)} %collective-permute-done.1.refs_1_), channel_id=1, source_target_pairs={{0,128},{128,256},{256,384},{384,0},{1,129},{129,257},{257,385},{3... | collective-permute-start | bytes 1376264 | tf_op jit(solution)/shard_map/ppermute | solution.py:152
  40.5 0.0 collective-permute-done.refs_4_
  40.5 1.5 all-to-all-done.1.queries_ref
  42.0 0.0 copy-start.1
  42.0 0.7 copy-done.1
  42.8 2.6 %attend.1 = bf16[8,2,16,512]{3,2,1,0:T(8,128)(2,1)} custom-call(s32[1,2]{1,0:T(1,128)} %lengths_ref.1, bf16[8,2,16,576]{3,2,1,0:T(8,128)(2,1)} %copy-done.1, bf16[2,576,256]{2,1,0:T(8,128)(2,1)} %bitcast.27), custom_call_target="tpu_custom_call" | custom-call | tf_op jit(solution)/shard_map/attend/pallas_call | solution.py:129
  45.3 5.1 %all-to-all-start.2 = ((bf16[8,2,16,512]{3,2,1,0:T(8,128)(2,1)}), bf16[8,2,16,512]{3,2,1,0:T(8,128)(2,1)S(1)}, u32[]{:S(2)}, u32[]{:S(2)}) async-start(bf16[8,2,16,512]{3,2,1,0:T(8,128)(2,1)} %attend.1), calls=%async_computation.2 | async-start | bytes 524288 | tf_op jit(solution)/shard_map/all_to_all | solution.py:141
  50.5 0.0 collective-permute-done.2.refs_2_
  50.5 1.9 %collective-permute-start.5 = (bf16[256,896]{1,0:T(8,128)(2,1)S(1)}, bf16[256,896]{1,0:T(8,128)(2,1)}, u32[]{:S(2)}, u32[]{:S(2)}) collective-permute-start(bf16[256,896]{1,0:T(8,128)(2,1)S(1)} %collective-permute-done.2.refs_2_), channel_id=1, source_target_pairs={{0,128},{128,256},{256,384},{384,0},{1,129},{129,257},{257,385},{3... | collective-permute-start | bytes 1376264 | tf_op jit(solution)/shard_map/ppermute | solution.py:152
  52.4 0.0 collective-permute-done.4.refs_5_
  52.4 4.6 %collective-permute-start.6 = (bf16[256,896]{1,0:T(8,128)(2,1)S(1)}, bf16[256,896]{1,0:T(8,128)(2,1)}, u32[]{:S(2)}, u32[]{:S(2)}) collective-permute-start(bf16[256,896]{1,0:T(8,128)(2,1)S(1)} %collective-permute-done.4.refs_5_), channel_id=1, source_target_pairs={{0,384},{128,0},{256,128},{384,256},{1,385},{129,1},{257,129},{385... | collective-permute-start | bytes 1376264 | tf_op jit(solution)/shard_map/ppermute | solution.py:152
  57.0 0.0 collective-permute-done.3.refs_3_
  57.0 2.8 %all-to-all-done.2 = bf16[8,2,16,512]{3,2,1,0:T(8,128)(2,1)S(1)} async-done(((bf16[8,2,16,512]{3,2,1,0:T(8,128)(2,1)}), bf16[8,2,16,512]{3,2,1,0:T(8,128)(2,1)S(1)}, u32[]{:S(2)}, u32[]{:S(2)}) %all-to-all-start.2) | async-done | bytes 262176 | tf_op jit(solution)/shard_map/all_to_all | solution.py:141
  59.8 10.5 %all-gather.2.cloned.1.call-done = bf16[1024,1920]{1,0:T(8,128)(2,1)} async-done(((bf16[64,1920]{1,0:T(8,128)(2,1)}), bf16[1024,1920]{1,0:T(8,128)(2,1)}) %all-gather.2.cloned.1.call-update) | async-done | bytes 3932176 | tf_op jit(solution)/shard_map/all_gather | solution.py:276
  70.3 5.0 %gate_up.1 = bf16[4,2,8,16,512]{4,3,2,1,0:T(8,128)(2,1)} custom-call(bf16[8,2,4,16,1920]{4,3,2,1,0:T(8,128)(2,1)} %bitcast.18, bf16[1792,256]{1,0:T(8,128)(2,1)} %bitcast.25, bf16[1792,256]{1,0:T(8,128)(2,1)} %bitcast.26), custom_call_target="tpu_custom_call" | custom-call | tf_op jit(solution)/shard_map/gate_up/pallas_call | solution.py:159
  75.3 0.0 copy-start
  75.3 0.0 collective-permute-done.5.refs_6_
  75.3 0.0 collective-permute-done.6.refs_7_
  75.3 18.8 %all_to_all.26.parts_ref = bf16[4,256,512]{2,1,0:T(8,128)(2,1)S(1)} all-to-all(bf16[4,256,512]{2,1,0:T(8,128)(2,1)} %bitcast.21), channel_id=1, replica_groups=mesh['x'=4,'k'=4,'h'=2,'z'=8,'c'=2] {'x'}, dimensions={0} | all-to-all | bytes 2097152 | tf_op jit(solution)/shard_map/all_to_all | solution.py:293
  94.1 0.2 active_rows.1.mine_ref
  94.3 3.1 %collective-permute-start.7 = (bf16[256,256]{1,0:T(8,128)(2,1)S(1)}, bf16[256,256]{1,0:T(8,128)(2,1)S(1)}, u32[]{:S(2)}, u32[]{:S(2)}) collective-permute-start(bf16[256,256]{1,0:T(8,128)(2,1)S(1)} %active_rows.1.mine_ref), channel_id=1, source_target_pairs={{0,16},{16,0},{1,17},{17,1},{2,18},{18,2},{3,19},{19,3},{4,20},{20... | collective-permute-start | bytes 393224 | tf_op jit(solution)/shard_map/ppermute | solution.py:147
  97.4 0.1 pad_add_fusion.place_ref
  97.5 2.5 %collective-permute-done.7.other_ref = bf16[256,256]{1,0:T(8,128)(2,1)S(1)} collective-permute-done((bf16[256,256]{1,0:T(8,128)(2,1)S(1)}, bf16[256,256]{1,0:T(8,128)(2,1)S(1)}, u32[]{:S(2)}, u32[]{:S(2)}) %collective-permute-start.7) | collective-permute-done | bytes 131104 | tf_op jit(solution)/shard_map/ppermute | solution.py:147
  100.0 0.0 copy-done
  100.0 4.3 %down_rows.1 = (bf16[4,128,896]{2,1,0:T(8,128)(2,1)S(1)}, f32[4,128,896]{2,1,0:T(8,128)}) custom-call(s32[2]{0:T(128)S(1)} %pad_add_fusion.place_ref, bf16[256,256]{1,0:T(8,128)(2,1)S(1)} %active_rows.1.mine_ref, bf16[256,256]{1,0:T(8,128)(2,1)S(1)} %collective-permute-done.7.other_ref, bf16[8,2,4,16,1920]{4,3,2,1,0:T(8,128)(2,1)} %bitcast.19, ...), custom_call_target="tpu_custom_call" | custom-call | tf_op jit(solution)/shard_map/down_rows/pallas_call | solution.py:195
  104.3 4.4 %collective-permute-start.8 = (bf16[4,128,896]{2,1,0:T(8,128)(2,1)S(1)}, bf16[4,128,896]{2,1,0:T(8,128)(2,1)S(1)}, u32[]{:S(2)}, u32[]{:S(2)}) collective-permute-start(bf16[4,128,896]{2,1,0:T(8,128)(2,1)S(1)} %get-tuple-element.36), channel_id=1, source_target_pairs={{0,1},{1,0},{2,3},{3,2},{4,5},{5,4},{6,7},{7,6},{8,9},{9,8},{10,11... | collective-permute-start | bytes 2752520 | tf_op jit(solution)/shard_map/ppermute | solution.py:147
  108.8 2.1 %collective-permute-done.8 = bf16[4,128,896]{2,1,0:T(8,128)(2,1)S(1)} collective-permute-done((bf16[4,128,896]{2,1,0:T(8,128)(2,1)S(1)}, bf16[4,128,896]{2,1,0:T(8,128)(2,1)S(1)}, u32[]{:S(2)}, u32[]{:S(2)}) %collective-permute-start.8) | collective-permute-done | bytes 917536 | tf_op jit(solution)/shard_map/ppermute | solution.py:147
  110.9 1.7 %add_convert_fusion = bf16[4,128,896]{2,1,0:T(8,128)(2,1)S(1)} fusion(f32[4,128,896]{2,1,0:T(8,128)} %get-tuple-element.35, bf16[4,128,896]{2,1,0:T(8,128)(2,1)S(1)} %collective-permute-done.8), kind=kLoop, calls=%fused_computation | loop fusion | flops 1376256 | bytes 3670016 | tf_op jit(solution)/shard_map/convert_element_type | solution.py:298
  112.5 36.7 %all_to_all.27.landed_ref = bf16[32,16,896]{2,1,0:T(8,128)(2,1)S(1)} all-to-all(bf16[32,16,896]{2,1,0:T(8,128)(2,1)S(1)} %bitcast.22), channel_id=1, replica_groups=mesh['x'=4,'k'=4,'h'=2,'z'=8,'c'=2] {'k','z'}, dimensions={0} | all-to-all | bytes 1835008 | tf_op jit(solution)/shard_map/all_to_all | solution.py:300
  149.3 1.3 last_sum.1
Async XLA Ops:
  7.2 63.1 %all-gather.2.cloned.1.call-start = ((), (), s32[]{:S(2)}) async-start(), calls=%async_computation.5 | async-start | bytes 4177920 | tf_op jit(solution)/shard_map/all_gather | solution.py:276
  20.1 14.4 %collective-permute-start.1 = (bf16[256,896]{1,0:T(8,128)(2,1)}, bf16[256,896]{1,0:T(8,128)(2,1)S(1)}, u32[]{:S(2)}, u32[]{:S(2)}) collective-permute-start(bf16[256,896]{1,0:T(8,128)(2,1)} %get-tuple-element.23), channel_id=1, source_target_pairs={{0,16},{16,0},{1,17},{17,1},{2,18},{18,2},{3,19},{19,3},{4,20},{20... | collective-permute-start | bytes 1376264 | tf_op jit(solution)/shard_map/ppermute | solution.py:147
  23.3 18.7 %all-to-all-start.1 = ((bf16[8,2,16,576]{3,2,1,0:T(8,128)(2,1)}), bf16[8,2,16,576]{3,2,1,0:T(8,128)(2,1)S(1)}, u32[]{:S(2)}, u32[]{:S(2)}) async-start(bf16[8,2,16,576]{3,2,1,0:T(8,128)(2,1)} %bitcast.8), calls=%async_computation.1 | async-start | bytes 655360 | tf_op jit(solution)/shard_map/all_to_all | solution.py:127
  29.3 11.2 %collective-permute-start = (bf16[256,896]{1,0:T(8,128)(2,1)}, bf16[256,896]{1,0:T(8,128)(2,1)S(1)}, u32[]{:S(2)}, u32[]{:S(2)}) collective-permute-start(bf16[256,896]{1,0:T(8,128)(2,1)} %get-tuple-element.27.refs_0_), channel_id=1, source_target_pairs={{0,384},{128,0},{256,128},{384,256},{1,385},{129,1},{257,129},{385... | collective-permute-start | bytes 1376264 | tf_op jit(solution)/shard_map/ppermute | solution.py:152
  32.0 18.4 %collective-permute-start.2 = (bf16[256,896]{1,0:T(8,128)(2,1)}, bf16[256,896]{1,0:T(8,128)(2,1)S(1)}, u32[]{:S(2)}, u32[]{:S(2)}) collective-permute-start(bf16[256,896]{1,0:T(8,128)(2,1)} %get-tuple-element.27.refs_0_), channel_id=1, source_target_pairs={{0,128},{128,256},{256,384},{384,0},{1,129},{129,257},{257,385},{3... | collective-permute-start | bytes 1376264 | tf_op jit(solution)/shard_map/ppermute | solution.py:152
  34.6 17.8 %collective-permute-start.4 = (bf16[256,896]{1,0:T(8,128)(2,1)S(1)}, bf16[256,896]{1,0:T(8,128)(2,1)S(1)}, u32[]{:S(2)}, u32[]{:S(2)}) collective-permute-start(bf16[256,896]{1,0:T(8,128)(2,1)S(1)} %collective-permute-done.1.refs_1_), channel_id=1, source_target_pairs={{0,384},{128,0},{256,128},{384,256},{1,385},{129,1},{257,129},{385... | collective-permute-start | bytes 1376264 | tf_op jit(solution)/shard_map/ppermute | solution.py:152
  38.6 18.4 %collective-permute-start.3 = (bf16[256,896]{1,0:T(8,128)(2,1)S(1)}, bf16[256,896]{1,0:T(8,128)(2,1)S(1)}, u32[]{:S(2)}, u32[]{:S(2)}) collective-permute-start(bf16[256,896]{1,0:T(8,128)(2,1)S(1)} %collective-permute-done.1.refs_1_), channel_id=1, source_target_pairs={{0,128},{128,256},{256,384},{384,0},{1,129},{129,257},{257,385},{3... | collective-permute-start | bytes 1376264 | tf_op jit(solution)/shard_map/ppermute | solution.py:152
  42.0 0.7 copy-start.1
  45.3 14.5 %all-to-all-start.2 = ((bf16[8,2,16,512]{3,2,1,0:T(8,128)(2,1)}), bf16[8,2,16,512]{3,2,1,0:T(8,128)(2,1)S(1)}, u32[]{:S(2)}, u32[]{:S(2)}) async-start(bf16[8,2,16,512]{3,2,1,0:T(8,128)(2,1)} %attend.1), calls=%async_computation.2 | async-start | bytes 524288 | tf_op jit(solution)/shard_map/all_to_all | solution.py:141
  50.5 24.8 %collective-permute-start.5 = (bf16[256,896]{1,0:T(8,128)(2,1)S(1)}, bf16[256,896]{1,0:T(8,128)(2,1)}, u32[]{:S(2)}, u32[]{:S(2)}) collective-permute-start(bf16[256,896]{1,0:T(8,128)(2,1)S(1)} %collective-permute-done.2.refs_2_), channel_id=1, source_target_pairs={{0,128},{128,256},{256,384},{384,0},{1,129},{129,257},{257,385},{3... | collective-permute-start | bytes 1376264 | tf_op jit(solution)/shard_map/ppermute | solution.py:152
  52.4 22.9 %collective-permute-start.6 = (bf16[256,896]{1,0:T(8,128)(2,1)S(1)}, bf16[256,896]{1,0:T(8,128)(2,1)}, u32[]{:S(2)}, u32[]{:S(2)}) collective-permute-start(bf16[256,896]{1,0:T(8,128)(2,1)S(1)} %collective-permute-done.4.refs_5_), channel_id=1, source_target_pairs={{0,384},{128,0},{256,128},{384,256},{1,385},{129,1},{257,129},{385... | collective-permute-start | bytes 1376264 | tf_op jit(solution)/shard_map/ppermute | solution.py:152
  75.3 24.7 %copy-start = (bf16[256,896]{1,0:T(8,128)(2,1)S(1)}, bf16[256,896]{1,0:T(8,128)(2,1)}, u32[]{:S(2)}) copy-start(bf16[256,896]{1,0:T(8,128)(2,1)} %get-tuple-element.27.refs_0_) | copy-start | bytes 1376260
  94.3 5.7 %collective-permute-start.7 = (bf16[256,256]{1,0:T(8,128)(2,1)S(1)}, bf16[256,256]{1,0:T(8,128)(2,1)S(1)}, u32[]{:S(2)}, u32[]{:S(2)}) collective-permute-start(bf16[256,256]{1,0:T(8,128)(2,1)S(1)} %active_rows.1.mine_ref), channel_id=1, source_target_pairs={{0,16},{16,0},{1,17},{17,1},{2,18},{18,2},{3,19},{19,3},{4,20},{20... | collective-permute-start | bytes 393224 | tf_op jit(solution)/shard_map/ppermute | solution.py:147
  104.3 6.5 %collective-permute-start.8 = (bf16[4,128,896]{2,1,0:T(8,128)(2,1)S(1)}, bf16[4,128,896]{2,1,0:T(8,128)(2,1)S(1)}, u32[]{:S(2)}, u32[]{:S(2)}) collective-permute-start(bf16[4,128,896]{2,1,0:T(8,128)(2,1)S(1)} %get-tuple-element.36), channel_id=1, source_target_pairs={{0,1},{1,0},{2,3},{3,2},{4,5},{5,4},{6,7},{7,6},{8,9},{9,8},{10,11... | collective-permute-start | bytes 2752520 | tf_op jit(solution)/shard_map/ppermute | solution.py:147
Sparse Core Ops, SparseCore 0:
  20.2 49.9 all-gather.1

commit v5 on v4

--- a/solution.py
+++ b/solution.py
@@ -99,7 +99,7 @@
         second = jnp.dot(other_ref[...], weights[number + 1][...], preferred_element_type=F32)
         total = (first.astype(BF).astype(F32) + second.astype(BF).astype(F32)) * coef
         send_ref[place] = total[:half].astype(BF)
-        keep_ref[place] = total[half:]
+        keep_ref[place] = total[half:].astype(BF)
 
 
 def attend_kernel(lengths_ref, queries_ref, cache_ref, out_ref):
@@ -194,7 +194,7 @@
     shape = (x_size, count // cores, weights[0].shape[1])
     return pl.pallas_call(
         down_kernel,
-        out_shape=(jax.ShapeDtypeStruct(shape, BF), jax.ShapeDtypeStruct(shape, F32)),
+        out_shape=(jax.ShapeDtypeStruct(shape, BF), jax.ShapeDtypeStruct(shape, BF)),
         grid_spec=pltpu.PrefetchScalarGridSpec(
             num_scalar_prefetch=1,
             grid=(1,),
@@ -295,7 +295,7 @@
     active_other = swap(active, "h")
     place = jnp.stack([lax.rem(core + 1, cores), x_place])
     sent, kept = down(active, active_other, gathered, place, weights)
-    out = (kept + swap(sent, "c").astype(F32)).astype(BF)
+    out = (kept.astype(F32) + swap(sent, "c").astype(F32)).astype(BF)
     both = out.reshape(-1, rows, columns)
     landed = lax.all_to_all(both, ("k", "z"), split_axis=0, concat_axis=0, tiled=True)
     return last(landed, latent_b)

time: 158 us -> 156 us (0.987)
  no operation moved by 1% of the time
where the time goes in v5:
time: 156 us; the launch traced here: 155 us
  blocking collectives  65.9 us (42%)
  starting transfers between devices  39.5 us (25%)
  waiting for transfers between devices  19.4 us (12%)
  Pallas kernels  14.7 us (9%)
  between operations  14.2 us (9%)
    all_to_all x1, blocking collectives, shards(): lax.all_to_all(both, ('k', 'z'), split_axis=0, concat_axis=0, tiled=True)  36.7 us
    all_to_all x1, blocking collectives, shards(): lax.all_to_all(partial, 'x', split_axis=0, concat_axis=0, tiled=True)  18.8 us
    ppermute x6, starting transfers between devices, shift(): lax.ppermute(array, 'x', [(i, (i + step) % size) for i in range(size)])  17.7 us
    ppermute x3, starting transfers between devices, swap(): return lax.ppermute(array, axis, [(0, 1), (1, 0)])  10.8 us
    all_gather x1, waiting for transfers between devices, shards(): lax.all_gather(sliced.reshape(x_size * rows, width + lanes), ('z', 'c'),...  10.5 us
    all_to_all x1, blocking collectives, shards(): lax.all_to_all(normed, 'x', split_axis=0, concat_axis=0, tiled=True)  10.4 us
    all_to_all x1, starting transfers between devices, attention(): lax.all_to_all(asked, ('k', 'h'), split_axis=0, concat_axis=0, tiled=True)  5.93 us
    all_to_all x1, starting transfers between devices, answer(): lax.all_to_all(result, ('k', 'h'), split_axis=0, concat_axis=0, tiled=True)  5.12 us
  transfers between devices with their start and end apart: 12, of which 5 were waited for; matrix products, arithmetic and copies ran while one was open for 0% of the time, Pallas kernels for 5%

profile of v5, /device:TPU:1, one launch (start us, length us, event | category | flops | bytes accessed | tf_op | source)
XLA Modules:
  0.0 154.7 jit_solution(10530900663942910664)
XLA Ops:
  7.2 0.0 all-gather.2.cloned.1.call-start
  7.2 2.5 %norm_rows.1 = (bf16[4,16,1920]{2,1,0:T(8,128)(2,1)}, bf16[256,896]{1,0:T(8,128)(2,1)}, bf16[256,896]{1,0:T(8,128)(2,1)}) custom-call(bf16[16,7168]{1,0:T(8,128)(2,1)} %tokens_ref.1, f32[1,7168]{1,0:T(1,128)} %bitcast.28, s32[8,16]{1,0:T(8,128)} %bitcast.29, f32[8,16]{1,0:T(8,128)} %bitcast.30, bf16[256,1792]{1,0:T(8,128)(2,1)} %bitcast.24), custom_call_target="tpu_custom_call" | custom-call | tf_op jit(solution)/shard_map/norm_rows/pallas_call | solution.py:260
  9.7 10.4 %all_to_all.25 = bf16[4,16,1920]{2,1,0:T(8,128)(2,1)} all-to-all(bf16[4,16,1920]{2,1,0:T(8,128)(2,1)} %get-tuple-element.20), channel_id=1, replica_groups=mesh['x'=4,'k'=4,'h'=2,'z'=8,'c'=2] {'x'}, dimensions={0} | all-to-all | bytes 491520 | tf_op jit(solution)/shard_map/all_to_all | solution.py:275
  20.1 0.0 all-gather.2.cloned.1.call-update
  20.1 3.2 %collective-permute-start.1 = (bf16[256,896]{1,0:T(8,128)(2,1)}, bf16[256,896]{1,0:T(8,128)(2,1)S(1)}, u32[]{:S(2)}, u32[]{:S(2)}) collective-permute-start(bf16[256,896]{1,0:T(8,128)(2,1)} %get-tuple-element.23), channel_id=1, source_target_pairs={{0,16},{16,0},{1,17},{17,1},{2,18},{18,2},{3,19},{19,3},{4,20},{20... | collective-permute-start | bytes 1376264 | tf_op jit(solution)/shard_map/ppermute | solution.py:147
  23.3 5.9 %all-to-all-start.1 = ((bf16[8,2,16,576]{3,2,1,0:T(8,128)(2,1)}), bf16[8,2,16,576]{3,2,1,0:T(8,128)(2,1)S(1)}, u32[]{:S(2)}, u32[]{:S(2)}) async-start(bf16[8,2,16,576]{3,2,1,0:T(8,128)(2,1)} %bitcast.8), calls=%async_computation.1 | async-start | bytes 655360 | tf_op jit(solution)/shard_map/all_to_all | solution.py:127
  29.3 2.8 %collective-permute-start = (bf16[256,896]{1,0:T(8,128)(2,1)}, bf16[256,896]{1,0:T(8,128)(2,1)S(1)}, u32[]{:S(2)}, u32[]{:S(2)}) collective-permute-start(bf16[256,896]{1,0:T(8,128)(2,1)} %get-tuple-element.27.refs_0_), channel_id=1, source_target_pairs={{0,384},{128,0},{256,128},{384,256},{1,385},{129,1},{257,129},{385... | collective-permute-start | bytes 1376264 | tf_op jit(solution)/shard_map/ppermute | solution.py:152
  32.0 2.5 %collective-permute-start.2 = (bf16[256,896]{1,0:T(8,128)(2,1)}, bf16[256,896]{1,0:T(8,128)(2,1)S(1)}, u32[]{:S(2)}, u32[]{:S(2)}) collective-permute-start(bf16[256,896]{1,0:T(8,128)(2,1)} %get-tuple-element.27.refs_0_), channel_id=1, source_target_pairs={{0,128},{128,256},{256,384},{384,0},{1,129},{129,257},{257,385},{3... | collective-permute-start | bytes 1376264 | tf_op jit(solution)/shard_map/ppermute | solution.py:152
  34.5 0.0 collective-permute-done.1.refs_1_
  34.6 4.0 %collective-permute-start.4 = (bf16[256,896]{1,0:T(8,128)(2,1)S(1)}, bf16[256,896]{1,0:T(8,128)(2,1)S(1)}, u32[]{:S(2)}, u32[]{:S(2)}) collective-permute-start(bf16[256,896]{1,0:T(8,128)(2,1)S(1)} %collective-permute-done.1.refs_1_), channel_id=1, source_target_pairs={{0,384},{128,0},{256,128},{384,256},{1,385},{129,1},{257,129},{385... | collective-permute-start | bytes 1376264 | tf_op jit(solution)/shard_map/ppermute | solution.py:152
  38.6 1.9 %collective-permute-start.3 = (bf16[256,896]{1,0:T(8,128)(2,1)S(1)}, bf16[256,896]{1,0:T(8,128)(2,1)S(1)}, u32[]{:S(2)}, u32[]{:S(2)}) collective-permute-start(bf16[256,896]{1,0:T(8,128)(2,1)S(1)} %collective-permute-done.1.refs_1_), channel_id=1, source_target_pairs={{0,128},{128,256},{256,384},{384,0},{1,129},{129,257},{257,385},{3... | collective-permute-start | bytes 1376264 | tf_op jit(solution)/shard_map/ppermute | solution.py:152
  40.5 0.0 collective-permute-done.refs_4_
  40.5 1.5 all-to-all-done.1.queries_ref
  42.0 0.0 copy-start.1
  42.0 0.7 copy-done.1
  42.8 2.6 %attend.1 = bf16[8,2,16,512]{3,2,1,0:T(8,128)(2,1)} custom-call(s32[1,2]{1,0:T(1,128)} %lengths_ref.1, bf16[8,2,16,576]{3,2,1,0:T(8,128)(2,1)} %copy-done.1, bf16[2,576,256]{2,1,0:T(8,128)(2,1)} %bitcast.27), custom_call_target="tpu_custom_call" | custom-call | tf_op jit(solution)/shard_map/attend/pallas_call | solution.py:129
  45.3 5.1 %all-to-all-start.2 = ((bf16[8,2,16,512]{3,2,1,0:T(8,128)(2,1)}), bf16[8,2,16,512]{3,2,1,0:T(8,128)(2,1)S(1)}, u32[]{:S(2)}, u32[]{:S(2)}) async-start(bf16[8,2,16,512]{3,2,1,0:T(8,128)(2,1)} %attend.1), calls=%async_computation.2 | async-start | bytes 524288 | tf_op jit(solution)/shard_map/all_to_all | solution.py:141
  50.5 0.0 collective-permute-done.2.refs_2_
  50.5 1.9 %collective-permute-start.5 = (bf16[256,896]{1,0:T(8,128)(2,1)S(1)}, bf16[256,896]{1,0:T(8,128)(2,1)}, u32[]{:S(2)}, u32[]{:S(2)}) collective-permute-start(bf16[256,896]{1,0:T(8,128)(2,1)S(1)} %collective-permute-done.2.refs_2_), channel_id=1, source_target_pairs={{0,128},{128,256},{256,384},{384,0},{1,129},{129,257},{257,385},{3... | collective-permute-start | bytes 1376264 | tf_op jit(solution)/shard_map/ppermute | solution.py:152
  52.4 0.0 collective-permute-done.4.refs_5_
  52.4 4.6 %collective-permute-start.6 = (bf16[256,896]{1,0:T(8,128)(2,1)S(1)}, bf16[256,896]{1,0:T(8,128)(2,1)}, u32[]{:S(2)}, u32[]{:S(2)}) collective-permute-start(bf16[256,896]{1,0:T(8,128)(2,1)S(1)} %collective-permute-done.4.refs_5_), channel_id=1, source_target_pairs={{0,384},{128,0},{256,128},{384,256},{1,385},{129,1},{257,129},{385... | collective-permute-start | bytes 1376264 | tf_op jit(solution)/shard_map/ppermute | solution.py:152
  57.0 0.0 collective-permute-done.3.refs_3_
  57.0 2.8 %all-to-all-done.2 = bf16[8,2,16,512]{3,2,1,0:T(8,128)(2,1)S(1)} async-done(((bf16[8,2,16,512]{3,2,1,0:T(8,128)(2,1)}), bf16[8,2,16,512]{3,2,1,0:T(8,128)(2,1)S(1)}, u32[]{:S(2)}, u32[]{:S(2)}) %all-to-all-start.2) | async-done | bytes 262176 | tf_op jit(solution)/shard_map/all_to_all | solution.py:141
  59.8 10.5 %all-gather.2.cloned.1.call-done = bf16[1024,1920]{1,0:T(8,128)(2,1)} async-done(((bf16[64,1920]{1,0:T(8,128)(2,1)}), bf16[1024,1920]{1,0:T(8,128)(2,1)}) %all-gather.2.cloned.1.call-update) | async-done | bytes 3932176 | tf_op jit(solution)/shard_map/all_gather | solution.py:276
  70.3 5.0 %gate_up.1 = bf16[4,2,8,16,512]{4,3,2,1,0:T(8,128)(2,1)} custom-call(bf16[8,2,4,16,1920]{4,3,2,1,0:T(8,128)(2,1)} %bitcast.18, bf16[1792,256]{1,0:T(8,128)(2,1)} %bitcast.25, bf16[1792,256]{1,0:T(8,128)(2,1)} %bitcast.26), custom_call_target="tpu_custom_call" | custom-call | tf_op jit(solution)/shard_map/gate_up/pallas_call | solution.py:159
  75.3 0.0 copy-start
  75.3 0.0 collective-permute-done.5.refs_6_
  75.3 0.0 collective-permute-done.6.refs_7_
  75.3 18.8 %all_to_all.26.parts_ref = bf16[4,256,512]{2,1,0:T(8,128)(2,1)S(1)} all-to-all(bf16[4,256,512]{2,1,0:T(8,128)(2,1)} %bitcast.21), channel_id=1, replica_groups=mesh['x'=4,'k'=4,'h'=2,'z'=8,'c'=2] {'x'}, dimensions={0} | all-to-all | bytes 2097152 | tf_op jit(solution)/shard_map/all_to_all | solution.py:293
  94.1 0.2 active_rows.1.mine_ref
  94.3 3.1 %collective-permute-start.7 = (bf16[256,256]{1,0:T(8,128)(2,1)S(1)}, bf16[256,256]{1,0:T(8,128)(2,1)S(1)}, u32[]{:S(2)}, u32[]{:S(2)}) collective-permute-start(bf16[256,256]{1,0:T(8,128)(2,1)S(1)} %active_rows.1.mine_ref), channel_id=1, source_target_pairs={{0,16},{16,0},{1,17},{17,1},{2,18},{18,2},{3,19},{19,3},{4,20},{20... | collective-permute-start | bytes 393224 | tf_op jit(solution)/shard_map/ppermute | solution.py:147
  97.4 0.1 pad_add_fusion.place_ref
  97.5 2.5 %collective-permute-done.7.other_ref = bf16[256,256]{1,0:T(8,128)(2,1)S(1)} collective-permute-done((bf16[256,256]{1,0:T(8,128)(2,1)S(1)}, bf16[256,256]{1,0:T(8,128)(2,1)S(1)}, u32[]{:S(2)}, u32[]{:S(2)}) %collective-permute-start.7) | collective-permute-done | bytes 131104 | tf_op jit(solution)/shard_map/ppermute | solution.py:147
  100.0 0.0 copy-done
  100.0 3.1 %down_rows.1 = (bf16[4,128,896]{2,1,0:T(8,128)(2,1)S(1)}, bf16[4,128,896]{2,1,0:T(8,128)(2,1)S(1)}) custom-call(s32[2]{0:T(128)S(1)} %pad_add_fusion.place_ref, bf16[256,256]{1,0:T(8,128)(2,1)S(1)} %active_rows.1.mine_ref, bf16[256,256]{1,0:T(8,128)(2,1)S(1)} %collective-permute-done.7.other_ref, bf16[8,2,4,16,1920]{4,3,2,1,0:T(8,128)(2,1)} %bitcast.19, ...), custom_call_target="tpu_custom_call" | custom-call | tf_op jit(solution)/shard_map/down_rows/pallas_call | solution.py:195
  103.1 4.5 %collective-permute-start.8 = (bf16[4,128,896]{2,1,0:T(8,128)(2,1)S(1)}, bf16[4,128,896]{2,1,0:T(8,128)(2,1)S(1)}, u32[]{:S(2)}, u32[]{:S(2)}) collective-permute-start(bf16[4,128,896]{2,1,0:T(8,128)(2,1)S(1)} %get-tuple-element.36), channel_id=1, source_target_pairs={{0,1},{1,0},{2,3},{3,2},{4,5},{5,4},{6,7},{7,6},{8,9},{9,8},{10,11... | collective-permute-start | bytes 2752520 | tf_op jit(solution)/shard_map/ppermute | solution.py:147
  107.5 2.1 %collective-permute-done.8 = bf16[4,128,896]{2,1,0:T(8,128)(2,1)S(1)} collective-permute-done((bf16[4,128,896]{2,1,0:T(8,128)(2,1)S(1)}, bf16[4,128,896]{2,1,0:T(8,128)(2,1)S(1)}, u32[]{:S(2)}, u32[]{:S(2)}) %collective-permute-start.8) | collective-permute-done | bytes 917536 | tf_op jit(solution)/shard_map/ppermute | solution.py:147
  109.6 0.2 add_convert_fusion
  109.8 36.7 %all_to_all.27.landed_ref = bf16[32,16,896]{2,1,0:T(8,128)(2,1)S(1)} all-to-all(bf16[32,16,896]{2,1,0:T(8,128)(2,1)S(1)} %bitcast.22), channel_id=1, replica_groups=mesh['x'=4,'k'=4,'h'=2,'z'=8,'c'=2] {'k','z'}, dimensions={0} | all-to-all | bytes 1835008 | tf_op jit(solution)/shard_map/all_to_all | solution.py:300
  146.6 1.3 last_sum.1
Async XLA Ops:
  7.2 63.1 %all-gather.2.cloned.1.call-start = ((), (), s32[]{:S(2)}) async-start(), calls=%async_computation.5 | async-start | bytes 4177920 | tf_op jit(solution)/shard_map/all_gather | solution.py:276
  20.1 14.4 %collective-permute-start.1 = (bf16[256,896]{1,0:T(8,128)(2,1)}, bf16[256,896]{1,0:T(8,128)(2,1)S(1)}, u32[]{:S(2)}, u32[]{:S(2)}) collective-permute-start(bf16[256,896]{1,0:T(8,128)(2,1)} %get-tuple-element.23), channel_id=1, source_target_pairs={{0,16},{16,0},{1,17},{17,1},{2,18},{18,2},{3,19},{19,3},{4,20},{20... | collective-permute-start | bytes 1376264 | tf_op jit(solution)/shard_map/ppermute | solution.py:147
  23.3 18.7 %all-to-all-start.1 = ((bf16[8,2,16,576]{3,2,1,0:T(8,128)(2,1)}), bf16[8,2,16,576]{3,2,1,0:T(8,128)(2,1)S(1)}, u32[]{:S(2)}, u32[]{:S(2)}) async-start(bf16[8,2,16,576]{3,2,1,0:T(8,128)(2,1)} %bitcast.8), calls=%async_computation.1 | async-start | bytes 655360 | tf_op jit(solution)/shard_map/all_to_all | solution.py:127
  29.3 11.2 %collective-permute-start = (bf16[256,896]{1,0:T(8,128)(2,1)}, bf16[256,896]{1,0:T(8,128)(2,1)S(1)}, u32[]{:S(2)}, u32[]{:S(2)}) collective-permute-start(bf16[256,896]{1,0:T(8,128)(2,1)} %get-tuple-element.27.refs_0_), channel_id=1, source_target_pairs={{0,384},{128,0},{256,128},{384,256},{1,385},{129,1},{257,129},{385... | collective-permute-start | bytes 1376264 | tf_op jit(solution)/shard_map/ppermute | solution.py:152
  32.0 18.4 %collective-permute-start.2 = (bf16[256,896]{1,0:T(8,128)(2,1)}, bf16[256,896]{1,0:T(8,128)(2,1)S(1)}, u32[]{:S(2)}, u32[]{:S(2)}) collective-permute-start(bf16[256,896]{1,0:T(8,128)(2,1)} %get-tuple-element.27.refs_0_), channel_id=1, source_target_pairs={{0,128},{128,256},{256,384},{384,0},{1,129},{129,257},{257,385},{3... | collective-permute-start | bytes 1376264 | tf_op jit(solution)/shard_map/ppermute | solution.py:152
  34.6 17.8 %collective-permute-start.4 = (bf16[256,896]{1,0:T(8,128)(2,1)S(1)}, bf16[256,896]{1,0:T(8,128)(2,1)S(1)}, u32[]{:S(2)}, u32[]{:S(2)}) collective-permute-start(bf16[256,896]{1,0:T(8,128)(2,1)S(1)} %collective-permute-done.1.refs_1_), channel_id=1, source_target_pairs={{0,384},{128,0},{256,128},{384,256},{1,385},{129,1},{257,129},{385... | collective-permute-start | bytes 1376264 | tf_op jit(solution)/shard_map/ppermute | solution.py:152
  38.6 18.4 %collective-permute-start.3 = (bf16[256,896]{1,0:T(8,128)(2,1)S(1)}, bf16[256,896]{1,0:T(8,128)(2,1)S(1)}, u32[]{:S(2)}, u32[]{:S(2)}) collective-permute-start(bf16[256,896]{1,0:T(8,128)(2,1)S(1)} %collective-permute-done.1.refs_1_), channel_id=1, source_target_pairs={{0,128},{128,256},{256,384},{384,0},{1,129},{129,257},{257,385},{3... | collective-permute-start | bytes 1376264 | tf_op jit(solution)/shard_map/ppermute | solution.py:152
  42.0 0.7 copy-start.1
  45.3 14.5 %all-to-all-start.2 = ((bf16[8,2,16,512]{3,2,1,0:T(8,128)(2,1)}), bf16[8,2,16,512]{3,2,1,0:T(8,128)(2,1)S(1)}, u32[]{:S(2)}, u32[]{:S(2)}) async-start(bf16[8,2,16,512]{3,2,1,0:T(8,128)(2,1)} %attend.1), calls=%async_computation.2 | async-start | bytes 524288 | tf_op jit(solution)/shard_map/all_to_all | solution.py:141
  50.5 24.8 %collective-permute-start.5 = (bf16[256,896]{1,0:T(8,128)(2,1)S(1)}, bf16[256,896]{1,0:T(8,128)(2,1)}, u32[]{:S(2)}, u32[]{:S(2)}) collective-permute-start(bf16[256,896]{1,0:T(8,128)(2,1)S(1)} %collective-permute-done.2.refs_2_), channel_id=1, source_target_pairs={{0,128},{128,256},{256,384},{384,0},{1,129},{129,257},{257,385},{3... | collective-permute-start | bytes 1376264 | tf_op jit(solution)/shard_map/ppermute | solution.py:152
  52.4 22.9 %collective-permute-start.6 = (bf16[256,896]{1,0:T(8,128)(2,1)S(1)}, bf16[256,896]{1,0:T(8,128)(2,1)}, u32[]{:S(2)}, u32[]{:S(2)}) collective-permute-start(bf16[256,896]{1,0:T(8,128)(2,1)S(1)} %collective-permute-done.4.refs_5_), channel_id=1, source_target_pairs={{0,384},{128,0},{256,128},{384,256},{1,385},{129,1},{257,129},{385... | collective-permute-start | bytes 1376264 | tf_op jit(solution)/shard_map/ppermute | solution.py:152
  75.3 24.7 %copy-start = (bf16[256,896]{1,0:T(8,128)(2,1)S(1)}, bf16[256,896]{1,0:T(8,128)(2,1)}, u32[]{:S(2)}) copy-start(bf16[256,896]{1,0:T(8,128)(2,1)} %get-tuple-element.27.refs_0_) | copy-start | bytes 1376260
  94.3 5.7 %collective-permute-start.7 = (bf16[256,256]{1,0:T(8,128)(2,1)S(1)}, bf16[256,256]{1,0:T(8,128)(2,1)S(1)}, u32[]{:S(2)}, u32[]{:S(2)}) collective-permute-start(bf16[256,256]{1,0:T(8,128)(2,1)S(1)} %active_rows.1.mine_ref), channel_id=1, source_target_pairs={{0,16},{16,0},{1,17},{17,1},{2,18},{18,2},{3,19},{19,3},{4,20},{20... | collective-permute-start | bytes 393224 | tf_op jit(solution)/shard_map/ppermute | solution.py:147
  103.1 6.5 %collective-permute-start.8 = (bf16[4,128,896]{2,1,0:T(8,128)(2,1)S(1)}, bf16[4,128,896]{2,1,0:T(8,128)(2,1)S(1)}, u32[]{:S(2)}, u32[]{:S(2)}) collective-permute-start(bf16[4,128,896]{2,1,0:T(8,128)(2,1)S(1)} %get-tuple-element.36), channel_id=1, source_target_pairs={{0,1},{1,0},{2,3},{3,2},{4,5},{5,4},{6,7},{7,6},{8,9},{9,8},{10,11... | collective-permute-start | bytes 2752520 | tf_op jit(solution)/shard_map/ppermute | solution.py:147
Sparse Core Ops, SparseCore 0:
  20.2 49.9 all-gather.1

commit v6 on v5

--- a/solution.py
+++ b/solution.py
@@ -13,7 +13,7 @@
 score_scale = 192.0 ** (-0.5)
 VMEM = pl.BlockSpec(memory_space=pltpu.VMEM)
 PARAMS = pltpu.CompilerParams(vmem_limit_bytes=48 * 1024 * 1024)
-WIDE = pltpu.CompilerParams(vmem_limit_bytes=60 * 1024 * 1024)
+WIDE = pltpu.CompilerParams(vmem_limit_bytes=57 * 1024 * 1024)
 
 
 def norm_kernel(tokens_ref, gain_ref, ids_ref, route_ref, down_ref, out_ref, mine_ref, send_ref):

time: 156 us -> 156 us (level)
  no operation moved by 1% of the time
where the time goes in v6:
time: 156 us; the launch traced here: 155 us
  blocking collectives  65.9 us (42%)
  starting transfers between devices  39.5 us (25%)
  waiting for transfers between devices  19.4 us (12%)
  Pallas kernels  14.7 us (9%)
  between operations  14.2 us (9%)
    all_to_all x1, blocking collectives, shards(): lax.all_to_all(both, ('k', 'z'), split_axis=0, concat_axis=0, tiled=True)  36.7 us
    all_to_all x1, blocking collectives, shards(): lax.all_to_all(partial, 'x', split_axis=0, concat_axis=0, tiled=True)  18.8 us
    ppermute x6, starting transfers between devices, shift(): lax.ppermute(array, 'x', [(i, (i + step) % size) for i in range(size)])  17.7 us
    ppermute x3, starting transfers between devices, swap(): return lax.ppermute(array, axis, [(0, 1), (1, 0)])  10.8 us
    all_gather x1, waiting for transfers between devices, shards(): lax.all_gather(sliced.reshape(x_size * rows, width + lanes), ('z', 'c'),...  10.5 us
    all_to_all x1, blocking collectives, shards(): lax.all_to_all(normed, 'x', split_axis=0, concat_axis=0, tiled=True)  10.4 us
    all_to_all x1, starting transfers between devices, attention(): lax.all_to_all(asked, ('k', 'h'), split_axis=0, concat_axis=0, tiled=True)  5.93 us
    all_to_all x1, starting transfers between devices, answer(): lax.all_to_all(result, ('k', 'h'), split_axis=0, concat_axis=0, tiled=True)  5.12 us
  transfers between devices with their start and end apart: 12, of which 5 were waited for; matrix products, arithmetic and copies ran while one was open for 0% of the time, Pallas kernels for 5%

profile of v6, /device:TPU:1, one launch (start us, length us, event | category | flops | bytes accessed | tf_op | source)
XLA Modules:
  0.0 154.7 jit_solution(10530900663942910664)
XLA Ops:
  7.2 0.0 all-gather.2.cloned.1.call-start
  7.2 2.5 %norm_rows.1 = (bf16[4,16,1920]{2,1,0:T(8,128)(2,1)}, bf16[256,896]{1,0:T(8,128)(2,1)}, bf16[256,896]{1,0:T(8,128)(2,1)}) custom-call(bf16[16,7168]{1,0:T(8,128)(2,1)} %tokens_ref.1, f32[1,7168]{1,0:T(1,128)} %bitcast.28, s32[8,16]{1,0:T(8,128)} %bitcast.29, f32[8,16]{1,0:T(8,128)} %bitcast.30, bf16[256,1792]{1,0:T(8,128)(2,1)} %bitcast.24), custom_call_target="tpu_custom_call" | custom-call | tf_op jit(solution)/shard_map/norm_rows/pallas_call | solution.py:260
  9.7 10.4 %all_to_all.25 = bf16[4,16,1920]{2,1,0:T(8,128)(2,1)} all-to-all(bf16[4,16,1920]{2,1,0:T(8,128)(2,1)} %get-tuple-element.20), channel_id=1, replica_groups=mesh['x'=4,'k'=4,'h'=2,'z'=8,'c'=2] {'x'}, dimensions={0} | all-to-all | bytes 491520 | tf_op jit(solution)/shard_map/all_to_all | solution.py:275
  20.1 0.0 all-gather.2.cloned.1.call-update
  20.1 3.2 %collective-permute-start.1 = (bf16[256,896]{1,0:T(8,128)(2,1)}, bf16[256,896]{1,0:T(8,128)(2,1)S(1)}, u32[]{:S(2)}, u32[]{:S(2)}) collective-permute-start(bf16[256,896]{1,0:T(8,128)(2,1)} %get-tuple-element.23), channel_id=1, source_target_pairs={{0,16},{16,0},{1,17},{17,1},{2,18},{18,2},{3,19},{19,3},{4,20},{20... | collective-permute-start | bytes 1376264 | tf_op jit(solution)/shard_map/ppermute | solution.py:147
  23.3 5.9 %all-to-all-start.1 = ((bf16[8,2,16,576]{3,2,1,0:T(8,128)(2,1)}), bf16[8,2,16,576]{3,2,1,0:T(8,128)(2,1)S(1)}, u32[]{:S(2)}, u32[]{:S(2)}) async-start(bf16[8,2,16,576]{3,2,1,0:T(8,128)(2,1)} %bitcast.8), calls=%async_computation.1 | async-start | bytes 655360 | tf_op jit(solution)/shard_map/all_to_all | solution.py:127
  29.3 2.8 %collective-permute-start = (bf16[256,896]{1,0:T(8,128)(2,1)}, bf16[256,896]{1,0:T(8,128)(2,1)S(1)}, u32[]{:S(2)}, u32[]{:S(2)}) collective-permute-start(bf16[256,896]{1,0:T(8,128)(2,1)} %get-tuple-element.27.refs_0_), channel_id=1, source_target_pairs={{0,384},{128,0},{256,128},{384,256},{1,385},{129,1},{257,129},{385... | collective-permute-start | bytes 1376264 | tf_op jit(solution)/shard_map/ppermute | solution.py:152
  32.0 2.5 %collective-permute-start.2 = (bf16[256,896]{1,0:T(8,128)(2,1)}, bf16[256,896]{1,0:T(8,128)(2,1)S(1)}, u32[]{:S(2)}, u32[]{:S(2)}) collective-permute-start(bf16[256,896]{1,0:T(8,128)(2,1)} %get-tuple-element.27.refs_0_), channel_id=1, source_target_pairs={{0,128},{128,256},{256,384},{384,0},{1,129},{129,257},{257,385},{3... | collective-permute-start | bytes 1376264 | tf_op jit(solution)/shard_map/ppermute | solution.py:152
  34.5 0.0 collective-permute-done.1.refs_1_
  34.6 4.0 %collective-permute-start.4 = (bf16[256,896]{1,0:T(8,128)(2,1)S(1)}, bf16[256,896]{1,0:T(8,128)(2,1)S(1)}, u32[]{:S(2)}, u32[]{:S(2)}) collective-permute-start(bf16[256,896]{1,0:T(8,128)(2,1)S(1)} %collective-permute-done.1.refs_1_), channel_id=1, source_target_pairs={{0,384},{128,0},{256,128},{384,256},{1,385},{129,1},{257,129},{385... | collective-permute-start | bytes 1376264 | tf_op jit(solution)/shard_map/ppermute | solution.py:152
  38.6 1.9 %collective-permute-start.3 = (bf16[256,896]{1,0:T(8,128)(2,1)S(1)}, bf16[256,896]{1,0:T(8,128)(2,1)S(1)}, u32[]{:S(2)}, u32[]{:S(2)}) collective-permute-start(bf16[256,896]{1,0:T(8,128)(2,1)S(1)} %collective-permute-done.1.refs_1_), channel_id=1, source_target_pairs={{0,128},{128,256},{256,384},{384,0},{1,129},{129,257},{257,385},{3... | collective-permute-start | bytes 1376264 | tf_op jit(solution)/shard_map/ppermute | solution.py:152
  40.5 0.0 collective-permute-done.refs_4_
  40.5 1.5 all-to-all-done.1.queries_ref
  42.0 0.0 copy-start.1
  42.0 0.7 copy-done.1
  42.8 2.6 %attend.1 = bf16[8,2,16,512]{3,2,1,0:T(8,128)(2,1)} custom-call(s32[1,2]{1,0:T(1,128)} %lengths_ref.1, bf16[8,2,16,576]{3,2,1,0:T(8,128)(2,1)} %copy-done.1, bf16[2,576,256]{2,1,0:T(8,128)(2,1)} %bitcast.27), custom_call_target="tpu_custom_call" | custom-call | tf_op jit(solution)/shard_map/attend/pallas_call | solution.py:129
  45.3 5.1 %all-to-all-start.2 = ((bf16[8,2,16,512]{3,2,1,0:T(8,128)(2,1)}), bf16[8,2,16,512]{3,2,1,0:T(8,128)(2,1)S(1)}, u32[]{:S(2)}, u32[]{:S(2)}) async-start(bf16[8,2,16,512]{3,2,1,0:T(8,128)(2,1)} %attend.1), calls=%async_computation.2 | async-start | bytes 524288 | tf_op jit(solution)/shard_map/all_to_all | solution.py:141
  50.5 0.0 collective-permute-done.2.refs_2_
  50.5 1.9 %collective-permute-start.5 = (bf16[256,896]{1,0:T(8,128)(2,1)S(1)}, bf16[256,896]{1,0:T(8,128)(2,1)}, u32[]{:S(2)}, u32[]{:S(2)}) collective-permute-start(bf16[256,896]{1,0:T(8,128)(2,1)S(1)} %collective-permute-done.2.refs_2_), channel_id=1, source_target_pairs={{0,128},{128,256},{256,384},{384,0},{1,129},{129,257},{257,385},{3... | collective-permute-start | bytes 1376264 | tf_op jit(solution)/shard_map/ppermute | solution.py:152
  52.4 0.0 collective-permute-done.4.refs_5_
  52.4 4.6 %collective-permute-start.6 = (bf16[256,896]{1,0:T(8,128)(2,1)S(1)}, bf16[256,896]{1,0:T(8,128)(2,1)}, u32[]{:S(2)}, u32[]{:S(2)}) collective-permute-start(bf16[256,896]{1,0:T(8,128)(2,1)S(1)} %collective-permute-done.4.refs_5_), channel_id=1, source_target_pairs={{0,384},{128,0},{256,128},{384,256},{1,385},{129,1},{257,129},{385... | collective-permute-start | bytes 1376264 | tf_op jit(solution)/shard_map/ppermute | solution.py:152
  57.0 0.0 collective-permute-done.3.refs_3_
  57.0 2.8 %all-to-all-done.2 = bf16[8,2,16,512]{3,2,1,0:T(8,128)(2,1)S(1)} async-done(((bf16[8,2,16,512]{3,2,1,0:T(8,128)(2,1)}), bf16[8,2,16,512]{3,2,1,0:T(8,128)(2,1)S(1)}, u32[]{:S(2)}, u32[]{:S(2)}) %all-to-all-start.2) | async-done | bytes 262176 | tf_op jit(solution)/shard_map/all_to_all | solution.py:141
  59.8 10.5 %all-gather.2.cloned.1.call-done = bf16[1024,1920]{1,0:T(8,128)(2,1)} async-done(((bf16[64,1920]{1,0:T(8,128)(2,1)}), bf16[1024,1920]{1,0:T(8,128)(2,1)}) %all-gather.2.cloned.1.call-update) | async-done | bytes 3932176 | tf_op jit(solution)/shard_map/all_gather | solution.py:276
  70.3 5.0 %gate_up.1 = bf16[4,2,8,16,512]{4,3,2,1,0:T(8,128)(2,1)} custom-call(bf16[8,2,4,16,1920]{4,3,2,1,0:T(8,128)(2,1)} %bitcast.18, bf16[1792,256]{1,0:T(8,128)(2,1)} %bitcast.25, bf16[1792,256]{1,0:T(8,128)(2,1)} %bitcast.26), custom_call_target="tpu_custom_call" | custom-call | tf_op jit(solution)/shard_map/gate_up/pallas_call | solution.py:159
  75.3 0.0 copy-start
  75.3 0.0 collective-permute-done.5.refs_6_
  75.3 0.0 collective-permute-done.6.refs_7_
  75.3 18.8 %all_to_all.26.parts_ref = bf16[4,256,512]{2,1,0:T(8,128)(2,1)S(1)} all-to-all(bf16[4,256,512]{2,1,0:T(8,128)(2,1)} %bitcast.21), channel_id=1, replica_groups=mesh['x'=4,'k'=4,'h'=2,'z'=8,'c'=2] {'x'}, dimensions={0} | all-to-all | bytes 2097152 | tf_op jit(solution)/shard_map/all_to_all | solution.py:293
  94.1 0.2 active_rows.1.mine_ref
  94.3 3.1 %collective-permute-start.7 = (bf16[256,256]{1,0:T(8,128)(2,1)S(1)}, bf16[256,256]{1,0:T(8,128)(2,1)S(1)}, u32[]{:S(2)}, u32[]{:S(2)}) collective-permute-start(bf16[256,256]{1,0:T(8,128)(2,1)S(1)} %active_rows.1.mine_ref), channel_id=1, source_target_pairs={{0,16},{16,0},{1,17},{17,1},{2,18},{18,2},{3,19},{19,3},{4,20},{20... | collective-permute-start | bytes 393224 | tf_op jit(solution)/shard_map/ppermute | solution.py:147
  97.4 0.1 pad_add_fusion.place_ref
  97.5 2.5 %collective-permute-done.7.other_ref = bf16[256,256]{1,0:T(8,128)(2,1)S(1)} collective-permute-done((bf16[256,256]{1,0:T(8,128)(2,1)S(1)}, bf16[256,256]{1,0:T(8,128)(2,1)S(1)}, u32[]{:S(2)}, u32[]{:S(2)}) %collective-permute-start.7) | collective-permute-done | bytes 131104 | tf_op jit(solution)/shard_map/ppermute | solution.py:147
  100.0 0.0 copy-done
  100.0 3.1 %down_rows.1 = (bf16[4,128,896]{2,1,0:T(8,128)(2,1)S(1)}, bf16[4,128,896]{2,1,0:T(8,128)(2,1)S(1)}) custom-call(s32[2]{0:T(128)S(1)} %pad_add_fusion.place_ref, bf16[256,256]{1,0:T(8,128)(2,1)S(1)} %active_rows.1.mine_ref, bf16[256,256]{1,0:T(8,128)(2,1)S(1)} %collective-permute-done.7.other_ref, bf16[8,2,4,16,1920]{4,3,2,1,0:T(8,128)(2,1)} %bitcast.19, ...), custom_call_target="tpu_custom_call" | custom-call | tf_op jit(solution)/shard_map/down_rows/pallas_call | solution.py:195
  103.1 4.5 %collective-permute-start.8 = (bf16[4,128,896]{2,1,0:T(8,128)(2,1)S(1)}, bf16[4,128,896]{2,1,0:T(8,128)(2,1)S(1)}, u32[]{:S(2)}, u32[]{:S(2)}) collective-permute-start(bf16[4,128,896]{2,1,0:T(8,128)(2,1)S(1)} %get-tuple-element.36), channel_id=1, source_target_pairs={{0,1},{1,0},{2,3},{3,2},{4,5},{5,4},{6,7},{7,6},{8,9},{9,8},{10,11... | collective-permute-start | bytes 2752520 | tf_op jit(solution)/shard_map/ppermute | solution.py:147
  107.5 2.1 %collective-permute-done.8 = bf16[4,128,896]{2,1,0:T(8,128)(2,1)S(1)} collective-permute-done((bf16[4,128,896]{2,1,0:T(8,128)(2,1)S(1)}, bf16[4,128,896]{2,1,0:T(8,128)(2,1)S(1)}, u32[]{:S(2)}, u32[]{:S(2)}) %collective-permute-start.8) | collective-permute-done | bytes 917536 | tf_op jit(solution)/shard_map/ppermute | solution.py:147
  109.6 0.2 add_convert_fusion
  109.8 36.7 %all_to_all.27.landed_ref = bf16[32,16,896]{2,1,0:T(8,128)(2,1)S(1)} all-to-all(bf16[32,16,896]{2,1,0:T(8,128)(2,1)S(1)} %bitcast.22), channel_id=1, replica_groups=mesh['x'=4,'k'=4,'h'=2,'z'=8,'c'=2] {'k','z'}, dimensions={0} | all-to-all | bytes 1835008 | tf_op jit(solution)/shard_map/all_to_all | solution.py:300
  146.6 1.3 last_sum.1
Async XLA Ops:
  7.2 63.1 %all-gather.2.cloned.1.call-start = ((), (), s32[]{:S(2)}) async-start(), calls=%async_computation.5 | async-start | bytes 4177920 | tf_op jit(solution)/shard_map/all_gather | solution.py:276
  20.1 14.4 %collective-permute-start.1 = (bf16[256,896]{1,0:T(8,128)(2,1)}, bf16[256,896]{1,0:T(8,128)(2,1)S(1)}, u32[]{:S(2)}, u32[]{:S(2)}) collective-permute-start(bf16[256,896]{1,0:T(8,128)(2,1)} %get-tuple-element.23), channel_id=1, source_target_pairs={{0,16},{16,0},{1,17},{17,1},{2,18},{18,2},{3,19},{19,3},{4,20},{20... | collective-permute-start | bytes 1376264 | tf_op jit(solution)/shard_map/ppermute | solution.py:147
  23.3 18.7 %all-to-all-start.1 = ((bf16[8,2,16,576]{3,2,1,0:T(8,128)(2,1)}), bf16[8,2,16,576]{3,2,1,0:T(8,128)(2,1)S(1)}, u32[]{:S(2)}, u32[]{:S(2)}) async-start(bf16[8,2,16,576]{3,2,1,0:T(8,128)(2,1)} %bitcast.8), calls=%async_computation.1 | async-start | bytes 655360 | tf_op jit(solution)/shard_map/all_to_all | solution.py:127
  29.3 11.2 %collective-permute-start = (bf16[256,896]{1,0:T(8,128)(2,1)}, bf16[256,896]{1,0:T(8,128)(2,1)S(1)}, u32[]{:S(2)}, u32[]{:S(2)}) collective-permute-start(bf16[256,896]{1,0:T(8,128)(2,1)} %get-tuple-element.27.refs_0_), channel_id=1, source_target_pairs={{0,384},{128,0},{256,128},{384,256},{1,385},{129,1},{257,129},{385... | collective-permute-start | bytes 1376264 | tf_op jit(solution)/shard_map/ppermute | solution.py:152
  32.0 18.4 %collective-permute-start.2 = (bf16[256,896]{1,0:T(8,128)(2,1)}, bf16[256,896]{1,0:T(8,128)(2,1)S(1)}, u32[]{:S(2)}, u32[]{:S(2)}) collective-permute-start(bf16[256,896]{1,0:T(8,128)(2,1)} %get-tuple-element.27.refs_0_), channel_id=1, source_target_pairs={{0,128},{128,256},{256,384},{384,0},{1,129},{129,257},{257,385},{3... | collective-permute-start | bytes 1376264 | tf_op jit(solution)/shard_map/ppermute | solution.py:152
  34.6 17.8 %collective-permute-start.4 = (bf16[256,896]{1,0:T(8,128)(2,1)S(1)}, bf16[256,896]{1,0:T(8,128)(2,1)S(1)}, u32[]{:S(2)}, u32[]{:S(2)}) collective-permute-start(bf16[256,896]{1,0:T(8,128)(2,1)S(1)} %collective-permute-done.1.refs_1_), channel_id=1, source_target_pairs={{0,384},{128,0},{256,128},{384,256},{1,385},{129,1},{257,129},{385... | collective-permute-start | bytes 1376264 | tf_op jit(solution)/shard_map/ppermute | solution.py:152
  38.6 18.4 %collective-permute-start.3 = (bf16[256,896]{1,0:T(8,128)(2,1)S(1)}, bf16[256,896]{1,0:T(8,128)(2,1)S(1)}, u32[]{:S(2)}, u32[]{:S(2)}) collective-permute-start(bf16[256,896]{1,0:T(8,128)(2,1)S(1)} %collective-permute-done.1.refs_1_), channel_id=1, source_target_pairs={{0,128},{128,256},{256,384},{384,0},{1,129},{129,257},{257,385},{3... | collective-permute-start | bytes 1376264 | tf_op jit(solution)/shard_map/ppermute | solution.py:152
  42.0 0.7 copy-start.1
  45.3 14.5 %all-to-all-start.2 = ((bf16[8,2,16,512]{3,2,1,0:T(8,128)(2,1)}), bf16[8,2,16,512]{3,2,1,0:T(8,128)(2,1)S(1)}, u32[]{:S(2)}, u32[]{:S(2)}) async-start(bf16[8,2,16,512]{3,2,1,0:T(8,128)(2,1)} %attend.1), calls=%async_computation.2 | async-start | bytes 524288 | tf_op jit(solution)/shard_map/all_to_all | solution.py:141
  50.5 24.8 %collective-permute-start.5 = (bf16[256,896]{1,0:T(8,128)(2,1)S(1)}, bf16[256,896]{1,0:T(8,128)(2,1)}, u32[]{:S(2)}, u32[]{:S(2)}) collective-permute-start(bf16[256,896]{1,0:T(8,128)(2,1)S(1)} %collective-permute-done.2.refs_2_), channel_id=1, source_target_pairs={{0,128},{128,256},{256,384},{384,0},{1,129},{129,257},{257,385},{3... | collective-permute-start | bytes 1376264 | tf_op jit(solution)/shard_map/ppermute | solution.py:152
  52.4 22.9 %collective-permute-start.6 = (bf16[256,896]{1,0:T(8,128)(2,1)S(1)}, bf16[256,896]{1,0:T(8,128)(2,1)}, u32[]{:S(2)}, u32[]{:S(2)}) collective-permute-start(bf16[256,896]{1,0:T(8,128)(2,1)S(1)} %collective-permute-done.4.refs_5_), channel_id=1, source_target_pairs={{0,384},{128,0},{256,128},{384,256},{1,385},{129,1},{257,129},{385... | collective-permute-start | bytes 1376264 | tf_op jit(solution)/shard_map/ppermute | solution.py:152
  75.3 24.7 %copy-start = (bf16[256,896]{1,0:T(8,128)(2,1)S(1)}, bf16[256,896]{1,0:T(8,128)(2,1)}, u32[]{:S(2)}) copy-start(bf16[256,896]{1,0:T(8,128)(2,1)} %get-tuple-element.27.refs_0_) | copy-start | bytes 1376260
  94.3 5.7 %collective-permute-start.7 = (bf16[256,256]{1,0:T(8,128)(2,1)S(1)}, bf16[256,256]{1,0:T(8,128)(2,1)S(1)}, u32[]{:S(2)}, u32[]{:S(2)}) collective-permute-start(bf16[256,256]{1,0:T(8,128)(2,1)S(1)} %active_rows.1.mine_ref), channel_id=1, source_target_pairs={{0,16},{16,0},{1,17},{17,1},{2,18},{18,2},{3,19},{19,3},{4,20},{20... | collective-permute-start | bytes 393224 | tf_op jit(solution)/shard_map/ppermute | solution.py:147
  103.1 6.5 %collective-permute-start.8 = (bf16[4,128,896]{2,1,0:T(8,128)(2,1)S(1)}, bf16[4,128,896]{2,1,0:T(8,128)(2,1)S(1)}, u32[]{:S(2)}, u32[]{:S(2)}) collective-permute-start(bf16[4,128,896]{2,1,0:T(8,128)(2,1)S(1)} %get-tuple-element.36), channel_id=1, source_target_pairs={{0,1},{1,0},{2,3},{3,2},{4,5},{5,4},{6,7},{7,6},{8,9},{9,8},{10,11... | collective-permute-start | bytes 2752520 | tf_op jit(solution)/shard_map/ppermute | solution.py:147
Sparse Core Ops, SparseCore 0:
  20.2 49.9 all-gather.1
